TPU v7x, 32 devices: a whole 2x2x4 slice. The times are simulated.
32 devices in a mesh: shard: 4 (over z), ctx: 4 (over x, core), tp: 2 (over y).
Axes of the slice: x: 2, y: 2, z: 4, core: 2. Of those that a mesh axis runs over, the one named last changes fastest.
Arguments:
- tokens: bfloat16 [4, 1024, 2048], P('shard', 'ctx'), may hold values from -6 to 6
- piece_starts: int32 [4, 2], P('shard'), may hold values from 0 to 768, as said below
- norm1_gain: bfloat16 [2048], P('shard'), may hold values from 0.25 to 1.75
- w_query: bfloat16 [2048, 2048], P('shard', 'tp'), may hold values from -0.1875 to 0.1875
- w_key: bfloat16 [2048, 2048], P('shard', 'tp'), may hold values from -0.1875 to 0.1875
- w_value: bfloat16 [2048, 2048], P('shard', 'tp'), may hold values from -0.125 to 0.125
- w_out: bfloat16 [2048, 2048], P('tp', 'shard'), may hold values from -0.5 to 0.5
- norm2_gain: bfloat16 [2048], P('shard'), may hold values from 0.25 to 1.75
- w_gate: bfloat16 [2048, 8192], P('shard', 'tp'), may hold values from -0.125 to 0.125
- w_up: bfloat16 [2048, 8192], P('shard', 'tp'), may hold values from -0.125 to 0.125
- w_down: bfloat16 [8192, 2048], P('tp', 'shard'), may hold values from -0.125 to 0.125
- cotangent: bfloat16 [4, 1024, 2048], P('shard', 'ctx'), may hold values from -6 to 6
Outputs:
- output: bfloat16 [4, 1024, 2048], P('shard', 'ctx')
- input_grad: bfloat16 [4, 1024, 2048], P('shard', 'ctx')
- grad_norm1: float32 [2048], P('shard')
- grad_query: float32 [2048, 2048], P('shard', 'tp')
- grad_key: float32 [2048, 2048], P('shard', 'tp')
- grad_value: float32 [2048, 2048], P('shard', 'tp')
- grad_out: float32 [2048, 2048], P('tp', 'shard')
- grad_norm2: float32 [2048], P('shard')
- grad_gate: float32 [2048, 8192], P('shard', 'tp')
- grad_up: float32 [2048, 8192], P('shard', 'tp')
- grad_down: float32 [8192, 2048], P('tp', 'shard')
Inputs may be any that keep to these rules, and one draw needn't show every extreme that they name: `piece_starts`: piece k of a sequence (k from 0 to 1) starts between k * (512) and (k + 1) * 512 - 256, so that the pieces of a sequence never intersect.
All inputs are finite; a program needn't handle non-finite values.
Results may differ from a plain program's by a relative error of at most 0.018.
Values may be sent and summed in bfloat16 or wider, within the bound.
No kernel may reach another device: no remote copies, remote signals or barrier semaphores. Data moves between devices by JAX's collectives and lax.ppermute only.
A program may use at most 320 MiB of HBM per device.

v0:
```python
import math

import jax
import jax.numpy as jnp
from jax import lax
from jax.sharding import PartitionSpec as P

HD = 64
PIECE = 256


epsilon = 1e-05
rope_base = 130000.0


def rms_norm(values, gain):
    factor = lax.rsqrt(jnp.mean(values * values, axis=-1, keepdims=True) + epsilon)
    return values * factor * gain


def rotate(values, positions):
    layout = values.shape
    halves = values.reshape(layout[:-1] + (layout[-1] // HD, 2, HD // 2))
    frequency = jnp.power(rope_base, -2.0 * jnp.arange(HD // 2, dtype=jnp.float32) / HD)
    angles = positions.astype(jnp.float32)[:, None] * frequency[None, :]
    cosine = jnp.cos(angles)[:, None, :]
    sine_table = jnp.sin(angles)[:, None, :]
    front_half = halves[..., 0, :]
    back_half = halves[..., 1, :]
    turned = jnp.stack(
        [
            front_half * cosine - back_half * sine_table,
            back_half * cosine + front_half * sine_table,
        ],
        axis=-2,
    )
    return turned.reshape(layout)


def visible(begins, length):
    places = jnp.arange(length, dtype=jnp.int32)
    inside = (places[None, :] >= begins[:, None]) & (places[None, :] < begins[:, None] + PIECE)
    shared = jnp.any(inside[:, :, None] & inside[:, None, :], axis=0)
    return (places[None, :] <= places[:, None]) | shared


def across_rows(left, right):
    return lax.dot_general(
        left, right, (((0,), (0,)), ((), ())), preferred_element_type=jnp.float32
    )


def against_weight(grad_rows, weight):
    return lax.dot_general(
        grad_rows, weight, (((1,), (1,)), ((), ())), preferred_element_type=jnp.float32
    )


def masked_scores(query_h, key_h, begins, length):
    score_scale = 1.0 / math.sqrt(HD)
    scores = (
        jnp.einsum("qhd,khd->hqk", query_h, key_h, preferred_element_type=jnp.float32) * score_scale
    )
    return jnp.where(visible(begins, length)[None], scores, -1e30)


def attend_forward(packed):
    queries, keys, values, begins = packed
    length = queries.shape[0]
    head_count = queries.shape[1] // HD
    query_h = queries.reshape(length, head_count, HD)
    key_h = keys.reshape(length, head_count, HD)
    value_h = values.reshape(length, head_count, HD)
    scores = masked_scores(query_h, key_h, begins, length)
    totals = jax.nn.logsumexp(scores, axis=-1, keepdims=True)
    weights = jnp.exp(scores - totals).astype(jnp.bfloat16)
    mixed = jnp.einsum("hqk,khd->qhd", weights, value_h, preferred_element_type=jnp.float32)
    return (mixed.reshape(length, head_count * HD).astype(jnp.bfloat16), totals)


def attend_backward(packed):
    queries, keys, values, begins, totals, grad_mixed = packed
    length = queries.shape[0]
    head_count = queries.shape[1] // HD
    score_scale = 1.0 / math.sqrt(HD)
    query_h = queries.reshape(length, head_count, HD)
    key_h = keys.reshape(length, head_count, HD)
    value_h = values.reshape(length, head_count, HD)
    grad_h = grad_mixed.reshape(length, head_count, HD)
    probs = jnp.exp(masked_scores(query_h, key_h, begins, length) - totals)
    grad_value = jnp.einsum(
        "hqk,qhd->khd", probs.astype(jnp.bfloat16), grad_h, preferred_element_type=jnp.float32
    )
    grad_probs = jnp.einsum("qhd,khd->hqk", grad_h, value_h, preferred_element_type=jnp.float32)
    centre = jnp.sum(probs * grad_probs, axis=-1, keepdims=True)
    grad_scores = (probs * (grad_probs - centre)).astype(jnp.bfloat16)
    grad_query = (
        jnp.einsum("hqk,khd->qhd", grad_scores, key_h, preferred_element_type=jnp.float32)
        * score_scale
    )
    grad_key = (
        jnp.einsum("hqk,qhd->khd", grad_scores, query_h, preferred_element_type=jnp.float32)
        * score_scale
    )
    places = jnp.arange(length, dtype=jnp.int32)
    flat_query = grad_query.reshape(length, head_count * HD)
    flat_key = grad_key.reshape(length, head_count * HD)
    unused, unrotate = jax.vjp(lambda field: rotate(field, places), flat_query)
    back_query = unrotate(flat_query)[0].astype(jnp.bfloat16)
    back_key = unrotate(flat_key)[0].astype(jnp.bfloat16)
    return (back_query, back_key, grad_value.reshape(length, head_count * HD).astype(jnp.bfloat16))


def local(
    tokens,
    piece_starts,
    norm1_gain,
    w_query,
    w_key,
    w_value,
    w_out,
    norm2_gain,
    w_gate,
    w_up,
    w_down,
    cotangent,
):
    seq_count, piece_len, width = tokens.shape
    offset = lax.axis_index("ctx") * piece_len
    local_places = offset + jnp.arange(piece_len, dtype=jnp.int32)
    token_rows = tokens.astype(jnp.float32).reshape(-1, width)
    gain_one, query_full, key_full, value_full, out_full = (
        lax.all_gather(norm1_gain, "shard", axis=0, tiled=True),
        lax.all_gather(w_query, "shard", axis=0, tiled=True),
        lax.all_gather(w_key, "shard", axis=0, tiled=True),
        lax.all_gather(w_value, "shard", axis=0, tiled=True),
        lax.all_gather(w_out, "shard", axis=1, tiled=True),
    )
    normed_f, norm1_pull = jax.vjp(rms_norm, token_rows, gain_one.astype(jnp.float32))
    normed = normed_f.astype(jnp.bfloat16)
    columns = query_full.shape[1]
    query_tok = rotate(
        jnp.dot(normed, query_full, preferred_element_type=jnp.float32).reshape(
            seq_count, piece_len, columns
        ),
        local_places,
    ).astype(jnp.bfloat16)
    key_tok = rotate(
        jnp.dot(normed, key_full, preferred_element_type=jnp.float32).reshape(
            seq_count, piece_len, columns
        ),
        local_places,
    ).astype(jnp.bfloat16)
    value_tok = (
        jnp.dot(normed, value_full, preferred_element_type=jnp.float32)
        .astype(jnp.bfloat16)
        .reshape(seq_count, piece_len, columns)
    )
    query_head, key_head, value_head = (
        lax.all_to_all(query_tok, "ctx", split_axis=2, concat_axis=1, tiled=True),
        lax.all_to_all(key_tok, "ctx", split_axis=2, concat_axis=1, tiled=True),
        lax.all_to_all(value_tok, "ctx", split_axis=2, concat_axis=1, tiled=True),
    )
    mixed_head, totals = lax.map(attend_forward, (query_head, key_head, value_head, piece_starts))
    mixed_tok = lax.all_to_all(mixed_head, "ctx", split_axis=1, concat_axis=2, tiled=True)
    mixed_rows = mixed_tok.reshape(-1, columns)
    after_attn = token_rows + lax.psum(
        jnp.dot(mixed_rows, out_full, preferred_element_type=jnp.float32), "tp"
    )
    gain_two, gate_full, up_full, down_full = (
        lax.all_gather(norm2_gain, "shard", axis=0, tiled=True),
        lax.all_gather(w_gate, "shard", axis=0, tiled=True),
        lax.all_gather(w_up, "shard", axis=0, tiled=True),
        lax.all_gather(w_down, "shard", axis=1, tiled=True),
    )
    normed_two_f, norm2_pull = jax.vjp(rms_norm, after_attn, gain_two.astype(jnp.float32))
    normed_two = normed_two_f.astype(jnp.bfloat16)
    gate = jnp.dot(normed_two, gate_full, preferred_element_type=jnp.float32)
    up_proj = jnp.dot(normed_two, up_full, preferred_element_type=jnp.float32)
    active, active_pull = jax.vjp(
        lambda gate_in, up_in: jax.nn.silu(gate_in) * up_in, gate, up_proj
    )
    hidden = active.astype(jnp.bfloat16)
    result = after_attn + lax.psum(
        jnp.dot(hidden, down_full, preferred_element_type=jnp.float32).astype(jnp.bfloat16), "tp"
    ).astype(jnp.float32)
    output = result.astype(jnp.bfloat16).reshape(tokens.shape)
    seed_rows = cotangent.reshape(-1, width)
    grad_down = across_rows(hidden, seed_rows)
    grad_hidden = against_weight(seed_rows, down_full)
    grad_gate_f, grad_up_f = active_pull(grad_hidden)
    grad_gate_b = grad_gate_f.astype(jnp.bfloat16)
    grad_up_b = grad_up_f.astype(jnp.bfloat16)
    grad_gate = across_rows(normed_two, grad_gate_b)
    grad_up = across_rows(normed_two, grad_up_b)
    grad_normed_two = against_weight(grad_gate_b, gate_full) + against_weight(grad_up_b, up_full)
    grad_normed_two = lax.psum(grad_normed_two, "tp")
    grad_attn_rows, grad_norm2 = norm2_pull(grad_normed_two)
    grad_after = seed_rows.astype(jnp.float32) + grad_attn_rows
    grad_after_b = grad_after.astype(jnp.bfloat16)
    grad_out = across_rows(mixed_rows, grad_after_b)
    grad_mixed = (
        against_weight(grad_after_b, out_full)
        .astype(jnp.bfloat16)
        .reshape(seq_count, piece_len, columns)
    )
    grad_mixed_head = lax.all_to_all(grad_mixed, "ctx", split_axis=2, concat_axis=1, tiled=True)
    grad_query_head, grad_key_head, grad_value_head = lax.map(
        attend_backward, (query_head, key_head, value_head, piece_starts, totals, grad_mixed_head)
    )
    grad_query_tok, grad_key_tok, grad_value_tok = (
        lax.all_to_all(grad_query_head, "ctx", split_axis=1, concat_axis=2, tiled=True),
        lax.all_to_all(grad_key_head, "ctx", split_axis=1, concat_axis=2, tiled=True),
        lax.all_to_all(grad_value_head, "ctx", split_axis=1, concat_axis=2, tiled=True),
    )
    grad_query_rows = grad_query_tok.reshape(-1, columns)
    grad_key_rows = grad_key_tok.reshape(-1, columns)
    grad_value_rows = grad_value_tok.reshape(-1, columns)
    grad_query = across_rows(normed, grad_query_rows)
    grad_key = across_rows(normed, grad_key_rows)
    grad_value = across_rows(normed, grad_value_rows)
    grad_normed = (
        against_weight(grad_query_rows, query_full)
        + against_weight(grad_key_rows, key_full)
        + against_weight(grad_value_rows, value_full)
    )
    grad_normed = lax.psum(grad_normed.astype(jnp.bfloat16), "tp").astype(jnp.float32)
    grad_token_rows, grad_norm1 = norm1_pull(grad_normed)
    input_grad = (grad_after + grad_token_rows).astype(jnp.bfloat16).reshape(tokens.shape)
    shares = (
        lax.psum_scatter(grad_norm1, ("shard", "ctx"), scatter_dimension=0, tiled=True),
        lax.psum_scatter(grad_query, ("shard", "ctx"), scatter_dimension=0, tiled=True),
        lax.psum_scatter(grad_key, ("shard", "ctx"), scatter_dimension=0, tiled=True),
        lax.psum_scatter(grad_value, ("shard", "ctx"), scatter_dimension=0, tiled=True),
        lax.psum_scatter(grad_out, ("shard", "ctx"), scatter_dimension=1, tiled=True),
        lax.psum_scatter(grad_norm2, ("shard", "ctx"), scatter_dimension=0, tiled=True),
        lax.psum_scatter(grad_gate, ("shard", "ctx"), scatter_dimension=0, tiled=True),
        lax.psum_scatter(grad_up, ("shard", "ctx"), scatter_dimension=0, tiled=True),
        lax.psum_scatter(grad_down, ("shard", "ctx"), scatter_dimension=1, tiled=True),
    )
    share_n1, share_q, share_k, share_v, share_o, share_n2, share_g, share_u, share_d = shares
    final = (
        lax.all_gather(share_n1.astype(jnp.bfloat16), "ctx", axis=0, tiled=True).astype(
            share_n1.dtype
        ),
        lax.all_gather(share_q.astype(jnp.bfloat16), "ctx", axis=0, tiled=True).astype(
            share_q.dtype
        ),
        lax.all_gather(share_k.astype(jnp.bfloat16), "ctx", axis=0, tiled=True).astype(
            share_k.dtype
        ),
        lax.all_gather(share_v.astype(jnp.bfloat16), "ctx", axis=0, tiled=True).astype(
            share_v.dtype
        ),
        lax.all_gather(share_o.astype(jnp.bfloat16), "ctx", axis=1, tiled=True).astype(
            share_o.dtype
        ),
        lax.all_gather(share_n2.astype(jnp.bfloat16), "ctx", axis=0, tiled=True).astype(
            share_n2.dtype
        ),
        lax.all_gather(share_g.astype(jnp.bfloat16), "ctx", axis=0, tiled=True).astype(
            share_g.dtype
        ),
        lax.all_gather(share_u.astype(jnp.bfloat16), "ctx", axis=0, tiled=True).astype(
            share_u.dtype
        ),
        lax.all_gather(share_d.astype(jnp.bfloat16), "ctx", axis=1, tiled=True).astype(
            share_d.dtype
        ),
    )
    return (
        output,
        input_grad,
        final[0],
        final[1],
        final[2],
        final[3],
        final[4],
        final[5],
        final[6],
        final[7],
        final[8],
    )


def solution(mesh):
    return jax.shard_map(
        local,
        mesh=mesh,
        in_specs=(
            P("shard", "ctx", None),
            P("shard", None),
            P("shard"),
            P("shard", "tp"),
            P("shard", "tp"),
            P("shard", "tp"),
            P("tp", "shard"),
            P("shard"),
            P("shard", "tp"),
            P("shard", "tp"),
            P("tp", "shard"),
            P("shard", "ctx", None),
        ),
        out_specs=(
            P("shard", "ctx", None),
            P("shard", "ctx", None),
            P("shard"),
            P("shard", "tp"),
            P("shard", "tp"),
            P("shard", "tp"),
            P("tp", "shard"),
            P("shard"),
            P("shard", "tp"),
            P("shard", "tp"),
            P("tp", "shard"),
        ),
        check_vma=False,
    )
```

profile of v0, /device:TPU:0, one launch (start us, length us, event | category | flops | bytes accessed | tf_op | source)
XLA Modules:
  0.0 3088.0 jit_solution(6999761469523948219)
XLA Ops:
  10.0 13.6 all-gather
  24.7 68.4 %all-gather.19.cloned.1.call-done = bf16[2048,1024]{1,0:T(8,128)(2,1)} async-done(((bf16[512,1024]{1,0:T(8,128)(2,1)}), bf16[2048,1024]{1,0:T(8,128)(2,1)}) %all-gather.19.cloned.1.call-update) | async-done | bytes 4194320 | tf_op jit(solution)/shard_map/all_gather | solution.py:136
  106.4 67.6 %all-gather.23.cloned.1.call-done = bf16[2048,1024]{1,0:T(8,128)(2,1)} async-done(((bf16[512,1024]{1,0:T(8,128)(2,1)}), bf16[2048,1024]{1,0:T(8,128)(2,1)}) %all-gather.23.cloned.1.call-update) | async-done | bytes 4194320 | tf_op jit(solution)/shard_map/all_gather | solution.py:135
  174.0 6.4 copy.129
  180.4 74.5 %all-gather.21.cloned.1.call-done = bf16[2048,1024]{1,0:T(8,128)(2,1)} async-done(((bf16[512,1024]{1,0:T(8,128)(2,1)}), bf16[2048,1024]{1,0:T(8,128)(2,1)}) %all-gather.21.cloned.1.call-update) | async-done | bytes 4194320 | tf_op jit(solution)/shard_map/all_gather | solution.py:134
  254.9 6.4 copy.126
  328.0 11.8 all_to_all.120
  340.7 4.9 fusion.58
  347.8 11.9 all-gather.1
  359.7 46.5 %all-reduce.12.cloned.1.call-done = f32[256,2048]{1,0:T(8,128)} async-done(((f32[256,2048]{1,0:T(8,128)}), f32[256,2048]{1,0:T(8,128)}) %all-reduce.12.cloned.1.call-update) | async-done | bytes 2097168 | tf_op jit(solution)/shard_map/psum | solution.py:167
  409.6 284.9 %all-gather.27.cloned.1.call-done = bf16[2048,4096]{1,0:T(8,128)(2,1)} async-done(((bf16[512,4096]{1,0:T(8,128)(2,1)}), bf16[2048,4096]{1,0:T(8,128)(2,1)}) %all-gather.27.cloned.1.call-update) | async-done | bytes 16777232 | tf_op jit(solution)/shard_map/all_gather | solution.py:172
  694.6 12.7 fusion.59
  707.2 274.0 %all-gather.29.cloned.1.call-done = bf16[2048,4096]{1,0:T(8,128)(2,1)} async-done(((bf16[512,4096]{1,0:T(8,128)(2,1)}), bf16[2048,4096]{1,0:T(8,128)(2,1)}) %all-gather.29.cloned.1.call-update) | async-done | bytes 16777232 | tf_op jit(solution)/shard_map/all_gather | solution.py:173
  981.2 12.7 fusion.60
  993.9 274.0 %all-gather.31.cloned.1.call-done = bf16[4096,2048]{1,0:T(8,128)(2,1)} async-done(((bf16[4096,512]{1,0:T(8,128)(2,1)}), bf16[4096,2048]{1,0:T(8,128)(2,1)}) %all-gather.31.cloned.1.call-update) | async-done | bytes 16777232 | tf_op jit(solution)/shard_map/all_gather | solution.py:174
  1267.9 13.6 multiply_convert_fusion.1
  1281.5 12.2 fusion.61
  1293.7 12.8 convolution_add_fusion.2
  1307.0 60.8 %all-reduce.14.cloned.1.call-done = f32[256,2048]{1,0:T(8,128)} async-done(((f32[256,2048]{1,0:T(8,128)}), f32[256,2048]{1,0:T(8,128)}) %all-reduce.14.cloned.1.call-update) | async-done | bytes 2097168 | tf_op jit(solution)/shard_map/psum | solution.py:197
  1395.1 7.5 all-to-all-done.4
  1405.0 12.9 multiply_reduce_fusion
  1417.9 8.5 multiply_convert_fusion
  1440.1 17.4 all_to_all.121
  1461.8 4.8 fusion.35
  1473.9 11.2 all_to_all.122
  1486.0 4.8 fusion.39
  1492.2 9.7 convolution_convert_fusion.1
  1508.3 11.2 all_to_all.123
  1522.2 4.8 fusion.37
  1528.2 15.0 fusion.63
  1543.3 15.2 fusion.64
  1559.8 15.0 fusion.29
  1574.9 12.4 convolution_convert_fusion
  1599.0 106.8 %reduce-scatter.10.cloned.1.call-done = f32[128,1024]{1,0:T(8,128)} async-done(((f32[2048,1024]{1,0:T(8,128)}), f32[128,1024]{1,0:T(8,128)}) %reduce-scatter.10.cloned.1.call-update) | async-done | bytes 524304 | tf_op jit(solution)/shard_map/reduce_scatter | solution.py:233
  1707.7 107.2 %reduce-scatter.12.cloned.1.call-done = f32[128,1024]{1,0:T(8,128)} async-done(((f32[2048,1024]{1,0:T(8,128)}), f32[128,1024]{1,0:T(8,128)}) %reduce-scatter.12.cloned.1.call-update) | async-done | bytes 524304 | tf_op jit(solution)/shard_map/reduce_scatter | solution.py:234
  1816.7 334.7 %reduce-scatter.16.cloned.1.call-done = f32[128,4096]{1,0:T(8,128)} async-done(((f32[2048,4096]{1,0:T(8,128)}), f32[128,4096]{1,0:T(8,128)}) %reduce-scatter.16.cloned.1.call-update) | async-done | bytes 2097168 | tf_op jit(solution)/shard_map/reduce_scatter | solution.py:237
  2154.2 333.0 %reduce-scatter.18.cloned.1.call-done = f32[128,4096]{1,0:T(8,128)} async-done(((f32[2048,4096]{1,0:T(8,128)}), f32[128,4096]{1,0:T(8,128)}) %reduce-scatter.18.cloned.1.call-update) | async-done | bytes 2097168 | tf_op jit(solution)/shard_map/reduce_scatter | solution.py:238
  2490.0 333.1 %reduce-scatter.20.cloned.1.call-done = f32[4096,128]{1,0:T(8,128)} async-done(((f32[4096,2048]{1,0:T(8,128)}), f32[4096,128]{1,0:T(8,128)}) %reduce-scatter.20.cloned.1.call-update) | async-done | bytes 2097168 | tf_op jit(solution)/shard_map/reduce_scatter | solution.py:239
  2827.0 61.0 %all-reduce.16.cloned.1.call-done = (bf16[256,2048]{1,0:T(8,128)(2,1)}, bf16[256,2048]{1,0:T(8,128)(2,1)}) async-done(((bf16[256,2048]{1,0:T(8,128)(2,1)}, bf16[256,2048]{1,0:T(8,128)(2,1)}), (bf16[256,2048]{1,0:T(8,128)(2,1)}, bf16[256,2048]{1,0:T(8,128)(2,1)})) %all-reduce.16.cloned.1.call-update) | async-done | bytes 2097168 | tf_op jit(solution)/shard_map/psum | solution.py:184
  2890.3 61.7 %all-reduce.6 = (bf16[2048]{0:T(1024)(128)(2,1)S(1)}, bf16[2048]{0:T(1024)(128)(2,1)S(1)}) all-reduce(f32[2048]{0:T(1024)S(1)} %get-tuple-element.54, f32[2048]{0:T(1024)S(1)} %copy-done.33), channel_id=2, replica_groups=mesh['shard'=4,'ctx'=4,'tp'=2] {'shard','ctx'}, use_global_device_ids=true, to_apply=%region_13.14.clone | all-reduce | flops 4096 | bytes 24576
  2952.0 5.2 all-gather.2
  2957.8 5.0 all-gather.3
  2979.0 21.9 all-gather.41.cloned.1.call-done
  3000.9 6.7 convert_element_type.289
  3007.6 30.1 all-gather.43.cloned.1.call-done
  3037.6 6.7 convert_element_type.291
  3044.3 29.9 all-gather.45.cloned.1.call-done
  3074.2 6.8 convert_element_type.293
  (259 shorter events, 201.8 us)
Async XLA Ops:
  7.2 16.4 copy-start.1
  7.2 85.9 %all-gather.19.cloned.1.call-start = ((), (), s32[]{:S(2)}) async-start(), calls=%async_computation.15 | async-start | bytes 5242880 | tf_op jit(solution)/shard_map/all_gather | solution.py:136
  7.9 166.1 %all-gather.23.cloned.1.call-start = ((), (), s32[]{:S(2)}) async-start(), calls=%async_computation.17 | async-start | bytes 5242880 | tf_op jit(solution)/shard_map/all_gather | solution.py:135
  8.7 246.2 %all-gather.21.cloned.1.call-start = ((), (), s32[]{:S(2)}) async-start(), calls=%async_computation.16 | async-start | bytes 5242880 | tf_op jit(solution)/shard_map/all_gather | solution.py:134
  9.4 331.3 %all-gather.25.cloned.1.call-start = ((), (), s32[]{:S(2)}) async-start(), calls=%async_computation.18 | async-start | bytes 5242880 | tf_op jit(solution)/shard_map/all_gather | solution.py:137
  102.7 171.0 %all-to-all-start = ((bf16[4,2,32768]{2,1,0:T(2,128)(2,1)}), bf16[4,2,32768]{2,1,0:T(2,128)(2,1)S(1)}, u32[]{:S(2)}, u32[]{:S(2)}) async-start(bf16[4,2,32768]{2,1,0:T(2,128)(2,1)} %reshape.589), calls=%async_computation | async-start | bytes 1048576 | tf_op jit(solution)/shard_map/all_to_all | solution.py:162
  267.2 10.4 copy-start.38
  273.7 16.9 copy-start.27
  273.7 12.7 all-to-all-start.1
  286.4 15.4 all-to-all-start.2
  290.5 115.7 %all-reduce.12.cloned.1.call-start = ((), (), s32[]{:S(2)}) async-start(), calls=%async_computation.19 | async-start | bytes 4194304 | tf_op jit(solution)/shard_map/psum | solution.py:167
  294.5 21.9 copy-start.4
  301.7 10.9 copy-start.12
  312.6 5.8 copy-start
  312.6 5.8 copy-start.23
  318.4 4.6 copy-start.31
  340.7 5.0 copy-start.21
  345.7 348.9 %all-gather.27.cloned.1.call-start = ((), (), s32[]{:S(2)}) async-start(), calls=%async_computation.20 | async-start | bytes 20971520 | tf_op jit(solution)/shard_map/all_gather | solution.py:172
  346.3 634.9 %all-gather.29.cloned.1.call-start = ((), (), s32[]{:S(2)}) async-start(), calls=%async_computation.21 | async-start | bytes 20971520 | tf_op jit(solution)/shard_map/all_gather | solution.py:173
  347.0 920.8 %all-gather.31.cloned.1.call-start = ((), (), s32[]{:S(2)}) async-start(), calls=%async_computation.22 | async-start | bytes 20971520 | tf_op jit(solution)/shard_map/all_gather | solution.py:174
  347.8 1020.1 %all-reduce.14.cloned.1.call-start = ((), (), s32[]{:S(2)}) async-start(), calls=%async_computation.23 | async-start | bytes 4194304 | tf_op jit(solution)/shard_map/psum | solution.py:197
  408.2 962.5 %copy-start.2 = (f32[256,2048]{1,0:T(8,128)}, f32[256,2048]{1,0:T(8,128)S(1)}, u32[]{:S(2)}) copy-start(f32[256,2048]{1,0:T(8,128)S(1)} %get-tuple-element.71) | copy-start | bytes 6291460
  1306.6 287.6 %reduce-scatter.14.cloned.1.call-start = ((), (), s32[]{:S(2)}) async-start(), calls=%async_computation.30 | async-start | bytes 8912896 | tf_op jit(solution)/shard_map/reduce_scatter | solution.py:235
  1390.3 12.3 all-to-all-start.4
  1393.8 203.1 %reduce-scatter.8.cloned.1.call-start = ((), (), s32[]{:S(2)}) async-start(), calls=%async_computation.24 | async-start | bytes 8912896 | tf_op jit(solution)/shard_map/reduce_scatter | solution.py:232
  1417.9 8.5 copy-start.13
  1461.8 4.8 copy-start.25
  1466.6 239.2 %reduce-scatter.10.cloned.1.call-start = ((), (), s32[]{:S(2)}) async-start(), calls=%async_computation.26 | async-start | bytes 8912896 | tf_op jit(solution)/shard_map/reduce_scatter | solution.py:233
  1490.8 324.0 %reduce-scatter.12.cloned.1.call-start = ((), (), s32[]{:S(2)}) async-start(), calls=%async_computation.28 | async-start | bytes 8912896 | tf_op jit(solution)/shard_map/reduce_scatter | solution.py:234
  1527.0 624.4 %reduce-scatter.16.cloned.1.call-start = ((), (), s32[]{:S(2)}) async-start(), calls=%async_computation.32 | async-start | bytes 35651584 | tf_op jit(solution)/shard_map/reduce_scatter | solution.py:237
  1543.3 943.9 %reduce-scatter.18.cloned.1.call-start = ((), (), s32[]{:S(2)}) async-start(), calls=%async_computation.34 | async-start | bytes 35651584 | tf_op jit(solution)/shard_map/reduce_scatter | solution.py:238
  1558.6 1264.5 %reduce-scatter.20.cloned.1.call-start = ((), (), s32[]{:S(2)}) async-start(), calls=%async_computation.36 | async-start | bytes 35651584 | tf_op jit(solution)/shard_map/reduce_scatter | solution.py:239
  1574.8 12.5 copy-start.26
  1574.9 1313.1 %all-reduce.16.cloned.1.call-start = ((), (), s32[]{:S(2)}) async-start(), calls=%async_computation.38 | async-start | bytes 4194304 | tf_op jit(solution)/shard_map/psum | solution.py:184
  1574.9 12.4 copy-start.19
  1594.1 1373.5 %all-gather.39.cloned.1.call-start = ((), (), s32[]{:S(2)}) async-start(), calls=%async_computation.31 | async-start | bytes 1310720 | tf_op jit(solution)/shard_map/all_gather | solution.py:255
  1596.0 1374.5 %all-gather.33.cloned.1.call-start = ((), (), s32[]{:S(2)}) async-start(), calls=%async_computation.25 | async-start | bytes 1310720 | tf_op jit(solution)/shard_map/all_gather | solution.py:246
  1598.7 1374.5 %all-gather.35.cloned.1.call-start = ((), (), s32[]{:S(2)}) async-start(), calls=%async_computation.27 | async-start | bytes 1310720 | tf_op jit(solution)/shard_map/all_gather | solution.py:249
  1707.6 1268.6 %all-gather.37.cloned.1.call-start = ((), (), s32[]{:S(2)}) async-start(), calls=%async_computation.29 | async-start | bytes 1310720 | tf_op jit(solution)/shard_map/all_gather | solution.py:252
  1816.6 1184.3 %all-gather.41.cloned.1.call-start = ((), (), s32[]{:S(2)}) async-start(), calls=%async_computation.33 | async-start | bytes 5242880 | tf_op jit(solution)/shard_map/all_gather | solution.py:261
  2154.1 671.7 %copy-start.40 = (u32[32]{0:T(128)S(1)}, u32[32]{0:T(128)}, u32[]{:S(2)}) copy-start(u32[32]{0:T(128)} %constant.109) | copy-start | bytes 388
  2154.1 883.5 %all-gather.43.cloned.1.call-start = ((), (), s32[]{:S(2)}) async-start(), calls=%async_computation.35 | async-start | bytes 5242880 | tf_op jit(solution)/shard_map/all_gather | solution.py:264
  2489.9 400.4 %copy-start.33 = (f32[2048]{0:T(1024)S(1)}, f32[2048]{0:T(1024)}, u32[]{:S(2)}) copy-start(f32[2048]{0:T(1024)} %get-tuple-element.52) | copy-start | bytes 24580
  2489.9 473.6 %copy-start.35 = (f32[256]{0:T(256)S(1)}, f32[256]{0:T(256)}, u32[]{:S(2)}) copy-start(f32[256]{0:T(256)} %copy-done.34) | copy-start | bytes 3076
  2489.9 473.6 %copy-start.3 = (f32[256,2048]{1,0:T(8,128)S(1)}, f32[256,2048]{1,0:T(8,128)}, u32[]{:S(2)}) copy-start(f32[256,2048]{1,0:T(8,128)} %copy-done.2) | copy-start | bytes 6291460
  2489.9 584.3 %all-gather.45.cloned.1.call-start = ((), (), s32[]{:S(2)}) async-start(), calls=%async_computation.37 | async-start | bytes 5242880 | tf_op jit(solution)/shard_map/all_gather | solution.py:267
  2951.9 14.0 copy-start.8
  2951.9 14.0 copy-start.18
  (21 other events, 44.2 us)
Sparse Core Ops, SparseCore 0:
  9.6 83.4 all-gather.18
  94.7 79.2 all-gather.22
  175.6 79.2 all-gather.20
  256.3 79.2 all-gather.24
  345.8 60.4 all-reduce.11
  407.8 286.7 all-gather.26
  696.2 284.9 all-gather.28
  982.9 284.9 all-gather.30
  1306.7 61.0 all-reduce.13
  1377.4 110.3 reduce-scatter.13
  1492.5 104.3 reduce-scatter.7
  1601.4 104.3 reduce-scatter.9
  1710.4 104.3 reduce-scatter.11
  1818.9 332.4 reduce-scatter.15
  2155.5 331.6 reduce-scatter.17
  2491.3 331.7 reduce-scatter.19
  2825.8 62.0 all-reduce.15
  2890.0 17.0 all-gather.38
  2909.3 16.9 all-gather.32
  2928.3 16.7 all-gather.34
  2947.4 16.7 all-gather.36
  2966.4 34.4 all-gather.40
  3003.1 34.4 all-gather.42
  3039.1 35.0 all-gather.44
where the time goes:
time: 3100 us; the launch traced here: 3090 us
  waiting for transfers between devices  2520 us (81%)
  matrix products  198 us (6%)
  blocking collectives  149 us (5%)
  other arithmetic  112 us (4%)
  local copies, waits for them, and re-layouts  73.4 us (2%)
    reduce_scatter x1, waiting for transfers between devices, local(): lax.psum_scatter(grad_gate, ('shard', 'ctx'), scatter_dimension=0, tiled=...  335 us
    reduce_scatter x1, waiting for transfers between devices, local(): lax.psum_scatter(grad_down, ('shard', 'ctx'), scatter_dimension=1, tiled=...  333 us
    reduce_scatter x1, waiting for transfers between devices, local(): lax.psum_scatter(grad_up, ('shard', 'ctx'), scatter_dimension=0, tiled=True)  333 us
    all_gather x1, waiting for transfers between devices, local(): lax.all_gather(w_gate, 'shard', axis=0, tiled=True)  285 us
    all_gather x1, waiting for transfers between devices, local(): lax.all_gather(w_up, 'shard', axis=0, tiled=True)  274 us
    all_gather x1, waiting for transfers between devices, local(): lax.all_gather(w_down, 'shard', axis=1, tiled=True)  274 us
    reduce_scatter x1, waiting for transfers between devices, local(): lax.psum_scatter(grad_value, ('shard', 'ctx'), scatter_dimension=0, tiled...  107 us
    reduce_scatter x1, waiting for transfers between devices, local(): lax.psum_scatter(grad_key, ('shard', 'ctx'), scatter_dimension=0, tiled=T...  107 us
  transfers between devices with their start and end apart: 28, of which 20 were waited for; matrix products, arithmetic and copies ran while one was open for 10% of the time, Pallas kernels for 0%

commit v1 on v0

v1 whole, which is shorter than its diff:
```python
import math

import jax
import jax.numpy as jnp
from jax import lax
from jax.sharding import PartitionSpec as P

HD = 64
PIECE = 256

EPS = 1e-05
ROPE_BASE = 130000.0
BF = jnp.bfloat16
F32 = jnp.float32


def flip(values, axis, bit, size):
    return lax.ppermute(values, axis, [(i, i ^ bit) for i in range(size)])


def bits_of(size):
    found, bit = [], size // 2
    while bit >= 1:
        found.append(bit)
        bit //= 2
    return found


def order_of(size):
    order = [0]
    for bit in bits_of(size):
        order = order + [o | bit for o in order]
    return order


def gather(block, axis, size):
    for bit in bits_of(size):
        block = jnp.concatenate([block, flip(block, axis, bit, size)], axis=0)
    return block


def reduce_blocks(partial, axis, size):
    for bit in reversed(bits_of(size)):
        half = partial.shape[0] // 2
        come = flip(partial[half:], axis, bit, size)
        partial = (partial[:half].astype(F32) + come.astype(F32)).astype(BF)
    return partial


def sum_tp(partial, size):
    for bit in bits_of(size):
        come = flip(partial, "tp", bit, size)
        partial = partial.astype(F32) + come.astype(F32)
        if bit > 1:
            partial = partial.astype(BF)
    return partial.astype(F32)


def mm(left, right):
    return jnp.dot(left, right, preferred_element_type=F32)


def mm_t(left, right):
    return lax.dot_general(left, right, (((0,), (0,)), ((), ())), preferred_element_type=F32)


def mm_nt(left, right):
    return lax.dot_general(left, right, (((1,), (1,)), ((), ())), preferred_element_type=F32)


def rope_tables(positions):
    frequency = jnp.power(ROPE_BASE, -2.0 * jnp.arange(HD // 2, dtype=F32) / HD)
    angles = positions.astype(F32)[:, None] * frequency[None, :]
    return jnp.cos(angles)[:, None, :], jnp.sin(angles)[:, None, :]


def rotate(values, cosine, sine):
    rows, columns = values.shape
    halves = values.reshape(rows, columns // HD, 2, HD // 2)
    front, back = halves[:, :, 0, :], halves[:, :, 1, :]
    turned = jnp.stack([front * cosine - back * sine, back * cosine + front * sine], axis=2)
    return turned.reshape(rows, columns)


def visible(begins, places):
    inside = (places[None, :] >= begins[:, None]) & (places[None, :] < begins[:, None] + PIECE)
    shared = jnp.any(inside[:, :, None] & inside[:, None, :], axis=0)
    return (places[None, :] <= places[:, None]) | shared


def heads_of(values):
    return values.reshape(values.shape[0], -1, HD)


def scores_of(query, key, seen):
    scores = jnp.einsum("qhd,khd->hqk", heads_of(query), heads_of(key), preferred_element_type=F32)
    return jnp.where(seen[None], scores * (1.0 / math.sqrt(HD)), -1e30)


def attend_forward(query, key, value, seen):
    scores = scores_of(query, key, seen)
    totals = jax.nn.logsumexp(scores, axis=-1, keepdims=True)
    weights = jnp.exp(scores - totals).astype(BF)
    mixed = jnp.einsum("hqk,khd->qhd", weights, heads_of(value), preferred_element_type=F32)
    return mixed.reshape(query.shape).astype(BF), totals


def attend_backward(query, key, value, seen, totals, grad, cosine, sine):
    scale = 1.0 / math.sqrt(HD)
    probs = jnp.exp(scores_of(query, key, seen) - totals)
    grad_h = heads_of(grad)
    grad_value = jnp.einsum("hqk,qhd->khd", probs.astype(BF), grad_h, preferred_element_type=F32)
    grad_probs = jnp.einsum("qhd,khd->hqk", grad_h, heads_of(value), preferred_element_type=F32)
    centre = jnp.sum(probs * grad_probs, axis=-1, keepdims=True)
    grad_scores = (probs * (grad_probs - centre)).astype(BF)
    grad_query = jnp.einsum("hqk,khd->qhd", grad_scores, heads_of(key), preferred_element_type=F32)
    grad_key = jnp.einsum("hqk,qhd->khd", grad_scores, heads_of(query), preferred_element_type=F32)
    grad_query = rotate(grad_query.reshape(query.shape) * scale, cosine, -sine)
    grad_key = rotate(grad_key.reshape(query.shape) * scale, cosine, -sine)
    return grad_query.astype(BF), grad_key.astype(BF), grad_value.reshape(query.shape).astype(BF)


def norm_forward(values, gain):
    factor = lax.rsqrt(jnp.mean(values * values, axis=-1, keepdims=True) + EPS)
    return values * factor, factor


def norm_backward(unit, factor, gain, grad):
    scaled = grad * gain
    back = factor * (scaled - unit * jnp.mean(scaled * unit, axis=-1, keepdims=True))
    return back, jnp.sum(grad * unit, axis=0)


def spread(share, index, size, axis):
    blocks = gather(share[None], "ctx", size)
    order = order_of(size)
    places = []
    for place in range(size):
        value = blocks[0]
        for at in range(1, size):
            value = jnp.where((index ^ order[at]) == place, blocks[at], value)
        places.append(value)
    return jnp.concatenate(places, axis=axis).astype(F32)


def body(n_shard, n_ctx, n_tp, *arguments):
    (tokens, piece_starts, gain1, w_query, w_key, w_value, w_out, gain2, w_gate, w_up, w_down, cotangent) = arguments
    sequences, rows, width = tokens.shape
    assert sequences == 1
    c = lax.axis_index("ctx")
    begins = piece_starts[0]
    places = jnp.concatenate([(c ^ o) * rows + jnp.arange(rows, dtype=jnp.int32) for o in order_of(n_ctx)])
    seen = visible(begins, places)
    cosine, sine = rope_tables(places)

    def columns_of(weight):
        share = weight.shape[1] // n_ctx
        return lax.dynamic_slice_in_dim(weight, c * share, share, axis=1)

    def rows_of(weight):
        share = weight.shape[0] // n_ctx
        return lax.dynamic_slice_in_dim(weight, c * share, share, axis=0)

    heads = w_query.shape[1] // n_ctx
    units = w_gate.shape[1] // n_ctx
    gains = lax.all_gather(jnp.stack([gain1, gain2]), "shard", axis=1, tiled=True).astype(F32)
    gain1_full, gain2_full = gains[0], gains[1]
    attn_pack = jnp.concatenate(
        [columns_of(w_query), columns_of(w_key), columns_of(w_value), rows_of(w_out).T], axis=1
    )
    attn_full = lax.all_gather(attn_pack, "shard", axis=0, tiled=True)
    wide_pack = jnp.concatenate([columns_of(w_gate), columns_of(w_up), rows_of(w_down).T], axis=1)
    wide_pack, attn_full = lax.optimization_barrier((wide_pack, attn_full))
    wide_full = lax.all_gather(wide_pack, "shard", axis=0, tiled=True)
    qkv_full, out_t = attn_full[:, : 3 * heads], attn_full[:, 3 * heads :]
    both_full, down_t = wide_full[:, : 2 * units], wide_full[:, 2 * units :]

    x = tokens[0].astype(F32)
    unit1, factor1 = norm_forward(x, gain1_full)
    n1 = gather((unit1 * gain1_full).astype(BF), "ctx", n_ctx)
    qkv = mm(n1, qkv_full)
    query = rotate(qkv[:, :heads], cosine, sine).astype(BF)
    key = rotate(qkv[:, heads : 2 * heads], cosine, sine).astype(BF)
    value = qkv[:, 2 * heads :].astype(BF)
    mixed, totals = attend_forward(query, key, value, seen)
    h1 = x + sum_tp(reduce_blocks(mm_nt(mixed, out_t).astype(BF), "ctx", n_ctx), n_tp)

    dy = gather(cotangent[0], "ctx", n_ctx)
    unit2, factor2 = norm_forward(h1, gain2_full)
    n2 = gather((unit2 * gain2_full).astype(BF), "ctx", n_ctx)
    both = mm(n2, both_full)
    gate, up = both[:, :units], both[:, units:]
    sigma = jax.nn.sigmoid(gate)
    silu = gate * sigma
    hidden = (silu * up).astype(BF)
    grad_down_t = mm_t(dy, hidden).astype(BF)
    grad_hidden = mm(dy, down_t)
    grad_gate = (grad_hidden * up * (sigma * (1.0 + gate * (1.0 - sigma)))).astype(BF)
    grad_up = (grad_hidden * silu).astype(BF)
    grad_both = jnp.concatenate([grad_gate, grad_up], axis=1)
    grad_both_w = mm_t(n2, grad_both).astype(BF)
    grad_n2 = sum_tp(reduce_blocks(mm_nt(grad_both, both_full).astype(BF), "ctx", n_ctx), n_tp)
    result = sum_tp(reduce_blocks(mm_nt(hidden, down_t).astype(BF), "ctx", n_ctx), n_tp)
    output = (h1 + result).astype(BF)[None]

    share_down = lax.psum_scatter(grad_down_t, "shard", scatter_dimension=0, tiled=True)
    share_both = lax.psum_scatter(grad_both_w, "shard", scatter_dimension=0, tiled=True)

    back2, grad_norm2 = norm_backward(unit2, factor2, gain2_full, grad_n2)
    grad_h1 = cotangent[0].astype(F32) + back2
    dh1 = gather(grad_h1.astype(BF), "ctx", n_ctx)
    grad_out_t = mm_t(dh1, mixed).astype(BF)
    grad_mixed = mm(dh1, out_t).astype(BF)
    dq, dk, dv = attend_backward(query, key, value, seen, totals, grad_mixed, cosine, sine)
    dqkv = jnp.concatenate([dq, dk, dv], axis=1)
    grad_attn = jnp.concatenate([mm_t(n1, dqkv).astype(BF), grad_out_t], axis=1)
    share_attn = lax.psum_scatter(grad_attn, "shard", scatter_dimension=0, tiled=True)
    grad_n1 = sum_tp(reduce_blocks(mm_nt(dqkv, qkv_full).astype(BF), "ctx", n_ctx), n_tp)
    back1, grad_norm1 = norm_backward(unit1, factor1, gain1_full, grad_n1)
    input_grad = (grad_h1 + back1).astype(BF)[None]

    norms = lax.psum(jnp.stack([grad_norm1, grad_norm2]), ("shard", "ctx"))
    share = width // n_shard
    norms = lax.dynamic_slice_in_dim(norms, lax.axis_index("shard") * share, share, axis=1)

    def spread_columns(values):
        return spread(values, c, n_ctx, 1)

    grad_q = spread_columns(share_attn[:, :heads])
    grad_k = spread_columns(share_attn[:, heads : 2 * heads])
    grad_v = spread_columns(share_attn[:, 2 * heads : 3 * heads])
    grad_o = spread(share_attn[:, 3 * heads :].T, c, n_ctx, 0)
    grad_g = spread_columns(share_both[:, :units])
    grad_u = spread_columns(share_both[:, units:])
    grad_d = spread(share_down.T, c, n_ctx, 0)
    return (output, input_grad, norms[0], grad_q, grad_k, grad_v, grad_o, norms[1], grad_g, grad_u, grad_d)


def solution(mesh):
    n_shard, n_ctx, n_tp = mesh.shape["shard"], mesh.shape["ctx"], mesh.shape["tp"]

    def local(*arguments):
        return body(n_shard, n_ctx, n_tp, *arguments)

    return jax.shard_map(
        local,
        mesh=mesh,
        in_specs=(
            P("shard", "ctx", None),
            P("shard", None),
            P("shard"),
            P("shard", "tp"),
            P("shard", "tp"),
            P("shard", "tp"),
            P("tp", "shard"),
            P("shard"),
            P("shard", "tp"),
            P("shard", "tp"),
            P("tp", "shard"),
            P("shard", "ctx", None),
        ),
        out_specs=(
            P("shard", "ctx", None),
            P("shard", "ctx", None),
            P("shard"),
            P("shard", "tp"),
            P("shard", "tp"),
            P("shard", "tp"),
            P("tp", "shard"),
            P("shard"),
            P("shard", "tp"),
            P("shard", "tp"),
            P("tp", "shard"),
        ),
        check_vma=False,
    )
```

time: 3100 us -> 806 us (0.26)
  waiting for transfers between devices: 2520 us -> 403 us
  matrix products: 198 us -> 123 us
  blocking collectives: 149 us -> 75.6 us
    reduce_scatter x7 -> x3, waiting for transfers between devices: 1220 us -> 11.6 us  [the longest x1 11.6 us: body(): lax.psum_scatter(grad_attn, 'shard', scatter_dimension=0, tiled=True)]
    all_gather x14 -> x2, waiting for transfers between devices: 1130 us -> 137 us  [the longest x1 75.9 us: body(): wide_full = lax.all_gather(wide_pack, 'shard', axis=0, tiled=True)]
    ppermute x0 -> x34, waiting for transfers between devices: none -> 254 us  [flip(): return lax.ppermute(values, axis, [(i, i ^ bit) for i in range(size)])]
    psum x3 -> x0, waiting for transfers between devices: 168 us -> none  [the longest x1 61 us: local(): lax.psum(jnp.dot(hidden, down_full, preferred_element_type=jnp.float32).a...]
    dot_general x27 -> x18, matrix products: 198 us -> 123 us  [the longest x4 36.3 us: mm(): return jnp.dot(left, right, preferred_element_type=F32)]
    psum x0 -> x1, blocking collectives: none -> 62.1 us  [body(): norms = lax.psum(jnp.stack([grad_norm1, grad_norm2]), ('shard', 'ctx'))]
    unnamed x1 -> x0, blocking collectives: 61.7 us -> none
    all_to_all x4 -> x0, blocking collectives: 51.7 us -> none  [the longest x1 17.4 us: local(): lax.all_to_all(grad_query_head, 'ctx', split_axis=1, concat_axis=2, tiled...]
  transfers between devices with their start and end apart: 28 -> 39, of which waited for: 20 -> 20; matrix products, arithmetic and copies ran while one was open for 10% -> 29% of each run, Pallas kernels for 0% -> 0%
where the time goes in v1:
time: 806 us; the launch traced here: 803 us
  waiting for transfers between devices  403 us (50%)
  matrix products  123 us (15%)
  other arithmetic  104 us (13%)
  blocking collectives  75.6 us (9%)
  local copies, waits for them, and re-layouts  54.5 us (7%)
  starting transfers between devices  26.7 us (3%)
  between operations  15.6 us (2%)
    ppermute x34, waiting for transfers between devices, flip(): return lax.ppermute(values, axis, [(i, i ^ bit) for i in range(size)])  254 us
    all_gather x1, waiting for transfers between devices, body(): wide_full = lax.all_gather(wide_pack, 'shard', axis=0, tiled=True)  75.9 us
    psum x1, blocking collectives, body(): norms = lax.psum(jnp.stack([grad_norm1, grad_norm2]), ('shard', 'ctx'))  62.1 us
    all_gather x1, waiting for transfers between devices, body(): attn_full = lax.all_gather(attn_pack, 'shard', axis=0, tiled=True)  60.9 us
    dot_general x4, matrix products, mm(): return jnp.dot(left, right, preferred_element_type=F32)  36.3 us
    unnamed x159, local copies, waits for them, and re-layouts  35.2 us
    dot_general x4, matrix products, mm_t(): lax.dot_general(left, right, (((0,), (0,)), ((), ())), preferred_element_...  28.3 us
    dot_general x4, matrix products, mm_nt(): lax.dot_general(left, right, (((1,), (1,)), ((), ())), preferred_element_...  26.6 us
  transfers between devices with their start and end apart: 39, of which 20 were waited for; matrix products, arithmetic and copies ran while one was open for 29% of the time, Pallas kernels for 0%

profile of v1, /device:TPU:0, one launch (start us, length us, event | category | flops | bytes accessed | tf_op | source)
XLA Modules:
  0.0 802.5 jit_solution(1818355228068910433)
XLA Ops:
  12.1 13.5 %all_gather.9 = bf16[2,2048]{1,0:T(2,128)(2,1)S(1)} all-gather(bf16[2,512]{1,0:T(2,128)(2,1)S(1)} %pad_maximum_fusion.39), channel_id=1, replica_groups=mesh['shard'=4,'ctx'=4,'tp'=2] {'shard'}, dimensions={1}, use_global_device_ids=true | all-gather | bytes 10240 | tf_op jit(solution)/shard_map/all_gather | solution.py:166
  34.7 60.9 %all-gather.3.cloned.1.call-done = bf16[2048,1024]{0,1:T(8,128)(2,1)} async-done(((bf16[512,1024]{0,1:T(8,128)(2,1)}), bf16[2048,1024]{0,1:T(8,128)(2,1)}) %all-gather.3.cloned.1.call-update) | async-done | bytes 4194320 | tf_op jit(solution)/shard_map/all_gather | solution.py:171
  95.9 3.1 pad_maximum_fusion.9
  104.7 7.7 fusion.18
  113.1 3.3 fusion
  116.4 3.7 exponential_reduce_fusion
  122.2 4.8 convolution_convert_fusion.8
  130.6 3.8 collective-permute-done.2
  137.0 23.9 %collective-permute-done.3 = bf16[256,2048]{1,0:T(8,128)(2,1)S(1)} collective-permute-done((bf16[256,2048]{1,0:T(8,128)(2,1)S(1)}, bf16[256,2048]{1,0:T(8,128)(2,1)S(1)}, u32[]{:S(2)}, u32[]{:S(2)}) %collective-permute-start.3) | collective-permute-done | bytes 1048608 | tf_op jit(solution)/shard_map/ppermute | solution.py:18
  162.9 23.2 %collective-permute-done.4 = bf16[256,2048]{1,0:T(8,128)(2,1)S(1)} collective-permute-done((bf16[256,2048]{1,0:T(8,128)(2,1)S(1)}, bf16[256,2048]{1,0:T(8,128)(2,1)S(1)}, u32[]{:S(2)}, u32[]{:S(2)}) %collective-permute-start.4) | collective-permute-done | bytes 1048608 | tf_op jit(solution)/shard_map/ppermute | solution.py:18
  188.6 22.4 %collective-permute-done.5 = bf16[256,2048]{1,0:T(8,128)(2,1)S(1)} collective-permute-done((bf16[256,2048]{1,0:T(8,128)(2,1)S(1)}, bf16[256,2048]{1,0:T(8,128)(2,1)S(1)}, u32[]{:S(2)}, u32[]{:S(2)}) %collective-permute-start.5) | collective-permute-done | bytes 1048608 | tf_op jit(solution)/shard_map/ppermute | solution.py:18
  213.0 24.0 %collective-permute-done.10 = bf16[256,2048]{1,0:T(8,128)(2,1)S(1)} collective-permute-done((bf16[256,2048]{1,0:T(8,128)(2,1)S(1)}, bf16[256,2048]{1,0:T(8,128)(2,1)S(1)}, u32[]{:S(2)}, u32[]{:S(2)}) %collective-permute-start.10) | collective-permute-done | bytes 1048608 | tf_op jit(solution)/shard_map/ppermute | solution.py:18
  238.7 75.9 %all-gather.5.cloned.1.call-done = bf16[2048,3072]{0,1:T(8,128)(2,1)} async-done(((bf16[512,3072]{0,1:T(8,128)(2,1)}), bf16[2048,3072]{0,1:T(8,128)(2,1)}) %all-gather.5.cloned.1.call-update) | async-done | bytes 12582928 | tf_op jit(solution)/shard_map/all_gather | solution.py:174
  314.6 12.6 %fusion.4 = f32[1024,2048]{1,0:T(8,128)S(1)} fusion(bf16[2048,3072]{0,1:T(8,128)(2,1)} %all-gather.5.cloned.1.call-done, bf16[512,2048]{1,0:T(8,128)(2,1)} %collective-permute-done.6, bf16[256,2048]{1,0:T(8,128)(2,1)} %copy-done.45, bf16[256,2048]{1,0:T(8,128)(2,1)} %copy-done.34), kind=kOutput, calls=%fused_computation.11 | convolution fusion | flops 8602517504 | bytes 20971520 | tf_op jit(solution)/shard_map/dot_general | solution.py:60
  327.2 11.2 %multiply_convert_fusion.2 = (bf16[1024,1024]{1,0:T(8,128)(2,1)}, bf16[1024,1024]{1,0:T(8,128)(2,1)}, bf16[1024,1024]{1,0:T(8,128)(2,1)S(1)}) fusion(f32[1024,2048]{1,0:T(8,128)S(1)} %fusion.4, bf16[2048,3072]{0,1:T(8,128)(2,1)} %all-gather.5.cloned.1.call-done, bf16[512,2048]{1,0:T(8,128)(2,1)} %collective-permute-done.11, ...), kind=kOutput, calls=%fused_computation.25 | convolution fusion | flops 4323278848 | bytes 23068672 | tf_op jit(solution)/shard_map/dot_general | solution.py:60
  339.7 8.3 %convolution_convert_fusion.3 = bf16[2048,1024]{1,0:T(8,128)(2,1)} fusion(bf16[1024,1024]{1,0:T(8,128)(2,1)S(1)} %get-tuple-element.45, bf16[512,2048]{1,0:T(8,128)(2,1)} %collective-permute-done.11, bf16[256,2048]{1,0:T(8,128)(2,1)S(1)} %copy-done.50, bf16[256,2048]{1,0:T(8,128)(2,1)S(1)} %bitcast.382), kind=kOutput, calls=%fused_computation.35 | convolution fusion | flops 4309647360 | bytes 10485760 | tf_op jit(solution)/shard_map/dot_general | solution.py:64
  348.1 12.6 %fusion.7 = bf16[1024,2048]{1,0:T(8,128)(2,1)S(1)} fusion(bf16[2048,3072]{0,1:T(8,128)(2,1)} %all-gather.5.cloned.1.call-done, bf16[1024,1024]{1,0:T(8,128)(2,1)} %get-tuple-element.44, bf16[1024,1024]{1,0:T(8,128)(2,1)} %get-tuple-element.43), kind=kOutput, calls=%fused_computation.32 | convolution fusion | flops 8600420352 | bytes 16777216 | tf_op jit(solution)/shard_map/dot_general | solution.py:68
  365.7 13.0 %convolution_convert_fusion = bf16[2048,2048]{1,0:T(8,128)(2,1)} fusion(bf16[1024,1024]{1,0:T(8,128)(2,1)S(1)} %copy-done.70, bf16[1024,1024]{1,0:T(8,128)(2,1)S(1)} %copy-done.69, bf16[512,2048]{1,0:T(8,128)(2,1)} %collective-permute-done.6, bf16[256,2048]{1,0:T(8,128)(2,1)S(1)} %copy-done.46, bf16[256,2048]{1,0:T(8,128)(2,1)S(1)} %copy-done.35), kind=kOutput, calls=%fused_computation.8 | convolution fusion | flops 8615100416 | bytes 16777216 | tf_op jit(solution)/shard_map/dot_general | solution.py:64
  379.0 3.1 add_convert_fusion.1
  383.7 23.7 %collective-permute-done.13 = bf16[256,2048]{1,0:T(8,128)(2,1)S(1)} collective-permute-done((bf16[256,2048]{1,0:T(8,128)(2,1)S(1)}, bf16[256,2048]{1,0:T(8,128)(2,1)S(1)}, u32[]{:S(2)}, u32[]{:S(2)}) %collective-permute-start.13) | collective-permute-done | bytes 1048608 | tf_op jit(solution)/shard_map/ppermute | solution.py:18
  409.4 22.9 %collective-permute-done.14 = bf16[256,2048]{1,0:T(8,128)(2,1)S(1)} collective-permute-done((bf16[256,2048]{1,0:T(8,128)(2,1)S(1)}, bf16[256,2048]{1,0:T(8,128)(2,1)S(1)}, u32[]{:S(2)}, u32[]{:S(2)}) %collective-permute-start.14) | collective-permute-done | bytes 1048608 | tf_op jit(solution)/shard_map/ppermute | solution.py:18
  436.1 22.0 %collective-permute-done.15 = bf16[256,2048]{1,0:T(8,128)(2,1)S(1)} collective-permute-done((bf16[256,2048]{1,0:T(8,128)(2,1)S(1)}, bf16[256,2048]{1,0:T(8,128)(2,1)S(1)}, u32[]{:S(2)}, u32[]{:S(2)}) %collective-permute-start.15) | collective-permute-done | bytes 1048608 | tf_op jit(solution)/shard_map/ppermute | solution.py:18
  458.5 4.1 collective-permute-done.16
  462.6 4.8 fusion.31
  467.5 10.9 %multiply_reduce_fusion = (f32[4,1024]{1,0:T(4,128)}, f32[4,1024,1024]{1,2,0:T(8,128)}) fusion(f32[4,1024,1024]{1,2,0:T(8,128)S(1)} %bitcast.378, f32[4,1024]{1,0:T(4,128)} %copy-done.54, pred[1024,1024]{0,1:T(8,128)(4,1)S(1)} %copy.43, bf16[1024,4,64]{0,2,1:T(8,128)(2,1)} %bitcast.397, bf16[1024,4,64]{0,2,1:T(8,128)(2,1)} %bitcast.394), kind=kOutput, calls=%fused_computation.1 | convolution fusion | flops 557838336 | bytes 35684352 | tf_op jit(solution)/shard_map/qhd,khd->hqk/dot_general | solution.py:113
  478.4 8.3 %multiply_convert_fusion = bf16[4,1024,1024]{1,2,0:T(8,128)(2,1)S(1)} fusion(f32[4,1024,1024]{1,2,0:T(8,128)} %get-tuple-element.104, f32[4,1024,1024]{1,2,0:T(8,128)S(1)} %bitcast.378, f32[4,1024]{1,0:T(4,128)} %get-tuple-element.103, f32[4,1024]{1,0:T(4,128)} %copy-done.54, pred[1024,1024]{0,1:T(8,128)(4,1)S(1)} %copy.43), kind=kLoop, calls=%fused_computation | loop fusion | flops 25165824 | bytes 43024384 | tf_op jit(solution)/shard_map/convert_element_type | solution.py:115
  495.2 8.7 %convolution_convert_fusion.7 = bf16[4,64,1024]{2,1,0:T(8,128)(2,1)S(1)} fusion(bf16[1024,4,64]{0,2,1:T(8,128)(2,1)S(1)} %bitcast.398, f32[4,1024,1024]{1,2,0:T(8,128)} %copy-done.2, f32[4,1024]{1,0:T(4,128)S(1)} %copy-done.55, pred[1024,1024]{0,1:T(8,128)(4,1)S(1)} %copy.43), kind=kOutput, calls=%fused_computation.86 | convolution fusion | flops 553910272 | bytes 18890752 | tf_op jit(solution)/shard_map/hqk,qhd->khd/dot_general | solution.py:112
  503.8 5.6 convolution_convert_fusion.5
  511.8 7.3 convolution_convert_fusion.4
  523.6 4.0 convolution_convert_fusion.2
  532.6 3.0 add_convert_fusion.2
  537.2 20.1 %collective-permute-done.32 = bf16[1,1024,512]{1,2,0:T(8,128)(2,1)S(1)} collective-permute-done((bf16[1,1024,512]{1,2,0:T(8,128)(2,1)}, bf16[1,1024,512]{1,2,0:T(8,128)(2,1)S(1)}, u32[]{:S(2)}, u32[]{:S(2)}) %collective-permute-start.32) | collective-permute-done | bytes 1048608 | tf_op jit(solution)/shard_map/ppermute | solution.py:18
  564.4 15.3 %collective-permute-done.8 = bf16[256,2048]{1,0:T(8,128)(2,1)S(1)} collective-permute-done((bf16[256,2048]{1,0:T(8,128)(2,1)}, bf16[256,2048]{1,0:T(8,128)(2,1)S(1)}, u32[]{:S(2)}, u32[]{:S(2)}) %collective-permute-start.8) | collective-permute-done | bytes 1048608 | tf_op jit(solution)/shard_map/ppermute | solution.py:18
  584.1 17.8 %collective-permute-done.18 = bf16[256,2048]{1,0:T(8,128)(2,1)} collective-permute-done((bf16[256,2048]{1,0:T(8,128)(2,1)}, bf16[256,2048]{1,0:T(8,128)(2,1)}, u32[]{:S(2)}, u32[]{:S(2)}) %collective-permute-start.18) | collective-permute-done | bytes 1048608 | tf_op jit(solution)/shard_map/ppermute | solution.py:18
  605.4 3.4 fusion.35
  614.6 3.9 maximum_convert_fusion.2
  618.5 9.0 %copy.53 = f32[4096,512]{1,0:T(8,128)} copy(f32[4096,512]{0,1:T(8,128)} %maximum_convert_fusion.2) | data formatting | bytes 16777216
  631.6 4.5 collective-permute-done.30
  636.1 3.1 pad_maximum_fusion.14
  639.2 11.6 %reduce-scatter.4.cloned.1.call-done = bf16[512,1024]{0,1:T(8,128)(2,1)} async-done(((bf16[2048,1024]{0,1:T(8,128)(2,1)}), bf16[512,1024]{0,1:T(8,128)(2,1)}) %reduce-scatter.4.cloned.1.call-update) | async-done | bytes 1048592 | tf_op jit(solution)/shard_map/reduce_scatter | solution.py:217
  654.8 62.1 %psum.7 = f32[2,2048]{1,0:T(2,128)S(1)} all-reduce(f32[2,2048]{1,0:T(2,128)S(1)} %pad_maximum_fusion.38), channel_id=1, replica_groups=mesh['shard'=4,'ctx'=4,'tp'=2] {'shard','ctx'}, use_global_device_ids=true, to_apply=%region_10.11 | all-reduce | flops 4096 | bytes 32768 | tf_op jit(solution)/shard_map/psum | solution.py:222
  720.4 3.1 collective-permute-done.24
  724.6 5.4 fusion.33
  732.0 3.1 fusion.49
  743.6 19.5 %collective-permute-done.28 = bf16[1,512,1024]{2,1,0:T(8,128)(2,1)S(1)} collective-permute-done((bf16[1,512,1024]{2,1,0:T(8,128)(2,1)S(1)}, bf16[1,512,1024]{2,1,0:T(8,128)(2,1)S(1)}, u32[]{:S(2)}, u32[]{:S(2)}) %collective-permute-start.28) | collective-permute-done | bytes 1048608 | tf_op jit(solution)/shard_map/ppermute | solution.py:18
  772.1 2.9 maximum_convert_fusion.5
  784.0 3.9 maximum_convert_fusion.1
  791.6 3.9 maximum_convert_fusion
  (311 shorter events, 137.8 us)
Async XLA Ops:
  7.2 88.4 %all-gather.3.cloned.1.call-start = ((), (), s32[]{:S(2)}) async-start(), calls=%async_computation.3 | async-start | bytes 5242880 | tf_op jit(solution)/shard_map/all_gather | solution.py:171
  12.0 302.5 %all-gather.5.cloned.1.call-start = ((), (), s32[]{:S(2)}) async-start(), calls=%async_computation.4 | async-start | bytes 15728640 | tf_op jit(solution)/shard_map/all_gather | solution.py:174
  27.3 68.6 %collective-permute-start = (bf16[256,2048]{1,0:T(8,128)(2,1)}, bf16[256,2048]{1,0:T(8,128)(2,1)}, u32[]{:S(2)}, u32[]{:S(2)}) collective-permute-start(bf16[256,2048]{1,0:T(8,128)(2,1)} %fusion.20), channel_id=1, source_target_pairs={{0,4},{2,6},{4,0},{6,2},{1,5},{3,7},{5,1},{7,3},{8,12},{10,14},{12... | collective-permute-start | bytes 3145736 | tf_op jit(solution)/shard_map/ppermute | solution.py:18
  34.7 64.4 %copy-start.65 = (s32[1,2]{1,0:T(1,128)S(1)}, s32[1,2]{1,0:T(1,128)}, u32[]{:S(2)}) copy-start(s32[1,2]{1,0:T(1,128)} %param.13) | copy-start | bytes 28
  95.7 435.4 %reduce-scatter.8.cloned.1.call-start = ((), (), s32[]{:S(2)}) async-start(), calls=%async_computation.7 | async-start | bytes 5242880 | tf_op jit(solution)/shard_map/reduce_scatter | solution.py:206
  99.0 5.6 collective-permute-start.1
  130.1 4.3 collective-permute-start.2
  135.3 50.8 %copy-start.6 = (bf16[1,256,2048]{2,1,0:T(8,128)(2,1)S(1)}, bf16[1,256,2048]{2,1,0:T(8,128)(2,1)}, u32[]{:S(2)}) copy-start(bf16[1,256,2048]{2,1,0:T(8,128)(2,1)} %param.12) | copy-start | bytes 3145732
  135.4 25.5 %collective-permute-start.3 = (bf16[256,2048]{1,0:T(8,128)(2,1)S(1)}, bf16[256,2048]{1,0:T(8,128)(2,1)S(1)}, u32[]{:S(2)}, u32[]{:S(2)}) collective-permute-start(bf16[256,2048]{1,0:T(8,128)(2,1)S(1)} %slice.282), channel_id=1, source_target_pairs={{0,4},{2,6},{4,0},{6,2},{1,5},{3,7},{5,1},{7,3},{8,12},{10,14},{12... | collective-permute-start | bytes 3145736 | tf_op jit(solution)/shard_map/ppermute | solution.py:18
  161.3 24.8 %collective-permute-start.4 = (bf16[256,2048]{1,0:T(8,128)(2,1)S(1)}, bf16[256,2048]{1,0:T(8,128)(2,1)S(1)}, u32[]{:S(2)}, u32[]{:S(2)}) collective-permute-start(bf16[256,2048]{1,0:T(8,128)(2,1)S(1)} %add_convert_fusion.8), channel_id=1, source_target_pairs={{0,1},{1,0},{2,3},{3,2},{4,5},{5,4},{6,7},{7,6},{8,9},{9,8},{10,11... | collective-permute-start | bytes 3145736 | tf_op jit(solution)/shard_map/ppermute | solution.py:18
  186.8 246.9 %copy-start.3 = (f32[256,2048]{1,0:T(8,128)}, f32[256,2048]{1,0:T(8,128)S(1)}, u32[]{:S(2)}) copy-start(f32[256,2048]{1,0:T(8,128)S(1)} %get-tuple-element.42) | copy-start | bytes 6291460
  187.1 51.6 %copy-start.34 = (bf16[256,2048]{1,0:T(8,128)(2,1)}, bf16[256,2048]{1,0:T(8,128)(2,1)S(1)}, u32[]{:S(2)}) copy-start(bf16[256,2048]{1,0:T(8,128)(2,1)S(1)} %multiply_convert_fusion.4) | copy-start | bytes 3145732
  187.1 24.0 %collective-permute-start.5 = (bf16[256,2048]{1,0:T(8,128)(2,1)S(1)}, bf16[256,2048]{1,0:T(8,128)(2,1)S(1)}, u32[]{:S(2)}, u32[]{:S(2)}) collective-permute-start(bf16[256,2048]{1,0:T(8,128)(2,1)S(1)} %multiply_convert_fusion.4), channel_id=1, source_target_pairs={{0,4},{2,6},{4,0},{6,2},{1,5},{3,7},{5,1},{7,3},{8,12},{10,14},{12... | collective-permute-start | bytes 3145736 | tf_op jit(solution)/shard_map/ppermute | solution.py:18
  211.1 27.6 %copy-start.45 = (bf16[256,2048]{1,0:T(8,128)(2,1)}, bf16[256,2048]{1,0:T(8,128)(2,1)S(1)}, u32[]{:S(2)}) copy-start(bf16[256,2048]{1,0:T(8,128)(2,1)S(1)} %collective-permute-done.5) | copy-start | bytes 3145732
  211.3 27.3 %collective-permute-start.6 = (bf16[512,2048]{1,0:T(8,128)(2,1)S(1)}, bf16[512,2048]{1,0:T(8,128)(2,1)}, u32[]{:S(2)}, u32[]{:S(2)}) collective-permute-start(bf16[512,2048]{1,0:T(8,128)(2,1)S(1)} %pad_maximum_fusion.10), channel_id=1, source_target_pairs={{0,2},{2,0},{4,6},{6,4},{1,3},{3,1},{5,7},{7,5},{8,10},{10,8},{12,... | collective-permute-start | bytes 6291464 | tf_op jit(solution)/shard_map/ppermute | solution.py:18
  211.4 25.6 %collective-permute-start.10 = (bf16[256,2048]{1,0:T(8,128)(2,1)S(1)}, bf16[256,2048]{1,0:T(8,128)(2,1)S(1)}, u32[]{:S(2)}, u32[]{:S(2)}) collective-permute-start(bf16[256,2048]{1,0:T(8,128)(2,1)S(1)} %bitcast.379), channel_id=1, source_target_pairs={{0,4},{2,6},{4,0},{6,2},{1,5},{3,7},{5,1},{7,3},{8,12},{10,14},{12... | collective-permute-start | bytes 3145736 | tf_op jit(solution)/shard_map/ppermute | solution.py:18
  238.6 88.6 %collective-permute-start.11 = (bf16[512,2048]{1,0:T(8,128)(2,1)}, bf16[512,2048]{1,0:T(8,128)(2,1)}, u32[]{:S(2)}, u32[]{:S(2)}) collective-permute-start(bf16[512,2048]{1,0:T(8,128)(2,1)} %pad_maximum_fusion.11), channel_id=1, source_target_pairs={{0,2},{2,0},{4,6},{6,4},{1,3},{3,1},{5,7},{7,5},{8,10},{10,8},{12,... | collective-permute-start | bytes 6291464 | tf_op jit(solution)/shard_map/ppermute | solution.py:18
  348.0 260.8 %reduce-scatter.6.cloned.1.call-start = ((), (), s32[]{:S(2)}) async-start(), calls=%async_computation.6 | async-start | bytes 10485760 | tf_op jit(solution)/shard_map/reduce_scatter | solution.py:207
  364.2 14.8 %collective-permute-start.12 = (bf16[512,2048]{1,0:T(8,128)(2,1)}, bf16[512,2048]{1,0:T(8,128)(2,1)}, u32[]{:S(2)}, u32[]{:S(2)}) collective-permute-start(bf16[512,2048]{1,0:T(8,128)(2,1)} %slice.293), channel_id=1, source_target_pairs={{0,2},{2,0},{4,6},{6,4},{1,3},{3,1},{5,7},{7,5},{8,10},{10,8},{12,... | collective-permute-start | bytes 6291464 | tf_op jit(solution)/shard_map/ppermute | solution.py:18
  378.8 272.0 %reduce-scatter.4.cloned.1.call-start = ((), (), s32[]{:S(2)}) async-start(), calls=%async_computation.5 | async-start | bytes 5242880 | tf_op jit(solution)/shard_map/reduce_scatter | solution.py:217
  382.2 51.5 %copy-start.13 = (bf16[1,256,2048]{2,1,0:T(8,128)(2,1)S(1)}, bf16[1,256,2048]{2,1,0:T(8,128)(2,1)}, u32[]{:S(2)}) copy-start(bf16[1,256,2048]{2,1,0:T(8,128)(2,1)} %param.23) | copy-start | bytes 3145732
  382.2 25.2 %collective-permute-start.13 = (bf16[256,2048]{1,0:T(8,128)(2,1)S(1)}, bf16[256,2048]{1,0:T(8,128)(2,1)S(1)}, u32[]{:S(2)}, u32[]{:S(2)}) collective-permute-start(bf16[256,2048]{1,0:T(8,128)(2,1)S(1)} %slice.295), channel_id=1, source_target_pairs={{0,4},{2,6},{4,0},{6,2},{1,5},{3,7},{5,1},{7,3},{8,12},{10,14},{12... | collective-permute-start | bytes 3145736 | tf_op jit(solution)/shard_map/ppermute | solution.py:18
  407.9 24.5 %collective-permute-start.14 = (bf16[256,2048]{1,0:T(8,128)(2,1)S(1)}, bf16[256,2048]{1,0:T(8,128)(2,1)S(1)}, u32[]{:S(2)}, u32[]{:S(2)}) collective-permute-start(bf16[256,2048]{1,0:T(8,128)(2,1)S(1)} %add_convert_fusion.5), channel_id=1, source_target_pairs={{0,1},{1,0},{2,3},{3,2},{4,5},{5,4},{6,7},{7,6},{8,9},{9,8},{10,11... | collective-permute-start | bytes 3145736 | tf_op jit(solution)/shard_map/ppermute | solution.py:18
  434.5 32.9 %copy-start.36 = (bf16[256,2048]{1,0:T(8,128)(2,1)}, bf16[256,2048]{1,0:T(8,128)(2,1)S(1)}, u32[]{:S(2)}) copy-start(bf16[256,2048]{1,0:T(8,128)(2,1)S(1)} %fusion.106) | copy-start | bytes 3145732
  434.6 23.6 %collective-permute-start.15 = (bf16[256,2048]{1,0:T(8,128)(2,1)S(1)}, bf16[256,2048]{1,0:T(8,128)(2,1)S(1)}, u32[]{:S(2)}, u32[]{:S(2)}) collective-permute-start(bf16[256,2048]{1,0:T(8,128)(2,1)S(1)} %fusion.106), channel_id=1, source_target_pairs={{0,4},{2,6},{4,0},{6,2},{1,5},{3,7},{5,1},{7,3},{8,12},{10,14},{12... | collective-permute-start | bytes 3145736 | tf_op jit(solution)/shard_map/ppermute | solution.py:18
  458.4 4.2 collective-permute-start.16
  522.3 10.3 %collective-permute-start.7 = (bf16[512,2048]{1,0:T(8,128)(2,1)}, bf16[512,2048]{1,0:T(8,128)(2,1)}, u32[]{:S(2)}, u32[]{:S(2)}) collective-permute-start(bf16[512,2048]{1,0:T(8,128)(2,1)} %slice.289), channel_id=1, source_target_pairs={{0,2},{2,0},{4,6},{6,4},{1,3},{3,1},{5,7},{7,5},{8,10},{10,8},{12,... | collective-permute-start | bytes 6291464 | tf_op jit(solution)/shard_map/ppermute | solution.py:18
  531.0 27.7 %collective-permute-start.17 = (bf16[512,2048]{1,0:T(8,128)(2,1)}, bf16[512,2048]{1,0:T(8,128)(2,1)}, u32[]{:S(2)}, u32[]{:S(2)}) collective-permute-start(bf16[512,2048]{1,0:T(8,128)(2,1)} %slice.301), channel_id=1, source_target_pairs={{0,2},{2,0},{4,6},{6,4},{1,3},{3,1},{5,7},{7,5},{8,10},{10,8},{12,... | collective-permute-start | bytes 6291464 | tf_op jit(solution)/shard_map/ppermute | solution.py:18
  531.0 26.2 %collective-permute-start.32 = (bf16[1,1024,512]{1,2,0:T(8,128)(2,1)}, bf16[1,1024,512]{1,2,0:T(8,128)(2,1)S(1)}, u32[]{:S(2)}, u32[]{:S(2)}) collective-permute-start(bf16[1,1024,512]{1,2,0:T(8,128)(2,1)} %bitcast.383), channel_id=1, source_target_pairs={{0,4},{2,6},{4,0},{6,2},{1,5},{3,7},{5,1},{7,3},{8,12},{10,14},{12... | collective-permute-start | bytes 3145736 | tf_op jit(solution)/shard_map/ppermute | solution.py:18
  536.7 43.0 %collective-permute-start.8 = (bf16[256,2048]{1,0:T(8,128)(2,1)}, bf16[256,2048]{1,0:T(8,128)(2,1)S(1)}, u32[]{:S(2)}, u32[]{:S(2)}) collective-permute-start(bf16[256,2048]{1,0:T(8,128)(2,1)} %slice.291), channel_id=1, source_target_pairs={{0,4},{2,6},{4,0},{6,2},{1,5},{3,7},{5,1},{7,3},{8,12},{10,14},{12... | collective-permute-start | bytes 3145736 | tf_op jit(solution)/shard_map/ppermute | solution.py:18
  558.7 46.7 %collective-permute-start.33 = (bf16[2,1024,512]{1,2,0:T(8,128)(2,1)}, bf16[2,1024,512]{1,2,0:T(8,128)(2,1)}, u32[]{:S(2)}, u32[]{:S(2)}) collective-permute-start(bf16[2,1024,512]{1,2,0:T(8,128)(2,1)} %pad_maximum_fusion.15), channel_id=1, source_target_pairs={{0,2},{2,0},{4,6},{6,4},{1,3},{3,1},{5,7},{7,5},{8,10},{10,8},{12,... | collective-permute-start | bytes 6291464 | tf_op jit(solution)/shard_map/ppermute | solution.py:18
  562.8 39.0 %collective-permute-start.18 = (bf16[256,2048]{1,0:T(8,128)(2,1)}, bf16[256,2048]{1,0:T(8,128)(2,1)}, u32[]{:S(2)}, u32[]{:S(2)}) collective-permute-start(bf16[256,2048]{1,0:T(8,128)(2,1)} %slice.303), channel_id=1, source_target_pairs={{0,4},{2,6},{4,0},{6,2},{1,5},{3,7},{5,1},{7,3},{8,12},{10,14},{12... | collective-permute-start | bytes 3145736 | tf_op jit(solution)/shard_map/ppermute | solution.py:18
  582.6 142.0 %collective-permute-start.9 = (bf16[256,2048]{1,0:T(8,128)(2,1)}, bf16[256,2048]{1,0:T(8,128)(2,1)}, u32[]{:S(2)}, u32[]{:S(2)}) collective-permute-start(bf16[256,2048]{1,0:T(8,128)(2,1)} %add_convert_fusion.7), channel_id=1, source_target_pairs={{0,1},{1,0},{2,3},{3,2},{4,5},{5,4},{6,7},{7,6},{8,9},{9,8},{10,11... | collective-permute-start | bytes 3145736 | tf_op jit(solution)/shard_map/ppermute | solution.py:18
  603.8 25.7 %collective-permute-start.19 = (bf16[256,2048]{1,0:T(8,128)(2,1)S(1)}, bf16[256,2048]{1,0:T(8,128)(2,1)}, u32[]{:S(2)}, u32[]{:S(2)}) collective-permute-start(bf16[256,2048]{1,0:T(8,128)(2,1)S(1)} %add_convert_fusion.4), channel_id=1, source_target_pairs={{0,1},{1,0},{2,3},{3,2},{4,5},{5,4},{6,7},{7,6},{8,9},{9,8},{10,11... | collective-permute-start | bytes 3145736 | tf_op jit(solution)/shard_map/ppermute | solution.py:18
  611.3 24.9 %collective-permute-start.30 = (bf16[1,512,1024]{2,1,0:T(8,128)(2,1)}, bf16[1,512,1024]{2,1,0:T(8,128)(2,1)}, u32[]{:S(2)}, u32[]{:S(2)}) collective-permute-start(bf16[1,512,1024]{2,1,0:T(8,128)(2,1)} %slice_bitcast_fusion.6), channel_id=1, source_target_pairs={{0,4},{2,6},{4,0},{6,2},{1,5},{3,7},{5,1},{7,3},{8,12},{10,14},{12... | collective-permute-start | bytes 3145736 | tf_op jit(solution)/shard_map/ppermute | solution.py:18
  631.6 93.0 %copy-start.4 = (f32[256,2048]{1,0:T(8,128)S(1)}, f32[256,2048]{1,0:T(8,128)}, u32[]{:S(2)}) copy-start(f32[256,2048]{1,0:T(8,128)} %copy-done.3) | copy-start | bytes 6291460
  631.6 93.0 %copy-start.62 = (f32[256]{0:T(256)S(1)}, f32[256]{0:T(256)}, u32[]{:S(2)}) copy-start(f32[256]{0:T(256)} %copy-done.61) | copy-start | bytes 3076
  639.2 92.8 %collective-permute-start.31 = (bf16[2,512,1024]{2,1,0:T(8,128)(2,1)}, bf16[2,512,1024]{2,1,0:T(8,128)(2,1)}, u32[]{:S(2)}, u32[]{:S(2)}) collective-permute-start(bf16[2,512,1024]{2,1,0:T(8,128)(2,1)} %pad_maximum_fusion.14), channel_id=1, source_target_pairs={{0,2},{2,0},{4,6},{6,4},{1,3},{3,1},{5,7},{7,5},{8,10},{10,8},{12,... | collective-permute-start | bytes 6291464 | tf_op jit(solution)/shard_map/ppermute | solution.py:18
  652.8 65.9 %collective-permute-start.22 = (bf16[1,512,256]{1,2,0:T(8,128)(2,1)}, bf16[1,512,256]{1,2,0:T(8,128)(2,1)}, u32[]{:S(2)}, u32[]{:S(2)}) collective-permute-start(bf16[1,512,256]{1,2,0:T(8,128)(2,1)} %get-tuple-element.86), channel_id=1, source_target_pairs={{0,4},{2,6},{4,0},{6,2},{1,5},{3,7},{5,1},{7,3},{8,12},{10,14},{12... | collective-permute-start | bytes 786440 | tf_op jit(solution)/shard_map/ppermute | solution.py:18
  654.3 63.3 %collective-permute-start.20 = (bf16[1,512,256]{1,2,0:T(8,128)(2,1)}, bf16[1,512,256]{1,2,0:T(8,128)(2,1)S(1)}, u32[]{:S(2)}, u32[]{:S(2)}) collective-permute-start(bf16[1,512,256]{1,2,0:T(8,128)(2,1)} %get-tuple-element.87), channel_id=1, source_target_pairs={{0,4},{2,6},{4,0},{6,2},{1,5},{3,7},{5,1},{7,3},{8,12},{10,14},{12... | collective-permute-start | bytes 786440 | tf_op jit(solution)/shard_map/ppermute | solution.py:18
  716.9 6.6 collective-permute-start.24
  718.7 11.3 %collective-permute-start.21 = (bf16[2,512,256]{1,2,0:T(8,128)(2,1)S(1)}, bf16[2,512,256]{1,2,0:T(8,128)(2,1)S(1)}, u32[]{:S(2)}, u32[]{:S(2)}) collective-permute-start(bf16[2,512,256]{1,2,0:T(8,128)(2,1)S(1)} %pad_maximum_fusion.34), channel_id=1, source_target_pairs={{0,2},{2,0},{4,6},{6,4},{1,3},{3,1},{5,7},{7,5},{8,10},{10,8},{12,... | collective-permute-start | bytes 1572872 | tf_op jit(solution)/shard_map/ppermute | solution.py:18
  719.8 10.2 %collective-permute-start.23 = (bf16[2,512,256]{1,2,0:T(8,128)(2,1)S(1)}, bf16[2,512,256]{1,2,0:T(8,128)(2,1)S(1)}, u32[]{:S(2)}, u32[]{:S(2)}) collective-permute-start(bf16[2,512,256]{1,2,0:T(8,128)(2,1)S(1)} %pad_maximum_fusion.35), channel_id=1, source_target_pairs={{0,2},{2,0},{4,6},{6,4},{1,3},{3,1},{5,7},{7,5},{8,10},{10,8},{12,... | collective-permute-start | bytes 1572872 | tf_op jit(solution)/shard_map/ppermute | solution.py:18
  724.5 5.5 collective-permute-start.25
  732.0 9.1 %collective-permute-start.26 = (bf16[1,256,512]{2,1,0:T(8,128)(2,1)S(1)}, bf16[1,256,512]{2,1,0:T(8,128)(2,1)S(1)}, u32[]{:S(2)}, u32[]{:S(2)}) collective-permute-start(bf16[1,256,512]{2,1,0:T(8,128)(2,1)S(1)} %get-tuple-element.81), channel_id=1, source_target_pairs={{0,4},{2,6},{4,0},{6,2},{1,5},{3,7},{5,1},{7,3},{8,12},{10,14},{12... | collective-permute-start | bytes 786440 | tf_op jit(solution)/shard_map/ppermute | solution.py:18
  735.2 28.0 %collective-permute-start.28 = (bf16[1,512,1024]{2,1,0:T(8,128)(2,1)S(1)}, bf16[1,512,1024]{2,1,0:T(8,128)(2,1)S(1)}, u32[]{:S(2)}, u32[]{:S(2)}) collective-permute-start(bf16[1,512,1024]{2,1,0:T(8,128)(2,1)S(1)} %get-tuple-element.58), channel_id=1, source_target_pairs={{0,4},{2,6},{4,0},{6,2},{1,5},{3,7},{5,1},{7,3},{8,12},{10,14},{12... | collective-permute-start | bytes 3145736 | tf_op jit(solution)/shard_map/ppermute | solution.py:18
  742.0 35.9 %collective-permute-start.27 = (bf16[2,256,512]{2,1,0:T(8,128)(2,1)}, bf16[2,256,512]{2,1,0:T(8,128)(2,1)}, u32[]{:S(2)}, u32[]{:S(2)}) collective-permute-start(bf16[2,256,512]{2,1,0:T(8,128)(2,1)} %pad_maximum_fusion.37), channel_id=1, source_target_pairs={{0,2},{2,0},{4,6},{6,4},{1,3},{3,1},{5,7},{7,5},{8,10},{10,8},{12,... | collective-permute-start | bytes 1572872 | tf_op jit(solution)/shard_map/ppermute | solution.py:18
  764.7 23.2 %collective-permute-start.29 = (bf16[2,512,1024]{2,1,0:T(8,128)(2,1)}, bf16[2,512,1024]{2,1,0:T(8,128)(2,1)}, u32[]{:S(2)}, u32[]{:S(2)}) collective-permute-start(bf16[2,512,1024]{2,1,0:T(8,128)(2,1)} %pad_maximum_fusion.13), channel_id=1, source_target_pairs={{0,2},{2,0},{4,6},{6,4},{1,3},{3,1},{5,7},{7,5},{8,10},{10,8},{12,... | collective-permute-start | bytes 6291464 | tf_op jit(solution)/shard_map/ppermute | solution.py:18
  (66 other events, 502.4 us)
Sparse Core Ops, SparseCore 0:
  12.1 83.4 all-gather.2
  97.8 216.7 all-gather.4
  348.1 74.9 reduce-scatter.7
  426.0 144.9 reduce-scatter.5
  573.3 77.4 reduce-scatter.3

commit v2 on v1

v2 whole, which is shorter than its diff:
```python
import math

import jax
import jax.numpy as jnp
from jax import lax
from jax.experimental import pallas as pl
from jax.experimental.pallas import tpu as pltpu
from jax.sharding import PartitionSpec as P

HD = 64
PIECE = 256

EPS = 1e-05
ROPE_BASE = 130000.0
BF = jnp.bfloat16
F32 = jnp.float32


def flip(values, axis, bit, size):
    return lax.ppermute(values, axis, [(i, i ^ bit) for i in range(size)])


def bits_of(size):
    found, bit = [], size // 2
    while bit >= 1:
        found.append(bit)
        bit //= 2
    return found


def order_of(size):
    order = [0]
    for bit in bits_of(size):
        order = order + [o | bit for o in order]
    return order


def tie(*values):
    return lax.optimization_barrier(values)


def gather(block, axis, size, dim=0):
    for bit in bits_of(size):
        block = jnp.concatenate([block, flip(block, axis, bit, size)], axis=dim)
    return block


def reduce_step(partial, axis, bit, size, dim=0):
    keep, give = jnp.split(partial, 2, axis=dim)
    come = flip(give, axis, bit, size)
    return (keep.astype(F32) + come.astype(F32)).astype(BF)


def mm(left, right):
    return jnp.dot(left, right, preferred_element_type=F32)


def mm_t(left, right):
    return lax.dot_general(left, right, (((0,), (0,)), ((), ())), preferred_element_type=F32)


def mm_nt(left, right):
    return lax.dot_general(left, right, (((1,), (1,)), ((), ())), preferred_element_type=F32)


def rope_tables(positions):
    frequency = jnp.power(ROPE_BASE, -2.0 * jnp.arange(HD // 2, dtype=F32) / HD)
    angles = positions.astype(F32)[:, None] * frequency[None, :]
    return jnp.cos(angles)[:, None, :], jnp.sin(angles)[:, None, :]


def rotate(values, cosine, sine):
    rows, columns = values.shape
    halves = values.reshape(rows, columns // HD, 2, HD // 2)
    front, back = halves[:, :, 0, :], halves[:, :, 1, :]
    turned = jnp.stack([front * cosine - back * sine, back * cosine + front * sine], axis=2)
    return turned.reshape(rows, columns)


def visible(begins, places):
    inside = (places[None, :] >= begins[:, None]) & (places[None, :] < begins[:, None] + PIECE)
    shared = jnp.any(inside[:, :, None] & inside[:, None, :], axis=0)
    return (places[None, :] <= places[:, None]) | shared


def attention_probs(query, key, bias):
    scores = mm_nt(query, key) * (1.0 / math.sqrt(HD)) + bias
    powers = jnp.exp(scores - jnp.max(scores, axis=-1, keepdims=True))
    return powers * (1.0 / jnp.sum(powers, axis=-1, keepdims=True))


def pair_specs(rows, count):
    return [pl.BlockSpec((rows, 2 * HD), lambda i: (0, i)) for _ in range(count)]


def attend_forward(query, key, value, bias):
    rows, columns = query.shape
    block = min(256, rows)

    def kernel(query_ref, key_ref, value_ref, bias_ref, out_ref):
        for head in range(2):
            lanes = slice(head * HD, (head + 1) * HD)
            k, v = key_ref[:, lanes], value_ref[:, lanes]
            for start in range(0, rows, block):
                now = slice(start, start + block)
                probs = attention_probs(query_ref[now, lanes], k, bias_ref[now, :])
                out_ref[now, lanes] = mm(probs.astype(BF), v).astype(BF)

    return pl.pallas_call(
        kernel,
        grid=(columns // (2 * HD),),
        in_specs=pair_specs(rows, 3) + [pl.BlockSpec((rows, rows), lambda i: (0, 0))],
        out_specs=pair_specs(rows, 1)[0],
        out_shape=jax.ShapeDtypeStruct((rows, columns), BF),
        compiler_params=pltpu.CompilerParams(vmem_limit_bytes=40 * 1024 * 1024),
        cost_estimate=pl.CostEstimate(
            flops=16 * rows * rows * columns,
            transcendentals=rows * rows * columns // HD,
            bytes_accessed=8 * rows * columns + 4 * rows * rows,
        ),
    )(query, key, value, bias)


def attend_backward(query, key, value, grad, bias, cosine, sine):
    rows, columns = query.shape
    block = min(256, rows)
    scale = 1.0 / math.sqrt(HD)

    def kernel(query_ref, key_ref, value_ref, grad_ref, bias_ref, cos_ref, sin_ref, dq_ref, dk_ref, dv_ref, q_acc, k_acc):
        lane = lax.broadcasted_iota(jnp.int32, (rows, 2 * HD), 1)
        front = lane % HD < HD // 2

        def turned_back(values):
            other = jnp.where(front, pltpu.roll(values, 2 * HD - HD // 2, 1), pltpu.roll(values, HD // 2, 1))
            return (values * cos_ref[...] + other * sin_ref[...]).astype(BF)

        for head in range(2):
            lanes = slice(head * HD, (head + 1) * HD)
            k, v = key_ref[:, lanes], value_ref[:, lanes]
            k_sum = jnp.zeros((HD, rows), F32)
            v_sum = jnp.zeros((HD, rows), F32)
            for start in range(0, rows, block):
                now = slice(start, start + block)
                q, g = query_ref[now, lanes], grad_ref[now, lanes]
                probs = attention_probs(q, k, bias_ref[now, :])
                v_sum += mm_t(g, probs.astype(BF))
                grad_probs = mm_nt(g, v)
                centre = jnp.sum(probs * grad_probs, axis=-1, keepdims=True)
                grad_scores = (probs * (grad_probs - centre)).astype(BF)
                q_acc[now, lanes] = mm(grad_scores, k) * scale
                k_sum += mm_t(q, grad_scores)
            k_acc[:, lanes] = k_sum.T * scale
            dv_ref[:, lanes] = v_sum.T.astype(BF)
        dq_ref[...] = turned_back(q_acc[...])
        dk_ref[...] = turned_back(k_acc[...])

    return pl.pallas_call(
        kernel,
        grid=(columns // (2 * HD),),
        in_specs=pair_specs(rows, 4)
        + [pl.BlockSpec((rows, rows), lambda i: (0, 0))]
        + [pl.BlockSpec((rows, 2 * HD), lambda i: (0, 0))] * 2,
        out_specs=pair_specs(rows, 3),
        out_shape=[jax.ShapeDtypeStruct((rows, columns), BF)] * 3,
        scratch_shapes=[pltpu.VMEM((rows, 2 * HD), F32)] * 2,
        compiler_params=pltpu.CompilerParams(vmem_limit_bytes=48 * 1024 * 1024),
        cost_estimate=pl.CostEstimate(
            flops=30 * rows * rows * columns,
            transcendentals=rows * rows * columns // HD,
            bytes_accessed=14 * rows * columns + 4 * rows * rows,
        ),
    )(query, key, value, grad, bias, cosine, sine)


def norm_forward(values):
    factor = lax.rsqrt(jnp.mean(values * values, axis=-1, keepdims=True) + EPS)
    return values * factor, factor


def norm_backward(unit, factor, gain, grad):
    scaled = grad * gain
    back = factor * (scaled - unit * jnp.mean(scaled * unit, axis=-1, keepdims=True))
    return back, jnp.sum(grad * unit, axis=0)


def place(pieces, targets, blocks, parts, axis):
    rows, columns = pieces[0].shape[0], pieces[0].shape[1] // parts
    total = len(pieces)

    def kernel(targets_ref, *refs):
        ins, outs = refs[:total], refs[total:]
        i = pl.program_id(0)
        for at, ref in enumerate(ins):

            @pl.when(i == at)
            def _():
                for j, out in enumerate(outs):
                    out[...] = ref[:, j * columns : (j + 1) * columns].astype(F32)

    def go(i, t):
        return (0, t[i]) if axis == 1 else (t[i], 0)

    shape = (rows, columns * blocks) if axis == 1 else (rows * blocks, columns)
    return pl.pallas_call(
        kernel,
        grid_spec=pltpu.PrefetchScalarGridSpec(
            num_scalar_prefetch=1,
            grid=(total,),
            in_specs=[pl.BlockSpec((rows, parts * columns), lambda i, t: (0, 0))] * total,
            out_specs=[pl.BlockSpec((rows, columns), go) for _ in range(parts)],
        ),
        out_shape=[jax.ShapeDtypeStruct(shape, F32) for _ in range(parts)],
        compiler_params=pltpu.CompilerParams(vmem_limit_bytes=32 * 1024 * 1024),
        cost_estimate=pl.CostEstimate(
            flops=0, transcendentals=0, bytes_accessed=6 * parts * rows * columns * blocks
        ),
    )(targets, *pieces)


def body(n_shard, n_ctx, n_tp, *arguments):
    (tokens, piece_starts, gain1, w_query, w_key, w_value, w_out, gain2, w_gate, w_up, w_down, cotangent) = arguments
    sequences, rows, width = tokens.shape
    assert sequences == 1
    z, c, t = lax.axis_index("shard"), lax.axis_index("ctx"), lax.axis_index("tp")
    short = rows // n_tp
    top = n_shard // 2
    high, low = z // top, z % top

    offsets = [(o, p) for o in order_of(n_ctx) for p in order_of(n_tp)]
    places = jnp.concatenate(
        [(c ^ o) * rows + (t ^ p) * short + jnp.arange(short, dtype=jnp.int32) for o, p in offsets]
    )
    bias = jnp.where(visible(piece_starts[0], places), 0.0, -1e30).astype(F32)
    cosine, sine = rope_tables(places)
    back_cosine = jnp.tile(cosine[:, 0, :], (1, 4))
    back_sine = jnp.tile(jnp.concatenate([sine[:, 0, :], -sine[:, 0, :]], axis=1), (1, 2))

    def own_first(values):
        return jnp.concatenate(
            [lax.dynamic_slice_in_dim(values, (t ^ p) * short, short, axis=0) for p in order_of(n_tp)]
        )

    def as_placed(found):
        result = jnp.zeros_like(found)
        for at, p in enumerate(order_of(n_tp)):
            block = found[at * short : (at + 1) * short]
            result = lax.dynamic_update_slice_in_dim(result, block, (t ^ p) * short, axis=0)
        return result[None]

    owners = jnp.stack([c ^ o for o in order_of(n_ctx)]).astype(jnp.int32)
    both_halves = jnp.concatenate([2 * owners + high, 2 * owners + 1 - high]).astype(jnp.int32)

    far_bits, tp_bits = bits_of(n_ctx)[:-1], bits_of(n_tp)
    chips = n_ctx // 2
    half = width // 2

    def halves(values, axis, bit, size, dim=0):
        keep, give = jnp.split(values, 2, axis=dim)
        return [keep, flip(give, axis, bit, size)]

    def added(keep, come):
        return (keep.astype(F32) + come.astype(F32)).astype(BF)

    def core_give(values):
        return halves(values, "ctx", 1, n_ctx)

    def ctx_give(values):
        for bit in reversed(far_bits[1:]):
            values = reduce_step(values, "ctx", bit, n_ctx)
        return halves(values, "ctx", far_bits[0], n_ctx)

    def tp_give(values, dim):
        for bit in reversed(tp_bits[1:]):
            values = reduce_step(values, "tp", bit, n_tp, dim)
        return halves(values, "tp", tp_bits[0], n_tp, dim)

    def first_give(values):
        right = values[:, half:].reshape(chips, n_tp * short, half)
        return ctx_give(values[:, :half]) + tp_give(right, 1)

    def last_give(keep, come, other_keep, other_come):
        right = added(other_keep, other_come).reshape(chips * short, half)
        return tp_give(added(keep, come), 0) + ctx_give(right)

    def reduced(keep, come, other_keep, other_come):
        return jnp.concatenate([added(keep, come), added(other_keep, other_come)], axis=1)

    def ctx_ask(values):
        for bit in far_bits[:-1]:
            values = jnp.concatenate([values, flip(values, "ctx", bit, n_ctx)], axis=0)
        return [values, flip(values, "ctx", far_bits[-1], n_ctx)]

    def tp_ask(values, dim):
        for bit in tp_bits[:-1]:
            values = jnp.concatenate([values, flip(values, "tp", bit, n_tp)], axis=dim)
        return [values, flip(values, "tp", tp_bits[-1], n_tp)]

    def first_ask(values):
        return tp_ask(values[:, :half], 0) + ctx_ask(values[:, half:])

    def last_ask(own, come, other_own, other_come):
        right = jnp.concatenate([other_own, other_come], axis=0).reshape(chips, short, half)
        return ctx_ask(jnp.concatenate([own, come], axis=0)) + tp_ask(right, 1)

    def joined(own, come, other_own, other_come):
        left = jnp.concatenate([own, come], axis=0)
        right = jnp.concatenate([other_own, other_come], axis=1).reshape(left.shape)
        return jnp.concatenate([left, right], axis=1)

    def core_ask(values):
        return [values, flip(values, "ctx", 1, n_ctx)]

    def stacked(*parts):
        return jnp.concatenate(parts, axis=0)

    def pair(values):
        return flip(values, "shard", top, n_shard)

    block = width // n_shard
    low_order = order_of(top)
    low_bits = bits_of(top)

    def folded(values):
        starts = [(side * top + (low ^ o)) * block for o in low_order for side in range(2)]
        return jnp.concatenate([lax.dynamic_slice_in_dim(values, s, block, axis=1) for s in starts], axis=1)

    def unfolded(values):
        where = jnp.asarray([low_order.index(o) for o in range(top)], jnp.int32)
        starts = [(2 * where[low ^ o] + side) * block for side in range(2) for o in range(top)]
        return jnp.concatenate([lax.dynamic_slice_in_dim(values, s, block, axis=1) for s in starts], axis=1)

    def low_ask(values):
        blocks = [values]
        for bit in low_bits:
            blocks = blocks + [flip(v, "shard", bit, n_shard) for v in blocks]
        return blocks

    def low_give(values, dim):
        for bit in reversed(low_bits[1:]):
            values = reduce_step(values, "shard", bit, n_shard, dim)
        return halves(values, "shard", low_bits[0], n_shard, dim)

    def packed(tied, *lengths):
        cuts, at = [], 0
        for length in lengths:
            cuts.append(list(tied[at : at + length]))
            at += length
        assert at == len(tied)
        return cuts

    def core_two(pieces):
        return pieces + [flip(v, "ctx", 1, n_ctx) for v in pieces]

    def ctx_two(values):
        pieces = [values]
        for bit in far_bits:
            pieces = pieces + [flip(v, "ctx", bit, n_ctx) for v in pieces]
        return pieces

    def swap(values, axis):
        size = values.shape[axis] // 2
        keep = lax.dynamic_slice_in_dim(values, high * size, size, axis=axis)
        give = lax.dynamic_slice_in_dim(values, (1 - high) * size, size, axis=axis)
        return keep, give

    heads = w_query.shape[1] // n_ctx
    units = w_gate.shape[1] // n_ctx // 2

    def attn_slice(weight, axis):
        return lax.dynamic_slice_in_dim(weight, c * heads, heads, axis=axis)

    def wide_slice(weight, side, axis):
        return lax.dynamic_slice_in_dim(weight, (2 * c + side) * units, units, axis=axis)

    attn_pack = [attn_slice(w, 1) for w in (w_query, w_key, w_value)] + [attn_slice(w_out, 0).T]
    attn_full = lax.all_gather(jnp.concatenate(attn_pack, axis=1), "shard", axis=0, tiled=True)
    gains = lax.all_gather(jnp.stack([gain1, gain2]), "shard", axis=1, tiled=True).astype(F32)
    gain1_full, gain2_full = gains[0], gains[1]
    x = own_first(tokens[0]).astype(F32)
    unit1, factor1 = norm_forward(x)
    n1 = gather((unit1 * gain1_full).astype(BF), "ctx", n_ctx)
    x, unit1, factor1 = x[:short], unit1[:short], factor1[:short]
    seed_all = own_first(cotangent[0])
    seed = seed_all[:short]
    seed_all = folded(seed_all)
    dy_pair = ctx_ask(seed_all)

    def ordered(own, come, axis):
        return jnp.where(
            high == 0,
            jnp.concatenate([own, come], axis=axis),
            jnp.concatenate([come, own], axis=axis),
        )

    give_gate, give_up = wide_slice(w_gate, 1 - high, 1), wide_slice(w_up, 1 - high, 1)
    give_down = wide_slice(w_down, 1 - high, 0)
    own_gate, own_up, own_down = wide_slice(w_gate, high, 1), wide_slice(w_up, high, 1), wide_slice(w_down, high, 0)
    dy_far = pair(seed_all[:short])
    attn_full, n1, dy_far, give_gate, give_up, give_down, *dy_near = tie(
        attn_full, n1, dy_far, give_gate, give_up, give_down, *dy_pair
    )

    qkv_full, out_full = attn_full[:, : 3 * heads], attn_full[:, 3 * heads :]
    come_gate = pair(give_gate)
    dy_far = first_ask(dy_far)
    qkv = mm(n1, qkv_full)
    query = rotate(qkv[:, :heads], cosine, sine).astype(BF)
    key = rotate(qkv[:, heads : 2 * heads], cosine, sine).astype(BF)
    value = qkv[:, 2 * heads :].astype(BF)
    mixed = attend_forward(query, key, value, bias)
    mixed, come_gate, give_up, give_down, *rest = tie(mixed, come_gate, give_up, give_down, *dy_far, *dy_near)
    dy_far, dy_near = rest[:4], rest[4:]
    come_up = pair(give_up)
    gate_blocks = low_ask(ordered(own_gate, come_gate, 0))
    partial = core_give(mm_nt(mixed, out_full).astype(BF))
    partial = first_give(added(*partial))
    partial = last_give(*tie(*partial))
    come_up, give_down, n1, *rest = tie(come_up, give_down, n1, *partial, *gate_blocks)
    partial, gate_blocks = rest[:4], rest[4:]
    up_blocks = low_ask(ordered(own_up, come_up, 0))
    h1 = x + reduced(*partial).astype(F32)
    unit2, factor2 = norm_forward(h1)
    n2_short = folded((unit2 * gain2_full).astype(BF))
    n2_far = pair(n2_short)
    near = first_ask(n2_short)
    *near, gate_full = tie(*near, stacked(*gate_blocks))
    near = last_ask(*near)
    n1_folded = folded(n1)
    dy_near = stacked(*dy_near)
    n2_far, give_down, n1_folded, gate_full, dy_near, *rest = tie(
        n2_far, give_down, n1_folded, gate_full, dy_near, *near, *up_blocks, *dy_far
    )
    near, up_blocks, dy_far = rest[:4], rest[4:-4], rest[-4:]

    come_down = pair(give_down)
    far = first_ask(n2_far)
    near = core_ask(joined(*near))
    up_full = stacked(*up_blocks)
    up_full, *rest = tie(up_full, *near, *far)
    near, far = rest[:2], rest[2:]
    wide_full = jnp.concatenate([gate_full, up_full], axis=1)
    n2_near = stacked(*near)

    def wide_forward(n2):
        both = mm(n2, wide_full)
        gate, up = both[:, :units], both[:, units:]
        sigma = jax.nn.sigmoid(gate)
        silu = gate * sigma
        return (silu * up).astype(BF), silu, up * (sigma * (1.0 + gate * (1.0 - sigma)))

    def wide_backward(dy, silu, slope):
        grad_hidden = mm_nt(dy, down_full)
        return (grad_hidden * slope).astype(BF), (grad_hidden * silu).astype(BF)

    def wide_input(grad_gate, grad_up):
        return mm_nt(jnp.concatenate([grad_gate, grad_up], axis=1), wide_full).astype(BF)

    far = last_ask(*far)
    forward_near = wide_forward(n2_near)
    come_down, n2_near, *rest = tie(come_down, n2_near, *forward_near, *far, *dy_far)
    forward_near, far, dy_far = rest[:3], rest[3:7], rest[7:]
    down_blocks = low_ask(ordered(own_down, come_down, 1))
    far = core_ask(joined(*far))
    dy_near = core_ask(dy_near)
    dy_far = last_ask(*dy_far)
    *far, dy_one, dy_two, one, two, three, four = tie(*far, *dy_near, *dy_far)
    dy_near = stacked(dy_one, dy_two)
    dy_far = core_ask(joined(one, two, three, four))
    n2_far = stacked(*far)
    forward_far = wide_forward(n2_far)
    n2_far, dy_near, *rest = tie(n2_far, dy_near, *forward_far, *dy_far, *down_blocks)
    forward_far, dy_far, down_full = rest[:3], rest[3:5], jnp.concatenate(rest[5:], axis=1)
    gate_near, up_near = wide_backward(dy_near, *forward_near[1:])
    near = wide_input(gate_near, up_near)
    near, gate_near, *dy_far = tie(near, gate_near, *dy_far)
    near = core_give(near)
    dy_far = stacked(*dy_far)
    gate_far, up_far = wide_backward(dy_far, *forward_far[1:])
    gate_far, up_far, dy_far, *near = tie(gate_far, up_far, dy_far, *near)
    near = first_give(added(*near))
    far = wide_input(gate_far, up_far)
    far, dy_far, n2_far, *near = tie(far, dy_far, n2_far, *near)
    far = core_give(far)
    near = last_give(*near)
    hidden = stacked(forward_near[0], forward_far[0])
    grad_down = mm_t(hidden, stacked(dy_near, dy_far)).astype(BF)
    grad_down, gate_near, *rest = tie(grad_down, gate_near, *far, *near)
    far, near = packed(rest, 2, 4)
    near = reduced(*near)
    far = first_give(added(*far))
    down_low = low_give(grad_down, 1)
    near, gate_near, n2_far, *far = tie(near, gate_near, n2_far, *far)
    far = last_give(*far)
    n2_both = stacked(n2_near, n2_far)
    grad_gate_w = mm_t(n2_both, stacked(gate_near, gate_far)).astype(BF)
    grad_gate_w, up_near, hidden, *rest = tie(grad_gate_w, up_near, hidden, *far, *down_low)
    far, down_low = packed(rest, 4, 2)

    far = pair(reduced(*far))
    down_keep, down_give = swap(added(*down_low), 1)
    down_keep = ctx_two(down_keep)
    grad_up_w = mm_t(n2_both, stacked(up_near, up_far)).astype(BF)
    grad_up_w, hidden = tie(grad_up_w, hidden)
    result = mm(hidden, down_full).astype(BF)
    far, grad_gate_w, grad_up_w, down_give, result, *down_keep = tie(
        far, grad_gate_w, grad_up_w, down_give, result, *down_keep
    )
    gate_low = low_give(grad_gate_w, 0)
    grad_n2 = unfolded(near.astype(F32) + far.astype(F32))
    back2, grad_norm2 = norm_backward(unit2, factor2, gain2_full, grad_n2)
    grad_h1 = seed.astype(F32) + back2
    dh1 = first_ask(grad_h1.astype(BF))
    down_give, *dh1 = tie(down_give, *dh1)
    dh1 = last_ask(*dh1)
    down_come = pair(down_give)
    result, grad_up_w, *rest = tie(result, grad_up_w, *dh1, *gate_low)
    dh1, gate_low = packed(rest, 4, 2)

    middle = result.shape[0] // 2
    dh1 = core_ask(joined(*dh1))
    result_near, result_far = core_give(result[:middle]), core_give(result[middle:])
    up_low = low_give(grad_up_w, 0)
    gate_keep, gate_give = swap(added(*gate_low), 0)
    gate_keep, gate_give, *rest = tie(gate_keep, gate_give, *dh1, *result_near, *result_far)
    dh1, result_near, result_far = packed(rest, 2, 2, 2)
    dh1, result_near = stacked(*dh1), added(*result_near)
    grad_out = mm_t(mixed, dh1).astype(BF)
    share_out = lax.psum_scatter(grad_out, "shard", scatter_dimension=1, tiled=True)
    dh1, grad_out = tie(dh1, grad_out)
    result_far = first_give(added(*result_far))
    grad_mixed = mm(dh1, out_full).astype(BF)
    grad_mixed, result_near, gate_keep, gate_give, down_come, *result_far = tie(
        grad_mixed, result_near, gate_keep, gate_give, down_come, *result_far
    )
    result_far = last_give(*result_far)
    gate_come = pair(gate_give)
    gate_keep, down_come = ctx_two(gate_keep), ctx_two(down_come)
    dq, dk, dv = attend_backward(query, key, value, grad_mixed, bias, back_cosine, back_sine)
    dq, dk, dv, gate_come, result_near, *rest = tie(
        dq, dk, dv, gate_come, result_near, *result_far, *gate_keep, *down_come, *up_low
    )
    result_far, gate_keep, down_come, up_low = packed(rest, 4, chips, chips, 2)
    dqkv = jnp.concatenate([dq, dk, dv], axis=1)
    grad_qkv = mm_t(n1_folded, dqkv).astype(BF)
    result_far = reduced(*result_far)
    up_keep, up_give = swap(added(*up_low), 0)

    dqkv, grad_qkv, gate_come, up_give, up_keep, share_out, result_near, result_far, *rest = tie(
        dqkv, grad_qkv, gate_come, up_give, up_keep, share_out, result_near, result_far, *gate_keep, *down_keep, *down_come
    )
    gate_keep, down_keep, down_come = packed(rest, chips, chips, chips)
    share_qkv = low_give(grad_qkv, 0)
    grad_n1 = core_give(mm_nt(dqkv, qkv_full).astype(BF))
    up_come = pair(up_give)
    result_near = first_give(result_near)
    gate_come, up_keep = ctx_two(gate_come), ctx_two(up_keep)
    down_pieces = core_two(down_keep) + core_two(down_come)
    up_come, share_out, result_far, *rest = tie(
        up_come, share_out, result_far,
        *share_qkv, *grad_n1, *result_near, *gate_come, *up_keep, *down_pieces, *gate_keep,
    )
    share_qkv, grad_n1, result_near, *rest = packed(rest, 2, 2, 4, chips, chips, 4 * chips, chips)
    gate_come, up_keep, down_pieces, gate_keep = rest
    share_qkv, qkv_give = swap(added(*share_qkv), 0)
    qkv_come = pair(qkv_give)
    grad_n1 = first_give(added(*grad_n1))
    up_come, share_out, result_far, *rest = tie(
        up_come, share_out, result_far, *grad_n1, *result_near, *down_pieces, *gate_keep, *gate_come, *up_keep
    )
    grad_n1, result_near, *rest = packed(rest, 4, 4, 4 * chips, chips, chips, chips)
    down_pieces, gate_keep, gate_come, up_keep = rest
    grad_n1 = last_give(*grad_n1)
    share_out = ctx_two(share_out)
    (grad_d,) = place(down_pieces, both_halves, 2 * n_ctx, 1, 0)
    grad_d, up_come, result_far, *rest = tie(
        grad_d, up_come, result_far, *grad_n1, *result_near, *share_out, *gate_keep, *gate_come, *up_keep
    )
    grad_n1, result_near, *rest = packed(rest, 4, 4, chips, chips, chips, chips)
    share_out, gate_keep, gate_come, up_keep = rest
    back1, grad_norm1 = norm_backward(unit1, factor1, gain1_full, reduced(*grad_n1).astype(F32))
    input_grad = tp_ask((grad_h1 + back1).astype(BF), 0)
    up_come = ctx_two(up_come)
    gate_pieces = core_two(gate_keep) + core_two(gate_come)
    share_qkv, qkv_come, result_far, grad_norm1, *rest = tie(
        share_qkv, qkv_come, result_far, grad_norm1, *input_grad, *result_near, *up_come, *gate_pieces, *up_keep, *share_out
    )
    input_grad, result_near, *rest = packed(rest, 2, 4, chips, 4 * chips, chips, chips)
    up_come, gate_pieces, up_keep, share_out = rest
    share_qkv = ctx_two(added(share_qkv, qkv_come))
    result_far = pair(result_far)
    result_near = last_give(*result_near)
    input_grad = as_placed(stacked(*input_grad))
    (grad_g,) = place(gate_pieces, both_halves, 2 * n_ctx, 1, 1)
    grad_g, result_far, input_grad, *rest = tie(
        grad_g, result_far, input_grad, *share_qkv, *result_near, *up_come, *up_keep, *share_out
    )
    share_qkv, result_near, up_come, up_keep, share_out = packed(rest, chips, 4, chips, chips, chips)
    qkv_pieces, out_pieces = core_two(share_qkv), core_two(share_out)
    up_pieces = core_two(up_keep) + core_two(up_come)
    output = h1 + unfolded(reduced(*result_near).astype(F32) + result_far.astype(F32))
    output = as_placed(stacked(*tp_ask(output.astype(BF), 0)))

    norms = jnp.stack([grad_norm1, grad_norm2]).reshape(-1, 128)
    for axis, size in (("tp", n_tp), ("ctx", n_ctx), ("shard", n_shard)):
        for bit in bits_of(size):
            norms = norms + flip(norms, axis, bit, size)
    norms = lax.dynamic_slice_in_dim(norms.reshape(2, width), z * block, block, axis=1)

    (grad_u,) = place(up_pieces, both_halves, 2 * n_ctx, 1, 1)
    (grad_o,) = place(out_pieces, owners, n_ctx, 1, 0)
    grad_q, grad_k, grad_v = place(qkv_pieces, owners, n_ctx, 3, 1)
    return (output, input_grad, norms[0], grad_q, grad_k, grad_v, grad_o, norms[1], grad_g, grad_u, grad_d)


def solution(mesh):
    n_shard, n_ctx, n_tp = mesh.shape["shard"], mesh.shape["ctx"], mesh.shape["tp"]

    def local(*arguments):
        return body(n_shard, n_ctx, n_tp, *arguments)

    return jax.shard_map(
        local,
        mesh=mesh,
        in_specs=(
            P("shard", "ctx", None),
            P("shard", None),
            P("shard"),
            P("shard", "tp"),
            P("shard", "tp"),
            P("shard", "tp"),
            P("tp", "shard"),
            P("shard"),
            P("shard", "tp"),
            P("shard", "tp"),
            P("tp", "shard"),
            P("shard", "ctx", None),
        ),
        out_specs=(
            P("shard", "ctx", None),
            P("shard", "ctx", None),
            P("shard"),
            P("shard", "tp"),
            P("shard", "tp"),
            P("shard", "tp"),
            P("tp", "shard"),
            P("shard"),
            P("shard", "tp"),
            P("shard", "tp"),
            P("tp", "shard"),
        ),
        check_vma=False,
    )
```

time: 806 us -> 734 us (0.911)
  waiting for transfers between devices: 403 us -> 328 us
  blocking collectives: 75.6 us -> 13.5 us
  starting transfers between devices: 26.7 us -> 85.4 us
  Pallas kernels: 0 us -> 58.3 us
  matrix products: 123 us -> 73.3 us
  other arithmetic: 104 us -> 66.3 us
  local copies, waits for them, and re-layouts: 54.5 us -> 87.1 us
    all_gather x2 -> x1, waiting for transfers between devices: 137 us -> 26.9 us  [body(): lax.all_gather(jnp.concatenate(attn_pack, axis=1), 'shard', axis=0, tiled...]
    psum x1 -> x0, blocking collectives: 62.1 us -> none  [body(): norms = lax.psum(jnp.stack([grad_norm1, grad_norm2]), ('shard', 'ctx'))]
    ppermute x34 -> x103, starting transfers between devices: 26.1 us -> 85.3 us  [flip(): return lax.ppermute(values, axis, [(i, i ^ bit) for i in range(size)])]
    pallas_call x0 -> x7, Pallas kernels: none -> 58.3 us  [the longest x5 24.3 us: place(): pl.pallas_call(kernel, grid_spec=pltpu.PrefetchScalarGridSpec(num_scalar_...]
    ppermute x34 -> x103, waiting for transfers between devices: 254 us -> 301 us  [flip(): return lax.ppermute(values, axis, [(i, i ^ bit) for i in range(size)])]
    dot_general x6 -> x0, matrix products: 31.9 us -> none  [the longest x1 10.9 us: attend_backward(): jnp.einsum('qhd,khd->hqk', grad_h, heads_of(value), preferred_element_typ...]
    convert_element_type x19 -> x40, other arithmetic: 45.1 us -> 26.8 us  [the longest x35 24.8 us: added(): return (keep.astype(F32) + come.astype(F32)).astype(BF)]
    split x0 -> x33, local copies, waits for them, and re-layouts: none -> 17.9 us  [halves(): keep, give = jnp.split(values, 2, axis=dim)]
  transfers between devices with their start and end apart: 39 -> 105, of which waited for: 20 -> 47; matrix products, arithmetic and copies ran while one was open for 29% -> 19% of each run, Pallas kernels for 0% -> 7%
where the time goes in v2:
time: 734 us; the launch traced here: 729 us
  waiting for transfers between devices  328 us (45%)
  local copies, waits for them, and re-layouts  87.1 us (12%)
  starting transfers between devices  85.4 us (12%)
  matrix products  73.3 us (10%)
  other arithmetic  66.3 us (9%)
  Pallas kernels  58.3 us (8%)
  between operations  16.9 us (2%)
  blocking collectives  13.5 us (2%)
    ppermute x103, waiting for transfers between devices, flip(): return lax.ppermute(values, axis, [(i, i ^ bit) for i in range(size)])  301 us
    ppermute x103, starting transfers between devices, flip(): return lax.ppermute(values, axis, [(i, i ^ bit) for i in range(size)])  85.3 us
    unnamed x278, local copies, waits for them, and re-layouts  38.3 us
    all_gather x1, waiting for transfers between devices, body(): lax.all_gather(jnp.concatenate(attn_pack, axis=1), 'shard', axis=0, tiled...  26.9 us
    dot_general x5, matrix products, mm_t(): lax.dot_general(left, right, (((0,), (0,)), ((), ())), preferred_element_...  25.5 us
    dot_general x5, matrix products, mm(): return jnp.dot(left, right, preferred_element_type=F32)  25 us
    convert_element_type x35, other arithmetic, added(): return (keep.astype(F32) + come.astype(F32)).astype(BF)  24.8 us
    pallas_call x5, Pallas kernels, place(): pl.pallas_call(kernel, grid_spec=pltpu.PrefetchScalarGridSpec(num_scalar_...  24.3 us
  transfers between devices with their start and end apart: 105, of which 47 were waited for; matrix products, arithmetic and copies ran while one was open for 19% of the time, Pallas kernels for 7%

profile of v2, /device:TPU:0, one launch (start us, length us, event | category | flops | bytes accessed | tf_op | source)
XLA Modules:
  0.0 729.3 jit_solution(3621240913586867946)
XLA Ops:
  11.2 13.5 %all_gather.7 = bf16[2,2048]{1,0:T(2,128)(2,1)S(1)} all-gather(bf16[2,512]{1,0:T(2,128)(2,1)S(1)} %pad_maximum_fusion.33), channel_id=1, replica_groups=mesh['shard'=4,'ctx'=4,'tp'=2] {'shard'}, dimensions={1}, use_global_device_ids=true | all-gather | bytes 10240 | tf_op jit(solution)/shard_map/all_gather | solution.py:377
  34.4 20.0 %collective-permute-done = bf16[256,2048]{1,0:T(8,128)(2,1)} collective-permute-done((bf16[256,2048]{1,0:T(8,128)(2,1)S(1)}, bf16[256,2048]{1,0:T(8,128)(2,1)}, u32[]{:S(2)}, u32[]{:S(2)}) %collective-permute-start) | collective-permute-done | bytes 1048608 | tf_op jit(solution)/shard_map/ppermute | solution.py:20
  61.0 4.1 or_select_fusion.bias_ref
  73.7 16.1 %collective-permute-done.2 = bf16[128,2048]{1,0:T(8,128)(2,1)} collective-permute-done((bf16[128,2048]{1,0:T(8,128)(2,1)}, bf16[128,2048]{1,0:T(8,128)(2,1)}, u32[]{:S(2)}, u32[]{:S(2)}) %collective-permute-start.2) | collective-permute-done | bytes 524320 | tf_op jit(solution)/shard_map/ppermute | solution.py:20
  89.8 26.9 %all-gather.2.cloned.1.call-done = bf16[2048,1024]{0,1:T(8,128)(2,1)} async-done(((bf16[512,1024]{0,1:T(8,128)(2,1)}), bf16[2048,1024]{0,1:T(8,128)(2,1)}) %all-gather.2.cloned.1.call-update) | async-done | bytes 4194320 | tf_op jit(solution)/shard_map/all_gather | solution.py:376
  116.7 6.2 fusion.8
  135.2 10.9 %shard_map.221 = bf16[1024,256]{1,0:T(8,128)(2,1)S(1)} custom-call(bf16[1024,256]{1,0:T(8,128)(2,1)S(1)} %copy.51.query_ref, bf16[1024,256]{1,0:T(8,128)(2,1)S(1)} %copy.52.key_ref, bf16[1024,256]{1,0:T(8,128)(2,1)S(1)} %copy.63.value_ref, f32[1024,1024]{1,0:T(8,128)S(1)} %copy-done.2), custom_call_target="tpu_custom_call" | custom-call | flops 4294967296 | bytes 6291456 | tf_op jit(solution)/shard_map/pallas_call | solution.py:109
  146.2 5.4 collective-permute-done.4
  154.4 4.1 collective-permute-done.8
  169.7 6.0 collective-permute-done.10
  183.6 16.6 %collective-permute-done.7 = bf16[512,512]{1,0:T(8,128)(2,1)S(1)} collective-permute-done((bf16[512,512]{1,0:T(8,128)(2,1)S(1)}, bf16[512,512]{1,0:T(8,128)(2,1)S(1)}, u32[]{:S(2)}, u32[]{:S(2)}) %collective-permute-start.7) | collective-permute-done | bytes 524320 | tf_op jit(solution)/shard_map/ppermute | solution.py:20
  215.5 13.8 %collective-permute-done.14 = bf16[128,2048]{1,0:T(8,128)(2,1)S(1)} collective-permute-done((bf16[128,2048]{1,0:T(8,128)(2,1)S(1)}, bf16[128,2048]{1,0:T(8,128)(2,1)S(1)}, u32[]{:S(2)}, u32[]{:S(2)}) %collective-permute-start.14) | collective-permute-done | bytes 524320 | tf_op jit(solution)/shard_map/ppermute | solution.py:20
  229.3 11.1 %collective-permute-done.19 = bf16[1024,512]{1,0:T(8,128)(2,1)S(1)} collective-permute-done((bf16[1024,512]{1,0:T(8,128)(2,1)S(1)}, bf16[1024,512]{1,0:T(8,128)(2,1)S(1)}, u32[]{:S(2)}, u32[]{:S(2)}) %collective-permute-start.19) | collective-permute-done | bytes 1048608 | tf_op jit(solution)/shard_map/ppermute | solution.py:20
  245.3 4.3 collective-permute-done.22
  255.9 7.0 fusion.78
  265.0 3.9 collective-permute-done.20
  272.6 11.2 %collective-permute-done.29 = bf16[2,128,1024]{2,1,0:T(8,128)(2,1)S(1)} collective-permute-done((bf16[2,128,1024]{2,1,0:T(8,128)(2,1)S(1)}, bf16[2,128,1024]{2,1,0:T(8,128)(2,1)S(1)}, u32[]{:S(2)}, u32[]{:S(2)}) %collective-permute-start.29) | collective-permute-done | bytes 524320 | tf_op jit(solution)/shard_map/ppermute | solution.py:20
  287.0 4.5 fusion.79
  301.1 4.9 convolution_convert_fusion.4
  323.3 4.8 convolution_convert_fusion.3
  328.0 7.3 %collective-permute-done.34 = bf16[2,128,1024]{2,1,0:T(8,128)(2,1)S(1)} collective-permute-done((bf16[2,128,1024]{2,1,0:T(8,128)(2,1)S(1)}, bf16[2,128,1024]{2,1,0:T(8,128)(2,1)S(1)}, u32[]{:S(2)}, u32[]{:S(2)}) %collective-permute-start.34) | collective-permute-done | bytes 524320 | tf_op jit(solution)/shard_map/ppermute | solution.py:20
  340.8 6.7 fusion.4
  351.4 10.5 %collective-permute-done.39 = bf16[2,128,1024]{2,1,0:T(8,128)(2,1)S(1)} collective-permute-done((bf16[2,128,1024]{2,1,0:T(8,128)(2,1)S(1)}, bf16[2,128,1024]{2,1,0:T(8,128)(2,1)S(1)}, u32[]{:S(2)}, u32[]{:S(2)}) %collective-permute-start.39) | collective-permute-done | bytes 524320 | tf_op jit(solution)/shard_map/ppermute | solution.py:20
  366.1 5.0 convolution_convert_fusion.7
  371.2 3.7 collective-permute-done.42
  374.9 6.4 convolution_convert_fusion.6
  386.0 4.7 convolution_convert_fusion
  390.8 3.8 collective-permute-done.44.refs_1_
  394.6 13.3 %collective-permute-done.43 = bf16[128,2048]{1,0:T(8,128)(2,1)S(1)} collective-permute-done((bf16[128,2048]{1,0:T(8,128)(2,1)S(1)}, bf16[128,2048]{1,0:T(8,128)(2,1)S(1)}, u32[]{:S(2)}, u32[]{:S(2)}) %collective-permute-start.43) | collective-permute-done | bytes 524320 | tf_op jit(solution)/shard_map/ppermute | solution.py:20
  413.7 4.5 collective-permute-done.45
  421.2 9.9 %collective-permute-done.48 = bf16[2,128,1024]{2,1,0:T(8,128)(2,1)S(1)} collective-permute-done((bf16[2,128,1024]{2,1,0:T(8,128)(2,1)S(1)}, bf16[2,128,1024]{2,1,0:T(8,128)(2,1)S(1)}, u32[]{:S(2)}, u32[]{:S(2)}) %collective-permute-start.48) | collective-permute-done | bytes 524320 | tf_op jit(solution)/shard_map/ppermute | solution.py:20
  432.2 5.9 collective-permute-done.49
  467.6 4.6 add_convert_fusion.2
  480.5 29.8 %collective-permute-done.61 = bf16[1024,512]{1,0:T(8,128)(2,1)} collective-permute-done((bf16[1024,512]{1,0:T(8,128)(2,1)}, bf16[1024,512]{1,0:T(8,128)(2,1)}, u32[]{:S(2)}, u32[]{:S(2)}) %collective-permute-start.61) | collective-permute-done | bytes 1048608 | tf_op jit(solution)/shard_map/ppermute | solution.py:20
  510.4 23.1 %shard_map.222 = (bf16[1024,256]{1,0:T(8,128)(2,1)S(1)}, bf16[1024,256]{1,0:T(8,128)(2,1)S(1)}, bf16[1024,256]{1,0:T(8,128)(2,1)S(1)}) custom-call(bf16[1024,256]{1,0:T(8,128)(2,1)S(1)} %copy-done.33, bf16[1024,256]{1,0:T(8,128)(2,1)S(1)} %copy-done.31, bf16[1024,256]{1,0:T(8,128)(2,1)S(1)} %copy-done.35, ...), custom_call_target="tpu_custom_call" | custom-call | flops 8053063680 | bytes 7864320 | tf_op jit(solution)/shard_map/pallas_call | solution.py:157
  540.0 5.1 convolution_convert_fusion.5
  545.1 5.8 convolution_convert_fusion.2
  559.3 6.5 collective-permute-done.66
  568.7 12.0 %collective-permute-done.62.refs_4_ = bf16[512,512]{1,0:T(8,128)(2,1)} collective-permute-done((bf16[512,512]{1,0:T(8,128)(2,1)}, bf16[512,512]{1,0:T(8,128)(2,1)}, u32[]{:S(2)}, u32[]{:S(2)}) %collective-permute-start.62) | collective-permute-done | bytes 524320 | tf_op jit(solution)/shard_map/ppermute | solution.py:20
  581.3 8.7 %collective-permute-done.68.refs_1_ = bf16[512,512]{1,0:T(8,128)(2,1)S(1)} collective-permute-done((bf16[512,512]{1,0:T(8,128)(2,1)S(1)}, bf16[512,512]{1,0:T(8,128)(2,1)S(1)}, u32[]{:S(2)}, u32[]{:S(2)}) %collective-permute-start.68) | collective-permute-done | bytes 524320 | tf_op jit(solution)/shard_map/ppermute | solution.py:20
  592.7 10.7 %collective-permute-done.63 = bf16[1024,768]{1,0:T(8,128)(2,1)S(1)} collective-permute-done((bf16[1024,768]{1,0:T(8,128)(2,1)S(1)}, bf16[1024,768]{1,0:T(8,128)(2,1)S(1)}, u32[]{:S(2)}, u32[]{:S(2)}) %collective-permute-start.63) | collective-permute-done | bytes 1572896 | tf_op jit(solution)/shard_map/ppermute | solution.py:20
  606.7 9.6 %collective-permute-done.75 = bf16[2,128,1024]{2,1,0:T(8,128)(2,1)S(1)} collective-permute-done((bf16[2,128,1024]{2,1,0:T(8,128)(2,1)S(1)}, bf16[2,128,1024]{2,1,0:T(8,128)(2,1)S(1)}, u32[]{:S(2)}, u32[]{:S(2)}) %collective-permute-start.75) | collective-permute-done | bytes 524320 | tf_op jit(solution)/shard_map/ppermute | solution.py:20
  622.7 5.1 shard_map.223
  632.3 22.3 %collective-permute-done.73 = bf16[512,768]{1,0:T(8,128)(2,1)S(1)} collective-permute-done((bf16[512,768]{1,0:T(8,128)(2,1)S(1)}, bf16[512,768]{1,0:T(8,128)(2,1)S(1)}, u32[]{:S(2)}, u32[]{:S(2)}) %collective-permute-start.73) | collective-permute-done | bytes 786464 | tf_op jit(solution)/shard_map/ppermute | solution.py:20
  673.9 5.4 shard_map.224
  679.2 13.5 %collective-permute-done.93 = f32[32,128]{1,0:T(8,128)S(1)} collective-permute-done((f32[32,128]{1,0:T(8,128)S(1)}, f32[32,128]{1,0:T(8,128)S(1)}, u32[]{:S(2)}, u32[]{:S(2)}) %collective-permute-start.93) | collective-permute-done | bytes 16416 | tf_op jit(solution)/shard_map/ppermute | solution.py:20
  709.5 6.7 shard_map.227
  717.4 4.7 shard_map.225
  (672 shorter events, 261.5 us)
Async XLA Ops:
  7.2 109.5 %all-gather.2.cloned.1.call-start = ((), (), s32[]{:S(2)}) async-start(), calls=%async_computation.1 | async-start | bytes 5242880 | tf_op jit(solution)/shard_map/all_gather | solution.py:376
  11.1 534.0 %reduce-scatter.2.cloned.1.call-start = ((), (), s32[]{:S(2)}) async-start(), calls=%async_computation.2 | async-start | bytes 1310720 | tf_op jit(solution)/shard_map/reduce_scatter | solution.py:528
  28.1 26.2 %collective-permute-start = (bf16[256,2048]{1,0:T(8,128)(2,1)S(1)}, bf16[256,2048]{1,0:T(8,128)(2,1)}, u32[]{:S(2)}, u32[]{:S(2)}) collective-permute-start(bf16[256,2048]{1,0:T(8,128)(2,1)S(1)} %get-tuple-element.704), channel_id=1, source_target_pairs={{0,4},{2,6},{4,0},{6,2},{1,5},{3,7},{5,1},{7,3},{8,12},{10,14},{12... | collective-permute-start | bytes 3145736 | tf_op jit(solution)/shard_map/ppermute | solution.py:20
  30.8 59.0 %collective-permute-start.3 = (bf16[256,2048]{1,0:T(8,128)(2,1)}, bf16[256,2048]{1,0:T(8,128)(2,1)}, u32[]{:S(2)}, u32[]{:S(2)}) collective-permute-start(bf16[256,2048]{1,0:T(8,128)(2,1)} %pad_maximum_fusion.12), channel_id=1, source_target_pairs={{0,4},{2,6},{4,0},{6,2},{1,5},{3,7},{5,1},{7,3},{8,12},{10,14},{12... | collective-permute-start | bytes 3145736 | tf_op jit(solution)/shard_map/ppermute | solution.py:20
  33.3 56.5 %collective-permute-start.2 = (bf16[128,2048]{1,0:T(8,128)(2,1)}, bf16[128,2048]{1,0:T(8,128)(2,1)}, u32[]{:S(2)}, u32[]{:S(2)}) collective-permute-start(bf16[128,2048]{1,0:T(8,128)(2,1)} %slice.176), channel_id=1, source_target_pairs={{0,16},{8,24},{16,0},{24,8},{1,17},{9,25},{17,1},{25,9},{2,18},{10... | collective-permute-start | bytes 1572872 | tf_op jit(solution)/shard_map/ppermute | solution.py:20
  127.3 24.3 %collective-permute-start.4 = (bf16[512,512]{1,0:T(8,128)(2,1)}, bf16[512,512]{1,0:T(8,128)(2,1)}, u32[]{:S(2)}, u32[]{:S(2)}) collective-permute-start(bf16[512,512]{1,0:T(8,128)(2,1)} %get-tuple-element.324), channel_id=1, source_target_pairs={{0,16},{8,24},{16,0},{24,8},{1,17},{9,25},{17,1},{25,9},{2,18},{10... | collective-permute-start | bytes 1572872 | tf_op jit(solution)/shard_map/ppermute | solution.py:20
  130.0 16.1 %collective-permute-start.5 = (bf16[128,1024]{1,0:T(8,128)(2,1)S(1)}, bf16[128,1024]{1,0:T(8,128)(2,1)S(1)}, u32[]{:S(2)}, u32[]{:S(2)}) collective-permute-start(bf16[128,1024]{1,0:T(8,128)(2,1)S(1)} %get-tuple-element.385), channel_id=1, source_target_pairs={{0,1},{1,0},{2,3},{3,2},{4,5},{5,4},{6,7},{7,6},{8,9},{9,8},{10,11... | collective-permute-start | bytes 786440 | tf_op jit(solution)/shard_map/ppermute | solution.py:20
  166.4 35.9 %collective-permute-start.13 = (bf16[1024,512]{1,0:T(8,128)(2,1)S(1)}, bf16[1024,512]{1,0:T(8,128)(2,1)S(1)}, u32[]{:S(2)}, u32[]{:S(2)}) collective-permute-start(bf16[1024,512]{1,0:T(8,128)(2,1)S(1)} %maximum_select_fusion), channel_id=1, source_target_pairs={{0,8},{8,0},{16,24},{24,16},{1,9},{9,1},{17,25},{25,17},{2,10},{10... | collective-permute-start | bytes 3145736 | tf_op jit(solution)/shard_map/ppermute | solution.py:20
  166.5 33.7 %collective-permute-start.7 = (bf16[512,512]{1,0:T(8,128)(2,1)S(1)}, bf16[512,512]{1,0:T(8,128)(2,1)S(1)}, u32[]{:S(2)}, u32[]{:S(2)}) collective-permute-start(bf16[512,512]{1,0:T(8,128)(2,1)S(1)} %copy-done.98), channel_id=1, source_target_pairs={{0,16},{8,24},{16,0},{24,8},{1,17},{9,25},{17,1},{25,9},{2,18},{10... | collective-permute-start | bytes 1572872 | tf_op jit(solution)/shard_map/ppermute | solution.py:20
  178.4 24.0 %collective-permute-start.12 = (bf16[128,1024]{1,0:T(8,128)(2,1)S(1)}, bf16[128,1024]{1,0:T(8,128)(2,1)S(1)}, u32[]{:S(2)}, u32[]{:S(2)}) collective-permute-start(bf16[128,1024]{1,0:T(8,128)(2,1)S(1)} %get-tuple-element.767), channel_id=1, source_target_pairs={{0,4},{2,6},{4,0},{6,2},{1,5},{3,7},{5,1},{7,3},{8,12},{10,14},{12... | collective-permute-start | bytes 786440 | tf_op jit(solution)/shard_map/ppermute | solution.py:20
  181.2 21.1 %collective-permute-start.11 = (bf16[128,1024]{1,0:T(8,128)(2,1)S(1)}, bf16[128,1024]{1,0:T(8,128)(2,1)S(1)}, u32[]{:S(2)}, u32[]{:S(2)}) collective-permute-start(bf16[128,1024]{1,0:T(8,128)(2,1)S(1)} %get-tuple-element.769), channel_id=1, source_target_pairs={{0,1},{1,0},{2,3},{3,2},{4,5},{5,4},{6,7},{7,6},{8,9},{9,8},{10,11... | collective-permute-start | bytes 786440 | tf_op jit(solution)/shard_map/ppermute | solution.py:20
  204.5 24.8 %collective-permute-start.14 = (bf16[128,2048]{1,0:T(8,128)(2,1)S(1)}, bf16[128,2048]{1,0:T(8,128)(2,1)S(1)}, u32[]{:S(2)}, u32[]{:S(2)}) collective-permute-start(bf16[128,2048]{1,0:T(8,128)(2,1)S(1)} %pad_maximum_fusion.20), channel_id=1, source_target_pairs={{0,16},{8,24},{16,0},{24,8},{1,17},{9,25},{17,1},{25,9},{2,18},{10... | collective-permute-start | bytes 1572872 | tf_op jit(solution)/shard_map/ppermute | solution.py:20
  206.2 34.2 %collective-permute-start.19 = (bf16[1024,512]{1,0:T(8,128)(2,1)S(1)}, bf16[1024,512]{1,0:T(8,128)(2,1)S(1)}, u32[]{:S(2)}, u32[]{:S(2)}) collective-permute-start(bf16[1024,512]{1,0:T(8,128)(2,1)S(1)} %maximum_select_fusion.1), channel_id=1, source_target_pairs={{0,8},{8,0},{16,24},{24,16},{1,9},{9,1},{17,25},{25,17},{2,10},{10... | collective-permute-start | bytes 3145736 | tf_op jit(solution)/shard_map/ppermute | solution.py:20
  210.5 18.8 %collective-permute-start.18 = (bf16[2,128,1024]{2,1,0:T(8,128)(2,1)S(1)}, bf16[2,128,1024]{2,1,0:T(8,128)(2,1)S(1)}, u32[]{:S(2)}, u32[]{:S(2)}) collective-permute-start(bf16[2,128,1024]{2,1,0:T(8,128)(2,1)S(1)} %bitcast.113), channel_id=1, source_target_pairs={{0,1},{1,0},{2,3},{3,2},{4,5},{5,4},{6,7},{7,6},{8,9},{9,8},{10,11... | collective-permute-start | bytes 1572872 | tf_op jit(solution)/shard_map/ppermute | solution.py:20
  211.8 17.4 %collective-permute-start.17 = (bf16[256,1024]{1,0:T(8,128)(2,1)S(1)}, bf16[256,1024]{1,0:T(8,128)(2,1)S(1)}, u32[]{:S(2)}, u32[]{:S(2)}) collective-permute-start(bf16[256,1024]{1,0:T(8,128)(2,1)S(1)} %constant_dynamic-update-slice_fusion.1), channel_id=1, source_target_pairs={{0,4},{2,6},{4,0},{6,2},{1,5},{3,7},{5,1},{7,3},{8,12},{10,14},{12... | collective-permute-start | bytes 1572872 | tf_op jit(solution)/shard_map/ppermute | solution.py:20
  243.1 25.9 %collective-permute-start.20 = (bf16[512,512]{1,0:T(8,128)(2,1)S(1)}, bf16[512,512]{1,0:T(8,128)(2,1)S(1)}, u32[]{:S(2)}, u32[]{:S(2)}) collective-permute-start(bf16[512,512]{1,0:T(8,128)(2,1)S(1)} %copy-done.96), channel_id=1, source_target_pairs={{0,16},{8,24},{16,0},{24,8},{1,17},{9,25},{17,1},{25,9},{2,18},{10... | collective-permute-start | bytes 1572872 | tf_op jit(solution)/shard_map/ppermute | solution.py:20
  244.8 27.7 %collective-permute-start.27 = (bf16[512,2048]{1,0:T(8,128)(2,1)S(1)}, bf16[512,2048]{1,0:T(8,128)(2,1)S(1)}, u32[]{:S(2)}, u32[]{:S(2)}) collective-permute-start(bf16[512,2048]{1,0:T(8,128)(2,1)S(1)} %pad_maximum_fusion.5), channel_id=1, source_target_pairs={{0,2},{2,0},{4,6},{6,4},{1,3},{3,1},{5,7},{7,5},{8,10},{10,8},{12,... | collective-permute-start | bytes 6291464 | tf_op jit(solution)/shard_map/ppermute | solution.py:20
  250.1 18.9 %collective-permute-start.25 = (bf16[2,128,1024]{2,1,0:T(8,128)(2,1)S(1)}, bf16[2,128,1024]{2,1,0:T(8,128)(2,1)S(1)}, u32[]{:S(2)}, u32[]{:S(2)}) collective-permute-start(bf16[2,128,1024]{2,1,0:T(8,128)(2,1)S(1)} %bitcast.115), channel_id=1, source_target_pairs={{0,1},{1,0},{2,3},{3,2},{4,5},{5,4},{6,7},{7,6},{8,9},{9,8},{10,11... | collective-permute-start | bytes 1572872 | tf_op jit(solution)/shard_map/ppermute | solution.py:20
  251.5 17.5 %collective-permute-start.24 = (bf16[256,1024]{1,0:T(8,128)(2,1)S(1)}, bf16[256,1024]{1,0:T(8,128)(2,1)S(1)}, u32[]{:S(2)}, u32[]{:S(2)}) collective-permute-start(bf16[256,1024]{1,0:T(8,128)(2,1)S(1)} %constant_dynamic-update-slice_fusion.7), channel_id=1, source_target_pairs={{0,4},{2,6},{4,0},{6,2},{1,5},{3,7},{5,1},{7,3},{8,12},{10,14},{12... | collective-permute-start | bytes 1572872 | tf_op jit(solution)/shard_map/ppermute | solution.py:20
  272.5 24.3 %collective-permute-start.31 = (bf16[512,1024]{1,0:T(8,128)(2,1)S(1)}, bf16[512,1024]{1,0:T(8,128)(2,1)S(1)}, u32[]{:S(2)}, u32[]{:S(2)}) collective-permute-start(bf16[512,1024]{1,0:T(8,128)(2,1)S(1)} %maximum_select_fusion.2), channel_id=1, source_target_pairs={{0,8},{8,0},{16,24},{24,16},{1,9},{9,1},{17,25},{25,17},{2,10},{10... | collective-permute-start | bytes 3145736 | tf_op jit(solution)/shard_map/ppermute | solution.py:20
  350.8 24.0 %collective-permute-start.42 = (bf16[512,1024]{1,0:T(8,128)(2,1)S(1)}, bf16[512,1024]{1,0:T(8,128)(2,1)S(1)}, u32[]{:S(2)}, u32[]{:S(2)}) collective-permute-start(bf16[512,1024]{1,0:T(8,128)(2,1)S(1)} %get-tuple-element.685), channel_id=1, source_target_pairs={{0,8},{8,0},{16,24},{24,16},{1,9},{9,1},{17,25},{25,17},{2,10},{10... | collective-permute-start | bytes 3145736 | tf_op jit(solution)/shard_map/ppermute | solution.py:20
  384.2 23.7 %collective-permute-start.43 = (bf16[128,2048]{1,0:T(8,128)(2,1)S(1)}, bf16[128,2048]{1,0:T(8,128)(2,1)S(1)}, u32[]{:S(2)}, u32[]{:S(2)}) collective-permute-start(bf16[128,2048]{1,0:T(8,128)(2,1)S(1)} %pad_maximum_fusion.25), channel_id=1, source_target_pairs={{0,16},{8,24},{16,0},{24,8},{1,17},{9,25},{17,1},{25,9},{2,18},{10... | collective-permute-start | bytes 1572872 | tf_op jit(solution)/shard_map/ppermute | solution.py:20
  413.7 24.3 %collective-permute-start.49 = (bf16[1024,512]{1,0:T(8,128)(2,1)S(1)}, bf16[1024,512]{1,0:T(8,128)(2,1)S(1)}, u32[]{:S(2)}, u32[]{:S(2)}) collective-permute-start(bf16[1024,512]{1,0:T(8,128)(2,1)S(1)} %get-tuple-element.683), channel_id=1, source_target_pairs={{0,8},{8,0},{16,24},{24,16},{1,9},{9,1},{17,25},{25,17},{2,10},{10... | collective-permute-start | bytes 3145736 | tf_op jit(solution)/shard_map/ppermute | solution.py:20
  445.6 29.2 %collective-permute-start.53 = (bf16[512,512]{1,0:T(8,128)(2,1)}, bf16[512,512]{1,0:T(8,128)(2,1)S(1)}, u32[]{:S(2)}, u32[]{:S(2)}) collective-permute-start(bf16[512,512]{1,0:T(8,128)(2,1)} %get-tuple-element.474), channel_id=1, source_target_pairs={{0,16},{8,24},{16,0},{24,8},{1,17},{9,25},{17,1},{25,9},{2,18},{10... | collective-permute-start | bytes 1572872 | tf_op jit(solution)/shard_map/ppermute | solution.py:20
  450.3 60.1 %collective-permute-start.61 = (bf16[1024,512]{1,0:T(8,128)(2,1)}, bf16[1024,512]{1,0:T(8,128)(2,1)}, u32[]{:S(2)}, u32[]{:S(2)}) collective-permute-start(bf16[1024,512]{1,0:T(8,128)(2,1)} %get-tuple-element.679), channel_id=1, source_target_pairs={{0,8},{8,0},{16,24},{24,16},{1,9},{9,1},{17,25},{25,17},{2,10},{10... | collective-permute-start | bytes 3145736 | tf_op jit(solution)/shard_map/ppermute | solution.py:20
  457.8 17.0 %collective-permute-start.55 = (bf16[2,128,1024]{2,1,0:T(8,128)(2,1)}, bf16[2,128,1024]{2,1,0:T(8,128)(2,1)}, u32[]{:S(2)}, u32[]{:S(2)}) collective-permute-start(bf16[2,128,1024]{2,1,0:T(8,128)(2,1)} %get-tuple-element.715), channel_id=1, source_target_pairs={{0,1},{1,0},{2,3},{3,2},{4,5},{5,4},{6,7},{7,6},{8,9},{9,8},{10,11... | collective-permute-start | bytes 1572872 | tf_op jit(solution)/shard_map/ppermute | solution.py:20
  458.5 16.4 %collective-permute-start.54 = (bf16[256,1024]{1,0:T(8,128)(2,1)}, bf16[256,1024]{1,0:T(8,128)(2,1)S(1)}, u32[]{:S(2)}, u32[]{:S(2)}) collective-permute-start(bf16[256,1024]{1,0:T(8,128)(2,1)} %get-tuple-element.681), channel_id=1, source_target_pairs={{0,4},{2,6},{4,0},{6,2},{1,5},{3,7},{5,1},{7,3},{8,12},{10,14},{12... | collective-permute-start | bytes 1572872 | tf_op jit(solution)/shard_map/ppermute | solution.py:20
  477.0 56.5 %collective-permute-start.58 = (bf16[128,1024]{1,0:T(8,128)(2,1)S(1)}, bf16[128,1024]{1,0:T(8,128)(2,1)S(1)}, u32[]{:S(2)}, u32[]{:S(2)}) collective-permute-start(bf16[128,1024]{1,0:T(8,128)(2,1)S(1)} %get-tuple-element.747), channel_id=1, source_target_pairs={{0,4},{2,6},{4,0},{6,2},{1,5},{3,7},{5,1},{7,3},{8,12},{10,14},{12... | collective-permute-start | bytes 786440 | tf_op jit(solution)/shard_map/ppermute | solution.py:20
  478.2 55.4 %collective-permute-start.57 = (bf16[128,1024]{1,0:T(8,128)(2,1)S(1)}, bf16[128,1024]{1,0:T(8,128)(2,1)S(1)}, u32[]{:S(2)}, u32[]{:S(2)}) collective-permute-start(bf16[128,1024]{1,0:T(8,128)(2,1)S(1)} %get-tuple-element.749), channel_id=1, source_target_pairs={{0,1},{1,0},{2,3},{3,2},{4,5},{5,4},{6,7},{7,6},{8,9},{9,8},{10,11... | collective-permute-start | bytes 786440 | tf_op jit(solution)/shard_map/ppermute | solution.py:20
  479.6 54.0 %collective-permute-start.56 = (bf16[512,512]{1,0:T(8,128)(2,1)S(1)}, bf16[512,512]{1,0:T(8,128)(2,1)S(1)}, u32[]{:S(2)}, u32[]{:S(2)}) collective-permute-start(bf16[512,512]{1,0:T(8,128)(2,1)S(1)} %copy-done.110), channel_id=1, source_target_pairs={{0,16},{8,24},{16,0},{24,8},{1,17},{9,25},{17,1},{25,9},{2,18},{10... | collective-permute-start | bytes 1572872 | tf_op jit(solution)/shard_map/ppermute | solution.py:20
  480.0 53.6 %collective-permute-start.59 = (bf16[512,512]{1,0:T(8,128)(2,1)S(1)}, bf16[512,512]{1,0:T(8,128)(2,1)S(1)}, u32[]{:S(2)}, u32[]{:S(2)}) collective-permute-start(bf16[512,512]{1,0:T(8,128)(2,1)S(1)} %get-tuple-element.590.refs_0_), channel_id=1, source_target_pairs={{0,4},{2,6},{4,0},{6,2},{1,5},{3,7},{5,1},{7,3},{8,12},{10,14},{12... | collective-permute-start | bytes 1572872 | tf_op jit(solution)/shard_map/ppermute | solution.py:20
  510.4 23.3 %collective-permute-start.60 = (bf16[512,512]{1,0:T(8,128)(2,1)S(1)}, bf16[512,512]{1,0:T(8,128)(2,1)S(1)}, u32[]{:S(2)}, u32[]{:S(2)}) collective-permute-start(bf16[512,512]{1,0:T(8,128)(2,1)S(1)} %collective-permute-done.53.refs_4_), channel_id=1, source_target_pairs={{0,4},{2,6},{4,0},{6,2},{1,5},{3,7},{5,1},{7,3},{8,12},{10,14},{12... | collective-permute-start | bytes 1572872 | tf_op jit(solution)/shard_map/ppermute | solution.py:20
  551.2 52.1 %collective-permute-start.64 = (bf16[512,2048]{1,0:T(8,128)(2,1)S(1)}, bf16[512,2048]{1,0:T(8,128)(2,1)S(1)}, u32[]{:S(2)}, u32[]{:S(2)}) collective-permute-start(bf16[512,2048]{1,0:T(8,128)(2,1)S(1)} %get-tuple-element.649), channel_id=1, source_target_pairs={{0,2},{2,0},{4,6},{6,4},{1,3},{3,1},{5,7},{7,5},{8,10},{10,8},{12,... | collective-permute-start | bytes 6291464 | tf_op jit(solution)/shard_map/ppermute | solution.py:20
  556.0 24.7 %collective-permute-start.62 = (bf16[512,512]{1,0:T(8,128)(2,1)}, bf16[512,512]{1,0:T(8,128)(2,1)}, u32[]{:S(2)}, u32[]{:S(2)}) collective-permute-start(bf16[512,512]{1,0:T(8,128)(2,1)} %get-tuple-element.508), channel_id=1, source_target_pairs={{0,16},{8,24},{16,0},{24,8},{1,17},{9,25},{17,1},{25,9},{2,18},{10... | collective-permute-start | bytes 1572872 | tf_op jit(solution)/shard_map/ppermute | solution.py:20
  556.8 46.6 %collective-permute-start.63 = (bf16[1024,768]{1,0:T(8,128)(2,1)S(1)}, bf16[1024,768]{1,0:T(8,128)(2,1)S(1)}, u32[]{:S(2)}, u32[]{:S(2)}) collective-permute-start(bf16[1024,768]{1,0:T(8,128)(2,1)S(1)} %get-tuple-element.671), channel_id=1, source_target_pairs={{0,8},{8,0},{16,24},{24,16},{1,9},{9,1},{17,25},{25,17},{2,10},{10... | collective-permute-start | bytes 4718600 | tf_op jit(solution)/shard_map/ppermute | solution.py:20
  567.9 22.1 %collective-permute-start.68 = (bf16[512,512]{1,0:T(8,128)(2,1)S(1)}, bf16[512,512]{1,0:T(8,128)(2,1)S(1)}, u32[]{:S(2)}, u32[]{:S(2)}) collective-permute-start(bf16[512,512]{1,0:T(8,128)(2,1)S(1)} %get-tuple-element.628.refs_0_), channel_id=1, source_target_pairs={{0,4},{2,6},{4,0},{6,2},{1,5},{3,7},{5,1},{7,3},{8,12},{10,14},{12... | collective-permute-start | bytes 1572872 | tf_op jit(solution)/shard_map/ppermute | solution.py:20
  622.3 32.3 %collective-permute-start.73 = (bf16[512,768]{1,0:T(8,128)(2,1)S(1)}, bf16[512,768]{1,0:T(8,128)(2,1)S(1)}, u32[]{:S(2)}, u32[]{:S(2)}) collective-permute-start(bf16[512,768]{1,0:T(8,128)(2,1)S(1)} %get-tuple-element.697), channel_id=1, source_target_pairs={{0,16},{8,24},{16,0},{24,8},{1,17},{9,25},{17,1},{25,9},{2,18},{10... | collective-permute-start | bytes 2359304 | tf_op jit(solution)/shard_map/ppermute | solution.py:20
  629.9 24.7 %collective-permute-start.79 = (bf16[128,2048]{1,0:T(8,128)(2,1)S(1)}, bf16[128,2048]{1,0:T(8,128)(2,1)S(1)}, u32[]{:S(2)}, u32[]{:S(2)}) collective-permute-start(bf16[128,2048]{1,0:T(8,128)(2,1)S(1)} %fusion.29), channel_id=1, source_target_pairs={{0,1},{1,0},{2,3},{3,2},{4,5},{5,4},{6,7},{7,6},{8,9},{9,8},{10,11... | collective-permute-start | bytes 1572872 | tf_op jit(solution)/shard_map/ppermute | solution.py:20
  631.3 23.9 %collective-permute-start.80 = (bf16[512,512]{1,0:T(8,128)(2,1)}, bf16[512,512]{1,0:T(8,128)(2,1)}, u32[]{:S(2)}, u32[]{:S(2)}) collective-permute-start(bf16[512,512]{1,0:T(8,128)(2,1)} %collective-permute-done.62.refs_4_), channel_id=1, source_target_pairs={{0,4},{2,6},{4,0},{6,2},{1,5},{3,7},{5,1},{7,3},{8,12},{10,14},{12... | collective-permute-start | bytes 1572872 | tf_op jit(solution)/shard_map/ppermute | solution.py:20
  631.7 23.4 %collective-permute-start.81 = (bf16[512,512]{1,0:T(8,128)(2,1)S(1)}, bf16[512,512]{1,0:T(8,128)(2,1)S(1)}, u32[]{:S(2)}, u32[]{:S(2)}) collective-permute-start(bf16[512,512]{1,0:T(8,128)(2,1)S(1)} %get-tuple-element.590.refs_0_), channel_id=1, source_target_pairs={{0,2},{2,0},{4,6},{6,4},{1,3},{3,1},{5,7},{7,5},{8,10},{10,8},{12,... | collective-permute-start | bytes 1572872 | tf_op jit(solution)/shard_map/ppermute | solution.py:20
  631.7 23.4 %collective-permute-start.82 = (bf16[512,512]{1,0:T(8,128)(2,1)S(1)}, bf16[512,512]{1,0:T(8,128)(2,1)S(1)}, u32[]{:S(2)}, u32[]{:S(2)}) collective-permute-start(bf16[512,512]{1,0:T(8,128)(2,1)S(1)} %copy-done.10), channel_id=1, source_target_pairs={{0,2},{2,0},{4,6},{6,4},{1,3},{3,1},{5,7},{7,5},{8,10},{10,8},{12,... | collective-permute-start | bytes 1572872 | tf_op jit(solution)/shard_map/ppermute | solution.py:20
  659.2 33.6 %collective-permute-start.88 = (bf16[128,1024]{1,0:T(8,128)(2,1)}, bf16[128,1024]{1,0:T(8,128)(2,1)}, u32[]{:S(2)}, u32[]{:S(2)}) collective-permute-start(bf16[128,1024]{1,0:T(8,128)(2,1)} %get-tuple-element.739), channel_id=1, source_target_pairs={{0,4},{2,6},{4,0},{6,2},{1,5},{3,7},{5,1},{7,3},{8,12},{10,14},{12... | collective-permute-start | bytes 786440 | tf_op jit(solution)/shard_map/ppermute | solution.py:20
  662.9 29.8 %collective-permute-start.87 = (bf16[128,1024]{1,0:T(8,128)(2,1)S(1)}, bf16[128,1024]{1,0:T(8,128)(2,1)S(1)}, u32[]{:S(2)}, u32[]{:S(2)}) collective-permute-start(bf16[128,1024]{1,0:T(8,128)(2,1)S(1)} %get-tuple-element.741), channel_id=1, source_target_pairs={{0,1},{1,0},{2,3},{3,2},{4,5},{5,4},{6,7},{7,6},{8,9},{9,8},{10,11... | collective-permute-start | bytes 786440 | tf_op jit(solution)/shard_map/ppermute | solution.py:20
  666.5 26.3 %collective-permute-start.86 = (bf16[512,768]{1,0:T(8,128)(2,1)S(1)}, bf16[512,768]{1,0:T(8,128)(2,1)S(1)}, u32[]{:S(2)}, u32[]{:S(2)}) collective-permute-start(bf16[512,768]{1,0:T(8,128)(2,1)S(1)} %add_convert_fusion.10.refs_0_), channel_id=1, source_target_pairs={{0,4},{2,6},{4,0},{6,2},{1,5},{3,7},{5,1},{7,3},{8,12},{10,14},{12... | collective-permute-start | bytes 2359304 | tf_op jit(solution)/shard_map/ppermute | solution.py:20
  668.0 24.8 %collective-permute-start.85 = (bf16[128,2048]{1,0:T(8,128)(2,1)S(1)}, bf16[128,2048]{1,0:T(8,128)(2,1)S(1)}, u32[]{:S(2)}, u32[]{:S(2)}) collective-permute-start(bf16[128,2048]{1,0:T(8,128)(2,1)S(1)} %copy-done.106), channel_id=1, source_target_pairs={{0,16},{8,24},{16,0},{24,8},{1,17},{9,25},{17,1},{25,9},{2,18},{10... | collective-permute-start | bytes 1572872 | tf_op jit(solution)/shard_map/ppermute | solution.py:20
  670.2 22.6 %collective-permute-start.93 = (f32[32,128]{1,0:T(8,128)S(1)}, f32[32,128]{1,0:T(8,128)S(1)}, u32[]{:S(2)}, u32[]{:S(2)}) collective-permute-start(f32[32,128]{1,0:T(8,128)S(1)} %add.537), channel_id=1, source_target_pairs={{0,16},{8,24},{16,0},{24,8},{1,17},{9,25},{17,1},{25,9},{2,18},{10... | collective-permute-start | bytes 49160 | tf_op jit(solution)/shard_map/ppermute | solution.py:20
  699.2 17.0 %collective-permute-start.89 = (bf16[128,2048]{1,0:T(8,128)(2,1)}, bf16[128,2048]{1,0:T(8,128)(2,1)}, u32[]{:S(2)}, u32[]{:S(2)}) collective-permute-start(bf16[128,2048]{1,0:T(8,128)(2,1)} %get-tuple-element.638), channel_id=1, source_target_pairs={{0,1},{1,0},{2,3},{3,2},{4,5},{5,4},{6,7},{7,6},{8,9},{9,8},{10,11... | collective-permute-start | bytes 1572872 | tf_op jit(solution)/shard_map/ppermute | solution.py:20
  701.3 16.1 %collective-permute-start.95 = (bf16[512,768]{1,0:T(8,128)(2,1)S(1)}, bf16[512,768]{1,0:T(8,128)(2,1)S(1)}, u32[]{:S(2)}, u32[]{:S(2)}) collective-permute-start(bf16[512,768]{1,0:T(8,128)(2,1)S(1)} %add_convert_fusion.10.refs_0_), channel_id=1, source_target_pairs={{0,2},{2,0},{4,6},{6,4},{1,3},{3,1},{5,7},{7,5},{8,10},{10,8},{12,... | collective-permute-start | bytes 2359304 | tf_op jit(solution)/shard_map/ppermute | solution.py:20
  (189 other events, 2026.4 us)
Sparse Core Ops, SparseCore 0:
  11.2 105.4 all-gather.1
  467.7 41.5 reduce-scatter.1

commit v3 on v2

--- a/solution.py
+++ b/solution.py
@@ -184,7 +184,7 @@
 
 
 def place(pieces, targets, blocks, parts, axis):
-    rows, columns = pieces[0].shape[0], pieces[0].shape[1] // parts
+    rows, columns = pieces[0][0].shape[1], pieces[0][0].shape[2] // parts
     total = len(pieces)
 
     def kernel(targets_ref, *refs):
@@ -206,7 +206,9 @@
         grid_spec=pltpu.PrefetchScalarGridSpec(
             num_scalar_prefetch=1,
             grid=(total,),
-            in_specs=[pl.BlockSpec((rows, parts * columns), lambda i, t: (0, 0))] * total,
+            in_specs=[
+                pl.BlockSpec((None, rows, parts * columns), lambda i, t, at=at: (at, 0, 0)) for _, at in pieces
+            ],
             out_specs=[pl.BlockSpec((rows, columns), go) for _ in range(parts)],
         ),
         out_shape=[jax.ShapeDtypeStruct(shape, F32) for _ in range(parts)],
@@ -214,7 +216,7 @@
         cost_estimate=pl.CostEstimate(
             flops=0, transcendentals=0, bytes_accessed=6 * parts * rows * columns * blocks
         ),
-    )(targets, *pieces)
+    )(targets, *[array for array, _ in pieces])
 
 
 def body(n_shard, n_ctx, n_tp, *arguments):
@@ -274,12 +276,13 @@
             values = reduce_step(values, "tp", bit, n_tp, dim)
         return halves(values, "tp", tp_bits[0], n_tp, dim)
 
-    def first_give(values):
-        right = values[:, half:].reshape(chips, n_tp * short, half)
-        return ctx_give(values[:, :half]) + tp_give(right, 1)
+    def first_give(left, right=None):
+        if right is None:
+            left, right = left[:, :half], left[:, half:]
+        return ctx_give(left) + tp_give(right.reshape(chips, n_tp * short, right.shape[1]), 1)
 
     def last_give(keep, come, other_keep, other_come):
-        right = added(other_keep, other_come).reshape(chips * short, half)
+        right = added(other_keep, other_come).reshape(chips * short, keep.shape[1])
         return tp_give(added(keep, come), 0) + ctx_give(right)
 
     def reduced(keep, come, other_keep, other_come):
@@ -402,7 +405,7 @@
 
     qkv_full, out_full = attn_full[:, : 3 * heads], attn_full[:, 3 * heads :]
     come_gate = pair(give_gate)
-    dy_far = first_ask(dy_far)
+    dy_far = last_ask(*first_ask(dy_far))
     qkv = mm(n1, qkv_full)
     query = rotate(qkv[:, :heads], cosine, sine).astype(BF)
     key = rotate(qkv[:, heads : 2 * heads], cosine, sine).astype(BF)
@@ -462,153 +465,147 @@
     down_blocks = low_ask(ordered(own_down, come_down, 1))
     far = core_ask(joined(*far))
     dy_near = core_ask(dy_near)
-    dy_far = last_ask(*dy_far)
-    *far, dy_one, dy_two, one, two, three, four = tie(*far, *dy_near, *dy_far)
+    dy_far = core_ask(joined(*dy_far))
+    *far, dy_one, dy_two, one, two = tie(*far, *dy_near, *dy_far)
     dy_near = stacked(dy_one, dy_two)
-    dy_far = core_ask(joined(one, two, three, four))
+    dy_far = [one, two]
     n2_far = stacked(*far)
     forward_far = wide_forward(n2_far)
     n2_far, dy_near, *rest = tie(n2_far, dy_near, *forward_far, *dy_far, *down_blocks)
     forward_far, dy_far, down_full = rest[:3], rest[3:5], jnp.concatenate(rest[5:], axis=1)
     gate_near, up_near = wide_backward(dy_near, *forward_near[1:])
     near = wide_input(gate_near, up_near)
-    near, gate_near, *dy_far = tie(near, gate_near, *dy_far)
+    near, gate_near, dy_near, n2_near, *dy_far = tie(near, gate_near, dy_near, n2_near, *dy_far)
     near = core_give(near)
     dy_far = stacked(*dy_far)
     gate_far, up_far = wide_backward(dy_far, *forward_far[1:])
-    gate_far, up_far, dy_far, *near = tie(gate_far, up_far, dy_far, *near)
+    gate_far, up_far, dy_far, dy_near, n2_near, *near = tie(gate_far, up_far, dy_far, dy_near, n2_near, *near)
     near = first_give(added(*near))
     far = wide_input(gate_far, up_far)
-    far, dy_far, n2_far, *near = tie(far, dy_far, n2_far, *near)
+    far, dy_far, dy_near, n2_far, n2_near, *near = tie(far, dy_far, dy_near, n2_far, n2_near, *near)
     far = core_give(far)
     near = last_give(*near)
-    hidden = stacked(forward_near[0], forward_far[0])
-    grad_down = mm_t(hidden, stacked(dy_near, dy_far)).astype(BF)
-    grad_down, gate_near, *rest = tie(grad_down, gate_near, *far, *near)
+    hidden_near, hidden_far = forward_near[0], forward_far[0]
+    grad_down = mm_t(stacked(hidden_near, hidden_far), stacked(dy_near, dy_far)).astype(BF)
+    grad_down, gate_near, hidden_near, n2_near, *rest = tie(grad_down, gate_near, hidden_near, n2_near, *far, *near)
     far, near = packed(rest, 2, 4)
     near = reduced(*near)
     far = first_give(added(*far))
     down_low = low_give(grad_down, 1)
-    near, gate_near, n2_far, *far = tie(near, gate_near, n2_far, *far)
+    near, gate_near, hidden_near, n2_far, n2_near, *far = tie(near, gate_near, hidden_near, n2_far, n2_near, *far)
     far = last_give(*far)
     n2_both = stacked(n2_near, n2_far)
-    grad_gate_w = mm_t(n2_both, stacked(gate_near, gate_far)).astype(BF)
-    grad_gate_w, up_near, hidden, *rest = tie(grad_gate_w, up_near, hidden, *far, *down_low)
+    n2_both, up_near, gate_near, hidden_near, *rest = tie(n2_both, up_near, gate_near, hidden_near, *far, *down_low)
     far, down_low = packed(rest, 4, 2)
 
     far = pair(reduced(*far))
     down_keep, down_give = swap(added(*down_low), 1)
     down_keep = ctx_two(down_keep)
-    grad_up_w = mm_t(n2_both, stacked(up_near, up_far)).astype(BF)
-    grad_up_w, hidden = tie(grad_up_w, hidden)
-    result = mm(hidden, down_full).astype(BF)
-    far, grad_gate_w, grad_up_w, down_give, result, *down_keep = tie(
-        far, grad_gate_w, grad_up_w, down_give, result, *down_keep
+    grad_gate_w = mm_t(n2_both, stacked(gate_near, gate_far)).astype(BF)
+    middle = n1.shape[0] // 2
+    result_keep, result_give = [
+        mm(stacked(hidden_near[part], hidden_far[part]), down_full).astype(BF)
+        for part in (slice(None, middle), slice(middle, None))
+    ]
+    far, grad_gate_w, up_near, n2_both, down_give, result_keep, result_give, *down_keep = tie(
+        far, grad_gate_w, up_near, n2_both, down_give, result_keep, result_give, *down_keep
     )
     gate_low = low_give(grad_gate_w, 0)
+    down_come = pair(down_give)
     grad_n2 = unfolded(near.astype(F32) + far.astype(F32))
     back2, grad_norm2 = norm_backward(unit2, factor2, gain2_full, grad_n2)
     grad_h1 = seed.astype(F32) + back2
-    dh1 = first_ask(grad_h1.astype(BF))
-    down_give, *dh1 = tie(down_give, *dh1)
-    dh1 = last_ask(*dh1)
-    down_come = pair(down_give)
-    result, grad_up_w, *rest = tie(result, grad_up_w, *dh1, *gate_low)
+    dh1 = last_ask(*first_ask(grad_h1.astype(BF)))
+    grad_up_w = mm_t(n2_both, stacked(up_near, up_far)).astype(BF)
+    result = added(result_keep, flip(result_give, "ctx", 1, n_ctx))
+    grad_up_w, result, down_come, *rest = tie(grad_up_w, result, down_come, *dh1, *gate_low)
     dh1, gate_low = packed(rest, 4, 2)
 
-    middle = result.shape[0] // 2
-    dh1 = core_ask(joined(*dh1))
-    result_near, result_far = core_give(result[:middle]), core_give(result[middle:])
+    dh1_own = joined(*dh1)
+    dh1_come = flip(dh1_own, "ctx", 1, n_ctx)
     up_low = low_give(grad_up_w, 0)
+    down_keep = core_two(down_keep)
+    mixed_own, out_own = mm(dh1_own, out_full).astype(BF), mm_t(mixed[:middle], dh1_own)
+    result, dh1_come, mixed_own, out_own, *rest = tie(result, dh1_come, mixed_own, out_own, *gate_low, *down_keep)
+    gate_low, down_keep = packed(rest, 2, 2 * chips)
+    result = first_give(result[:middle], result[middle:])
+    grad_out = (out_own + mm_t(mixed[middle:], dh1_come)).astype(BF)
+    share_out = lax.psum_scatter(grad_out, "shard", scatter_dimension=1, tiled=True)
+    dh1_come, grad_out = tie(dh1_come, grad_out)
     gate_keep, gate_give = swap(added(*gate_low), 0)
-    gate_keep, gate_give, *rest = tie(gate_keep, gate_give, *dh1, *result_near, *result_far)
-    dh1, result_near, result_far = packed(rest, 2, 2, 2)
-    dh1, result_near = stacked(*dh1), added(*result_near)
-    grad_out = mm_t(mixed, dh1).astype(BF)
-    share_out = lax.psum_scatter(grad_out, "shard", scatter_dimension=1, tiled=True)
-    dh1, grad_out = tie(dh1, grad_out)
-    result_far = first_give(added(*result_far))
-    grad_mixed = mm(dh1, out_full).astype(BF)
-    grad_mixed, result_near, gate_keep, gate_give, down_come, *result_far = tie(
-        grad_mixed, result_near, gate_keep, gate_give, down_come, *result_far
-    )
-    result_far = last_give(*result_far)
+    grad_mixed = stacked(mixed_own, mm(dh1_come, out_full).astype(BF))
     gate_come = pair(gate_give)
-    gate_keep, down_come = ctx_two(gate_keep), ctx_two(down_come)
+    gate_keep = ctx_two(gate_keep)
     dq, dk, dv = attend_backward(query, key, value, grad_mixed, bias, back_cosine, back_sine)
-    dq, dk, dv, gate_come, result_near, *rest = tie(
-        dq, dk, dv, gate_come, result_near, *result_far, *gate_keep, *down_come, *up_low
-    )
-    result_far, gate_keep, down_come, up_low = packed(rest, 4, chips, chips, 2)
+    dq, dk, dv, gate_come, down_come, *rest = tie(dq, dk, dv, gate_come, down_come, *result, *gate_keep, *up_low)
+    result, gate_keep, up_low = packed(rest, 4, chips, 2)
     dqkv = jnp.concatenate([dq, dk, dv], axis=1)
     grad_qkv = mm_t(n1_folded, dqkv).astype(BF)
-    result_far = reduced(*result_far)
-    up_keep, up_give = swap(added(*up_low), 0)
-
-    dqkv, grad_qkv, gate_come, up_give, up_keep, share_out, result_near, result_far, *rest = tie(
-        dqkv, grad_qkv, gate_come, up_give, up_keep, share_out, result_near, result_far, *gate_keep, *down_keep, *down_come
-    )
-    gate_keep, down_keep, down_come = packed(rest, chips, chips, chips)
+
+    dqkv, grad_qkv, gate_come, down_come, share_out, *rest = tie(
+        dqkv, grad_qkv, gate_come, down_come, share_out, *result, *up_low, *gate_keep
+    )
+    result, up_low, gate_keep = packed(rest, 4, 2, chips)
     share_qkv = low_give(grad_qkv, 0)
     grad_n1 = core_give(mm_nt(dqkv, qkv_full).astype(BF))
+    up_keep, up_give = swap(added(*up_low), 0)
     up_come = pair(up_give)
-    result_near = first_give(result_near)
-    gate_come, up_keep = ctx_two(gate_come), ctx_two(up_keep)
-    down_pieces = core_two(down_keep) + core_two(down_come)
-    up_come, share_out, result_far, *rest = tie(
-        up_come, share_out, result_far,
-        *share_qkv, *grad_n1, *result_near, *gate_come, *up_keep, *down_pieces, *gate_keep,
-    )
-    share_qkv, grad_n1, result_near, *rest = packed(rest, 2, 2, 4, chips, chips, 4 * chips, chips)
-    gate_come, up_keep, down_pieces, gate_keep = rest
+    result = last_give(*result)
+    three = jnp.stack([gate_come, down_come, up_keep])
+    three, *rest = tie(three, *grad_n1, *result, *gate_keep)
+    grad_n1, result, gate_keep = packed(rest, 2, 4, chips)
+    three, gate_keep = ctx_two(three), core_two(gate_keep)
+    grad_n1 = added(*grad_n1)
+    result_near, result_far = added(*result[:2]), pair(added(*result[2:]))
+    up_come, grad_n1, result_near, result_far, *rest = tie(
+        up_come, grad_n1, result_near, result_far, *share_qkv, *three, *gate_keep, *ctx_two(share_out)
+    )
+    share_qkv, three, gate_keep, share_out = packed(rest, 2, chips, 2 * chips, chips)
     share_qkv, qkv_give = swap(added(*share_qkv), 0)
     qkv_come = pair(qkv_give)
-    grad_n1 = first_give(added(*grad_n1))
-    up_come, share_out, result_far, *rest = tie(
-        up_come, share_out, result_far, *grad_n1, *result_near, *down_pieces, *gate_keep, *gate_come, *up_keep
-    )
-    grad_n1, result_near, *rest = packed(rest, 4, 4, 4 * chips, chips, chips, chips)
-    down_pieces, gate_keep, gate_come, up_keep = rest
+    grad_n1 = first_give(grad_n1)
+    three = core_two(three)
+    output = (h1 + unfolded(result_near.astype(F32) + result_far.astype(F32))).astype(BF)
+    up_come, output, *rest = tie(up_come, output, *grad_n1, *three)
+    grad_n1, three = packed(rest, 4, 2 * chips)
     grad_n1 = last_give(*grad_n1)
-    share_out = ctx_two(share_out)
-    (grad_d,) = place(down_pieces, both_halves, 2 * n_ctx, 1, 0)
-    grad_d, up_come, result_far, *rest = tie(
-        grad_d, up_come, result_far, *grad_n1, *result_near, *share_out, *gate_keep, *gate_come, *up_keep
-    )
-    grad_n1, result_near, *rest = packed(rest, 4, 4, chips, chips, chips, chips)
-    share_out, gate_keep, gate_come, up_keep = rest
+    up_come, output = ctx_two(up_come), tp_ask(output, 0)
+    (grad_g,) = place(
+        [(v[None], 0) for v in gate_keep] + [(v, 0) for v in three], both_halves, 2 * n_ctx, 1, 1
+    )
+    (grad_d,) = place(
+        [(v[None], 0) for v in down_keep] + [(v, 1) for v in three], both_halves, 2 * n_ctx, 1, 0
+    )
+    qkv_come, share_qkv, grad_g, grad_d, *rest = tie(
+        qkv_come, share_qkv, grad_g, grad_d, *grad_n1, *up_come, *output
+    )
+    grad_n1, up_come, output = packed(rest, 4, chips, 2)
+    share_qkv = ctx_two(added(share_qkv, qkv_come))
     back1, grad_norm1 = norm_backward(unit1, factor1, gain1_full, reduced(*grad_n1).astype(F32))
-    input_grad = tp_ask((grad_h1 + back1).astype(BF), 0)
-    up_come = ctx_two(up_come)
-    gate_pieces = core_two(gate_keep) + core_two(gate_come)
-    share_qkv, qkv_come, result_far, grad_norm1, *rest = tie(
-        share_qkv, qkv_come, result_far, grad_norm1, *input_grad, *result_near, *up_come, *gate_pieces, *up_keep, *share_out
-    )
-    input_grad, result_near, *rest = packed(rest, 2, 4, chips, 4 * chips, chips, chips)
-    up_come, gate_pieces, up_keep, share_out = rest
-    share_qkv = ctx_two(added(share_qkv, qkv_come))
-    result_far = pair(result_far)
-    result_near = last_give(*result_near)
+    input_grad, output = tp_ask((grad_h1 + back1).astype(BF), 0), as_placed(stacked(*output))
+    norms = jnp.stack([grad_norm1, grad_norm2]).reshape(-1, 128)
+
+    def met(values, axis, bits, size):
+        for bit in bits:
+            values = values + flip(values, axis, bit, size)
+        return values
+
+    norms, up_come = met(norms, "tp", tp_bits, n_tp), core_two(up_come)
+    norms, output, *rest = tie(norms, output, *share_qkv, *input_grad, *up_come)
+    share_qkv, input_grad, up_come = packed(rest, chips, 2, 2 * chips)
+    norms, share_qkv, share_out = met(norms, "ctx", [1], n_ctx), core_two(share_qkv), core_two(share_out)
     input_grad = as_placed(stacked(*input_grad))
-    (grad_g,) = place(gate_pieces, both_halves, 2 * n_ctx, 1, 1)
-    grad_g, result_far, input_grad, *rest = tie(
-        grad_g, result_far, input_grad, *share_qkv, *result_near, *up_come, *up_keep, *share_out
-    )
-    share_qkv, result_near, up_come, up_keep, share_out = packed(rest, chips, 4, chips, chips, chips)
-    qkv_pieces, out_pieces = core_two(share_qkv), core_two(share_out)
-    up_pieces = core_two(up_keep) + core_two(up_come)
-    output = h1 + unfolded(reduced(*result_near).astype(F32) + result_far.astype(F32))
-    output = as_placed(stacked(*tp_ask(output.astype(BF), 0)))
-
-    norms = jnp.stack([grad_norm1, grad_norm2]).reshape(-1, 128)
-    for axis, size in (("tp", n_tp), ("ctx", n_ctx), ("shard", n_shard)):
-        for bit in bits_of(size):
-            norms = norms + flip(norms, axis, bit, size)
+    (grad_u,) = place([(v, 2) for v in three] + [(v[None], 0) for v in up_come], both_halves, 2 * n_ctx, 1, 1)
+    grad_u, norms, *rest = tie(grad_u, norms, *share_qkv, *share_out)
+    share_qkv, share_out = packed(rest, 2 * chips, 2 * chips)
+    norms = met(norms, "ctx", far_bits, n_ctx)
+    (grad_o,) = place([(v[None], 0) for v in share_out], owners, n_ctx, 1, 0)
+    grad_o, norms, *share_qkv = tie(grad_o, norms, *share_qkv)
+    norms = met(norms, "shard", low_bits, n_shard)
+    grad_q, grad_k, grad_v = place([(v[None], 0) for v in share_qkv], owners, n_ctx, 3, 1)
+    grad_q, grad_k, grad_v, norms = tie(grad_q, grad_k, grad_v, norms)
+    norms = met(norms, "shard", [top], n_shard)
     norms = lax.dynamic_slice_in_dim(norms.reshape(2, width), z * block, block, axis=1)
-
-    (grad_u,) = place(up_pieces, both_halves, 2 * n_ctx, 1, 1)
-    (grad_o,) = place(out_pieces, owners, n_ctx, 1, 0)
-    grad_q, grad_k, grad_v = place(qkv_pieces, owners, n_ctx, 3, 1)
     return (output, input_grad, norms[0], grad_q, grad_k, grad_v, grad_o, norms[1], grad_g, grad_u, grad_d)
 
 

time: 734 us -> 696 us (0.948)
  waiting for transfers between devices: 328 us -> 297 us
  local copies, waits for them, and re-layouts: 87.1 us -> 68.7 us
  other arithmetic: 66.3 us -> 81.3 us
  starting transfers between devices: 85.4 us -> 73.4 us
  matrix products: 73.3 us -> 82.8 us
    ppermute x103 -> x92, waiting for transfers between devices: 301 us -> 270 us  [flip(): return lax.ppermute(values, axis, [(i, i ^ bit) for i in range(size)])]
    ppermute x103 -> x92, starting transfers between devices: 85.3 us -> 73.3 us  [flip(): return lax.ppermute(values, axis, [(i, i ^ bit) for i in range(size)])]
    unnamed x278 -> x251, local copies, waits for them, and re-layouts: 38.3 us -> 27.9 us
    concatenate x4 -> x6, other arithmetic: 2.63 us -> 11.1 us  [stacked(): return jnp.concatenate(parts, axis=0)]
    dot_general x5 -> x7, matrix products: 25 us -> 28.4 us  [mm(): return jnp.dot(left, right, preferred_element_type=F32)]
    dot_general x5 -> x6, matrix products: 25.5 us -> 28.9 us  [mm_t(): lax.dot_general(left, right, (((0,), (0,)), ((), ())), preferred_element_...]
    split x33 -> x28, local copies, waits for them, and re-layouts: 17.9 us -> 16.3 us  [halves(): keep, give = jnp.split(values, 2, axis=dim)]
    convert_element_type x35 -> x30, other arithmetic: 24.8 us -> 24.6 us  [added(): return (keep.astype(F32) + come.astype(F32)).astype(BF)]
  transfers between devices with their start and end apart: 105 -> 94, of which waited for: 47 -> 41; matrix products, arithmetic and copies ran while one was open for 19% -> 24% of each run, Pallas kernels for 7% -> 8%
where the time goes in v3:
time: 696 us; the launch traced here: 692 us
  waiting for transfers between devices  297 us (43%)
  matrix products  82.8 us (12%)
  other arithmetic  81.3 us (12%)
  starting transfers between devices  73.4 us (11%)
  local copies, waits for them, and re-layouts  68.7 us (10%)
  Pallas kernels  57.9 us (8%)
  between operations  16.6 us (2%)
  blocking collectives  13.5 us (2%)
    ppermute x92, waiting for transfers between devices, flip(): return lax.ppermute(values, axis, [(i, i ^ bit) for i in range(size)])  270 us
    ppermute x92, starting transfers between devices, flip(): return lax.ppermute(values, axis, [(i, i ^ bit) for i in range(size)])  73.3 us
    dot_general x6, matrix products, mm_t(): lax.dot_general(left, right, (((0,), (0,)), ((), ())), preferred_element_...  28.9 us
    dot_general x7, matrix products, mm(): return jnp.dot(left, right, preferred_element_type=F32)  28.4 us
    unnamed x251, local copies, waits for them, and re-layouts  27.9 us
    all_gather x1, waiting for transfers between devices, body(): lax.all_gather(jnp.concatenate(attn_pack, axis=1), 'shard', axis=0, tiled...  26.9 us
    dot_general x6, matrix products, mm_nt(): lax.dot_general(left, right, (((1,), (1,)), ((), ())), preferred_element_...  25.5 us
    convert_element_type x30, other arithmetic, added(): return (keep.astype(F32) + come.astype(F32)).astype(BF)  24.6 us
  transfers between devices with their start and end apart: 94, of which 41 were waited for; matrix products, arithmetic and copies ran while one was open for 24% of the time, Pallas kernels for 8%

profile of v3, /device:TPU:0, one launch (start us, length us, event | category | flops | bytes accessed | tf_op | source)
XLA Modules:
  0.0 691.5 jit_solution(1104716601006591282)
XLA Ops:
  11.2 13.5 %all_gather.7 = bf16[2,2048]{1,0:T(2,128)(2,1)S(1)} all-gather(bf16[2,512]{1,0:T(2,128)(2,1)S(1)} %pad_maximum_fusion.37), channel_id=1, replica_groups=mesh['shard'=4,'ctx'=4,'tp'=2] {'shard'}, dimensions={1}, use_global_device_ids=true | all-gather | bytes 10240 | tf_op jit(solution)/shard_map/all_gather | solution.py:380
  34.3 20.0 %collective-permute-done = bf16[256,2048]{1,0:T(8,128)(2,1)} collective-permute-done((bf16[256,2048]{1,0:T(8,128)(2,1)S(1)}, bf16[256,2048]{1,0:T(8,128)(2,1)}, u32[]{:S(2)}, u32[]{:S(2)}) %collective-permute-start) | collective-permute-done | bytes 1048608 | tf_op jit(solution)/shard_map/ppermute | solution.py:20
  61.0 4.1 or_select_fusion.bias_ref
  73.7 16.1 %collective-permute-done.2 = bf16[128,2048]{1,0:T(8,128)(2,1)} collective-permute-done((bf16[128,2048]{1,0:T(8,128)(2,1)}, bf16[128,2048]{1,0:T(8,128)(2,1)}, u32[]{:S(2)}, u32[]{:S(2)}) %collective-permute-start.2) | collective-permute-done | bytes 524320 | tf_op jit(solution)/shard_map/ppermute | solution.py:20
  89.8 26.9 %all-gather.2.cloned.1.call-done = bf16[2048,1024]{0,1:T(8,128)(2,1)} async-done(((bf16[512,1024]{0,1:T(8,128)(2,1)}), bf16[2048,1024]{0,1:T(8,128)(2,1)}) %all-gather.2.cloned.1.call-update) | async-done | bytes 4194320 | tf_op jit(solution)/shard_map/all_gather | solution.py:379
  120.8 6.2 fusion.8
  139.2 10.9 %shard_map.221 = bf16[1024,256]{1,0:T(8,128)(2,1)S(1)} custom-call(bf16[1024,256]{1,0:T(8,128)(2,1)S(1)} %copy.55.query_ref, bf16[1024,256]{1,0:T(8,128)(2,1)S(1)} %copy.56.key_ref, bf16[1024,256]{1,0:T(8,128)(2,1)S(1)} %copy.63.value_ref, f32[1024,1024]{1,0:T(8,128)S(1)} %copy-done.6), custom_call_target="tpu_custom_call" | custom-call | flops 4294967296 | bytes 6291456 | tf_op jit(solution)/shard_map/pallas_call | solution.py:109
  156.3 4.1 collective-permute-done.10
  169.4 8.2 %collective-permute-done.12 = bf16[2,128,1024]{2,1,0:T(8,128)(2,1)} collective-permute-done((bf16[2,128,1024]{2,1,0:T(8,128)(2,1)}, bf16[2,128,1024]{2,1,0:T(8,128)(2,1)}, u32[]{:S(2)}, u32[]{:S(2)}) %collective-permute-start.12) | collective-permute-done | bytes 524320 | tf_op jit(solution)/shard_map/ppermute | solution.py:20
  184.3 16.0 %collective-permute-done.9 = bf16[512,512]{1,0:T(8,128)(2,1)S(1)} collective-permute-done((bf16[512,512]{1,0:T(8,128)(2,1)S(1)}, bf16[512,512]{1,0:T(8,128)(2,1)S(1)}, u32[]{:S(2)}, u32[]{:S(2)}) %collective-permute-start.9) | collective-permute-done | bytes 524320 | tf_op jit(solution)/shard_map/ppermute | solution.py:20
  216.8 13.6 %collective-permute-done.16 = bf16[128,2048]{1,0:T(8,128)(2,1)S(1)} collective-permute-done((bf16[128,2048]{1,0:T(8,128)(2,1)S(1)}, bf16[128,2048]{1,0:T(8,128)(2,1)S(1)}, u32[]{:S(2)}, u32[]{:S(2)}) %collective-permute-start.16) | collective-permute-done | bytes 524320 | tf_op jit(solution)/shard_map/ppermute | solution.py:20
  230.4 11.1 %collective-permute-done.21 = bf16[1024,512]{1,0:T(8,128)(2,1)S(1)} collective-permute-done((bf16[1024,512]{1,0:T(8,128)(2,1)S(1)}, bf16[1024,512]{1,0:T(8,128)(2,1)S(1)}, u32[]{:S(2)}, u32[]{:S(2)}) %collective-permute-start.21) | collective-permute-done | bytes 1048608 | tf_op jit(solution)/shard_map/ppermute | solution.py:20
  245.4 5.3 collective-permute-done.24
  255.6 4.5 fusion.91
  261.3 8.2 %collective-permute-done.22 = bf16[512,512]{1,0:T(8,128)(2,1)S(1)} collective-permute-done((bf16[512,512]{1,0:T(8,128)(2,1)S(1)}, bf16[512,512]{1,0:T(8,128)(2,1)S(1)}, u32[]{:S(2)}, u32[]{:S(2)}) %collective-permute-start.22) | collective-permute-done | bytes 524320 | tf_op jit(solution)/shard_map/ppermute | solution.py:20
  281.9 4.5 fusion.92
  290.0 8.5 %collective-permute-done.31 = bf16[512,1024]{1,0:T(8,128)(2,1)S(1)} collective-permute-done((bf16[512,1024]{1,0:T(8,128)(2,1)S(1)}, bf16[512,1024]{1,0:T(8,128)(2,1)S(1)}, u32[]{:S(2)}, u32[]{:S(2)}) %collective-permute-start.31) | collective-permute-done | bytes 1048608 | tf_op jit(solution)/shard_map/ppermute | solution.py:20
  298.8 3.6 multiply_convert_fusion.3
  302.3 6.4 convolution_convert_fusion.5
  318.4 5.0 convolution_convert_fusion.4
  323.3 6.9 %collective-permute-done.34 = bf16[2,128,1024]{2,1,0:T(8,128)(2,1)S(1)} collective-permute-done((bf16[2,128,1024]{2,1,0:T(8,128)(2,1)S(1)}, bf16[2,128,1024]{2,1,0:T(8,128)(2,1)S(1)}, u32[]{:S(2)}, u32[]{:S(2)}) %collective-permute-start.34) | collective-permute-done | bytes 524320 | tf_op jit(solution)/shard_map/ppermute | solution.py:20
  338.4 6.9 fusion.4
  352.6 9.6 %collective-permute-done.39 = bf16[2,128,1024]{2,1,0:T(8,128)(2,1)S(1)} collective-permute-done((bf16[2,128,1024]{2,1,0:T(8,128)(2,1)S(1)}, bf16[2,128,1024]{2,1,0:T(8,128)(2,1)S(1)}, u32[]{:S(2)}, u32[]{:S(2)}) %collective-permute-start.39) | collective-permute-done | bytes 524320 | tf_op jit(solution)/shard_map/ppermute | solution.py:20
  367.4 8.5 %pad_maximum_fusion = bf16[2048,2048]{1,0:T(8,128)(2,1)} fusion(bf16[1024,2048]{1,0:T(8,128)(2,1)} %copy-done.43, bf16[1024,2048]{1,0:T(8,128)(2,1)} %copy-done.42), kind=kLoop, calls=%fused_computation.4 | loop fusion | flops 16777216 | bytes 16777216 | tf_op jit(solution)/shard_map/concatenate | solution.py:317
  384.2 7.7 %convolution_convert_fusion.8 = bf16[2048,512]{1,0:T(8,128)(2,1)} fusion(bf16[2048,2048]{1,0:T(8,128)(2,1)S(1)} %copy-done.45, bf16[1024,512]{1,0:T(8,128)(2,1)} %copy-done.116, bf16[1024,512]{1,0:T(8,128)(2,1)} %get-tuple-element.414), kind=kOutput, calls=%fused_computation.25 | convolution fusion | flops 4300210176 | bytes 12582912 | tf_op jit(solution)/shard_map/dot_general | solution.py:59
  392.0 4.4 convolution_convert_fusion
  396.4 4.3 convolution_convert_fusion.1
  400.7 6.3 collective-permute-done.43
  418.6 6.3 convolution_convert_fusion.7
  426.5 6.1 add_convert_fusion
  432.6 17.1 %collective-permute-done.46 = bf16[512,512]{1,0:T(8,128)(2,1)S(1)} collective-permute-done((bf16[512,512]{1,0:T(8,128)(2,1)S(1)}, bf16[512,512]{1,0:T(8,128)(2,1)S(1)}, u32[]{:S(2)}, u32[]{:S(2)}) %collective-permute-start.46) | collective-permute-done | bytes 524320 | tf_op jit(solution)/shard_map/ppermute | solution.py:20
  480.0 23.3 %shard_map.222 = (bf16[1024,256]{1,0:T(8,128)(2,1)S(1)}, bf16[1024,256]{1,0:T(8,128)(2,1)S(1)}, bf16[1024,256]{1,0:T(8,128)(2,1)S(1)}) custom-call(bf16[1024,256]{1,0:T(8,128)(2,1)S(1)} %copy-done.32, bf16[1024,256]{1,0:T(8,128)(2,1)S(1)} %copy-done.30, bf16[1024,256]{1,0:T(8,128)(2,1)S(1)} %copy.63.value_ref, ...), custom_call_target="tpu_custom_call" | custom-call | flops 8053063680 | bytes 7864320 | tf_op jit(solution)/shard_map/pallas_call | solution.py:157
  503.3 7.6 %collective-permute-done.59 = bf16[1024,512]{1,0:T(8,128)(2,1)} collective-permute-done((bf16[1024,512]{1,0:T(8,128)(2,1)}, bf16[1024,512]{1,0:T(8,128)(2,1)}, u32[]{:S(2)}, u32[]{:S(2)}) %collective-permute-start.59) | collective-permute-done | bytes 1048608 | tf_op jit(solution)/shard_map/ppermute | solution.py:20
  510.9 4.2 collective-permute-done.55
  517.2 4.9 convolution_convert_fusion.6
  522.1 5.7 convolution_convert_fusion.3
  535.7 7.6 %collective-permute-done.63 = bf16[128,2048]{1,0:T(8,128)(2,1)S(1)} collective-permute-done((bf16[128,2048]{1,0:T(8,128)(2,1)S(1)}, bf16[128,2048]{1,0:T(8,128)(2,1)S(1)}, u32[]{:S(2)}, u32[]{:S(2)}) %collective-permute-start.63) | collective-permute-done | bytes 524320 | tf_op jit(solution)/shard_map/ppermute | solution.py:20
  545.8 6.8 collective-permute-done.69
  552.6 25.2 %collective-permute-done.60 = bf16[512,512]{1,0:T(8,128)(2,1)S(1)} collective-permute-done((bf16[512,512]{1,0:T(8,128)(2,1)S(1)}, bf16[512,512]{1,0:T(8,128)(2,1)S(1)}, u32[]{:S(2)}, u32[]{:S(2)}) %collective-permute-start.60) | collective-permute-done | bytes 524320 | tf_op jit(solution)/shard_map/ppermute | solution.py:20
  578.7 11.6 %collective-permute-done.65 = bf16[1024,768]{1,0:T(8,128)(2,1)S(1)} collective-permute-done((bf16[1024,768]{1,0:T(8,128)(2,1)S(1)}, bf16[1024,768]{1,0:T(8,128)(2,1)S(1)}, u32[]{:S(2)}, u32[]{:S(2)}) %collective-permute-start.65) | collective-permute-done | bytes 1572896 | tf_op jit(solution)/shard_map/ppermute | solution.py:20
  595.6 7.7 %collective-permute-done.72 = bf16[2,128,1024]{2,1,0:T(8,128)(2,1)S(1)} collective-permute-done((bf16[2,128,1024]{2,1,0:T(8,128)(2,1)S(1)}, bf16[2,128,1024]{2,1,0:T(8,128)(2,1)S(1)}, u32[]{:S(2)}, u32[]{:S(2)}) %collective-permute-start.72) | collective-permute-done | bytes 524320 | tf_op jit(solution)/shard_map/ppermute | solution.py:20
  608.3 5.1 shard_map.224
  613.4 5.1 shard_map.223
  618.6 12.6 %collective-permute-done.70 = bf16[512,768]{1,0:T(8,128)(2,1)S(1)} collective-permute-done((bf16[512,768]{1,0:T(8,128)(2,1)S(1)}, bf16[512,768]{1,0:T(8,128)(2,1)S(1)}, u32[]{:S(2)}, u32[]{:S(2)}) %collective-permute-start.70) | collective-permute-done | bytes 786464 | tf_op jit(solution)/shard_map/ppermute | solution.py:20
  640.3 7.7 %collective-permute-done.79 = f32[32,128]{1,0:T(8,128)S(1)} collective-permute-done((f32[32,128]{1,0:T(8,128)S(1)}, f32[32,128]{1,0:T(8,128)S(1)}, u32[]{:S(2)}, u32[]{:S(2)}) %collective-permute-start.79) | collective-permute-done | bytes 16416 | tf_op jit(solution)/shard_map/ppermute | solution.py:20
  648.1 6.9 %collective-permute-done.80 = bf16[512,768]{1,0:T(8,128)(2,1)} collective-permute-done((bf16[512,768]{1,0:T(8,128)(2,1)}, bf16[512,768]{1,0:T(8,128)(2,1)}, u32[]{:S(2)}, u32[]{:S(2)}) %collective-permute-start.80) | collective-permute-done | bytes 786464 | tf_op jit(solution)/shard_map/ppermute | solution.py:20
  658.1 5.1 shard_map.225
  674.1 5.0 shard_map.227
  (619 shorter events, 241.6 us)
Async XLA Ops:
  7.2 109.5 %all-gather.2.cloned.1.call-start = ((), (), s32[]{:S(2)}) async-start(), calls=%async_computation.1 | async-start | bytes 5242880 | tf_op jit(solution)/shard_map/all_gather | solution.py:379
  11.1 511.0 %reduce-scatter.2.cloned.1.call-start = ((), (), s32[]{:S(2)}) async-start(), calls=%async_computation.2 | async-start | bytes 1310720 | tf_op jit(solution)/shard_map/reduce_scatter | solution.py:533
  28.1 26.2 %collective-permute-start = (bf16[256,2048]{1,0:T(8,128)(2,1)S(1)}, bf16[256,2048]{1,0:T(8,128)(2,1)}, u32[]{:S(2)}, u32[]{:S(2)}) collective-permute-start(bf16[256,2048]{1,0:T(8,128)(2,1)S(1)} %get-tuple-element.622), channel_id=1, source_target_pairs={{0,4},{2,6},{4,0},{6,2},{1,5},{3,7},{5,1},{7,3},{8,12},{10,14},{12... | collective-permute-start | bytes 3145736 | tf_op jit(solution)/shard_map/ppermute | solution.py:20
  30.8 59.0 %collective-permute-start.3 = (bf16[256,2048]{1,0:T(8,128)(2,1)}, bf16[256,2048]{1,0:T(8,128)(2,1)}, u32[]{:S(2)}, u32[]{:S(2)}) collective-permute-start(bf16[256,2048]{1,0:T(8,128)(2,1)} %pad_maximum_fusion.14), channel_id=1, source_target_pairs={{0,4},{2,6},{4,0},{6,2},{1,5},{3,7},{5,1},{7,3},{8,12},{10,14},{12... | collective-permute-start | bytes 3145736 | tf_op jit(solution)/shard_map/ppermute | solution.py:20
  33.3 56.5 %collective-permute-start.2 = (bf16[128,2048]{1,0:T(8,128)(2,1)}, bf16[128,2048]{1,0:T(8,128)(2,1)}, u32[]{:S(2)}, u32[]{:S(2)}) collective-permute-start(bf16[128,2048]{1,0:T(8,128)(2,1)} %slice.184), channel_id=1, source_target_pairs={{0,16},{8,24},{16,0},{24,8},{1,17},{9,25},{17,1},{25,9},{2,18},{10... | collective-permute-start | bytes 1572872 | tf_op jit(solution)/shard_map/ppermute | solution.py:20
  129.4 24.1 %collective-permute-start.4 = (bf16[512,512]{1,0:T(8,128)(2,1)}, bf16[512,512]{1,0:T(8,128)(2,1)}, u32[]{:S(2)}, u32[]{:S(2)}) collective-permute-start(bf16[512,512]{1,0:T(8,128)(2,1)} %get-tuple-element.286), channel_id=1, source_target_pairs={{0,16},{8,24},{16,0},{24,8},{1,17},{9,25},{17,1},{25,9},{2,18},{10... | collective-permute-start | bytes 1572872 | tf_op jit(solution)/shard_map/ppermute | solution.py:20
  131.4 22.1 %collective-permute-start.8 = (bf16[2,128,1024]{2,1,0:T(8,128)(2,1)}, bf16[2,128,1024]{2,1,0:T(8,128)(2,1)}, u32[]{:S(2)}, u32[]{:S(2)}) collective-permute-start(bf16[2,128,1024]{2,1,0:T(8,128)(2,1)} %bitcast.11), channel_id=1, source_target_pairs={{0,1},{1,0},{2,3},{3,2},{4,5},{5,4},{6,7},{7,6},{8,9},{9,8},{10,11... | collective-permute-start | bytes 1572872 | tf_op jit(solution)/shard_map/ppermute | solution.py:20
  133.7 19.8 %collective-permute-start.6 = (bf16[256,1024]{1,0:T(8,128)(2,1)}, bf16[256,1024]{1,0:T(8,128)(2,1)}, u32[]{:S(2)}, u32[]{:S(2)}) collective-permute-start(bf16[256,1024]{1,0:T(8,128)(2,1)} %pad_maximum_fusion.22), channel_id=1, source_target_pairs={{0,4},{2,6},{4,0},{6,2},{1,5},{3,7},{5,1},{7,3},{8,12},{10,14},{12... | collective-permute-start | bytes 1572872 | tf_op jit(solution)/shard_map/ppermute | solution.py:20
  166.2 36.3 %collective-permute-start.15 = (bf16[1024,512]{1,0:T(8,128)(2,1)S(1)}, bf16[1024,512]{1,0:T(8,128)(2,1)S(1)}, u32[]{:S(2)}, u32[]{:S(2)}) collective-permute-start(bf16[1024,512]{1,0:T(8,128)(2,1)S(1)} %maximum_select_fusion), channel_id=1, source_target_pairs={{0,8},{8,0},{16,24},{24,16},{1,9},{9,1},{17,25},{25,17},{2,10},{10... | collective-permute-start | bytes 3145736 | tf_op jit(solution)/shard_map/ppermute | solution.py:20
  166.4 33.9 %collective-permute-start.9 = (bf16[512,512]{1,0:T(8,128)(2,1)S(1)}, bf16[512,512]{1,0:T(8,128)(2,1)S(1)}, u32[]{:S(2)}, u32[]{:S(2)}) collective-permute-start(bf16[512,512]{1,0:T(8,128)(2,1)S(1)} %copy-done.88), channel_id=1, source_target_pairs={{0,16},{8,24},{16,0},{24,8},{1,17},{9,25},{17,1},{25,9},{2,18},{10... | collective-permute-start | bytes 1572872 | tf_op jit(solution)/shard_map/ppermute | solution.py:20
  179.2 23.3 %collective-permute-start.14 = (bf16[128,1024]{1,0:T(8,128)(2,1)S(1)}, bf16[128,1024]{1,0:T(8,128)(2,1)S(1)}, u32[]{:S(2)}, u32[]{:S(2)}) collective-permute-start(bf16[128,1024]{1,0:T(8,128)(2,1)S(1)} %get-tuple-element.681), channel_id=1, source_target_pairs={{0,4},{2,6},{4,0},{6,2},{1,5},{3,7},{5,1},{7,3},{8,12},{10,14},{12... | collective-permute-start | bytes 786440 | tf_op jit(solution)/shard_map/ppermute | solution.py:20
  180.9 21.6 %collective-permute-start.13 = (bf16[128,1024]{1,0:T(8,128)(2,1)S(1)}, bf16[128,1024]{1,0:T(8,128)(2,1)S(1)}, u32[]{:S(2)}, u32[]{:S(2)}) collective-permute-start(bf16[128,1024]{1,0:T(8,128)(2,1)S(1)} %get-tuple-element.683), channel_id=1, source_target_pairs={{0,1},{1,0},{2,3},{3,2},{4,5},{5,4},{6,7},{7,6},{8,9},{9,8},{10,11... | collective-permute-start | bytes 786440 | tf_op jit(solution)/shard_map/ppermute | solution.py:20
  206.1 24.3 %collective-permute-start.16 = (bf16[128,2048]{1,0:T(8,128)(2,1)S(1)}, bf16[128,2048]{1,0:T(8,128)(2,1)S(1)}, u32[]{:S(2)}, u32[]{:S(2)}) collective-permute-start(bf16[128,2048]{1,0:T(8,128)(2,1)S(1)} %pad_maximum_fusion.24), channel_id=1, source_target_pairs={{0,16},{8,24},{16,0},{24,8},{1,17},{9,25},{17,1},{25,9},{2,18},{10... | collective-permute-start | bytes 1572872 | tf_op jit(solution)/shard_map/ppermute | solution.py:20
  207.7 33.8 %collective-permute-start.21 = (bf16[1024,512]{1,0:T(8,128)(2,1)S(1)}, bf16[1024,512]{1,0:T(8,128)(2,1)S(1)}, u32[]{:S(2)}, u32[]{:S(2)}) collective-permute-start(bf16[1024,512]{1,0:T(8,128)(2,1)S(1)} %maximum_select_fusion.1), channel_id=1, source_target_pairs={{0,8},{8,0},{16,24},{24,16},{1,9},{9,1},{17,25},{25,17},{2,10},{10... | collective-permute-start | bytes 3145736 | tf_op jit(solution)/shard_map/ppermute | solution.py:20
  211.3 19.0 %collective-permute-start.20 = (bf16[2,128,1024]{2,1,0:T(8,128)(2,1)S(1)}, bf16[2,128,1024]{2,1,0:T(8,128)(2,1)S(1)}, u32[]{:S(2)}, u32[]{:S(2)}) collective-permute-start(bf16[2,128,1024]{2,1,0:T(8,128)(2,1)S(1)} %bitcast.152), channel_id=1, source_target_pairs={{0,1},{1,0},{2,3},{3,2},{4,5},{5,4},{6,7},{7,6},{8,9},{9,8},{10,11... | collective-permute-start | bytes 1572872 | tf_op jit(solution)/shard_map/ppermute | solution.py:20
  212.9 17.4 %collective-permute-start.19 = (bf16[256,1024]{1,0:T(8,128)(2,1)S(1)}, bf16[256,1024]{1,0:T(8,128)(2,1)S(1)}, u32[]{:S(2)}, u32[]{:S(2)}) collective-permute-start(bf16[256,1024]{1,0:T(8,128)(2,1)S(1)} %constant_dynamic-update-slice_fusion.1), channel_id=1, source_target_pairs={{0,4},{2,6},{4,0},{6,2},{1,5},{3,7},{5,1},{7,3},{8,12},{10,14},{12... | collective-permute-start | bytes 1572872 | tf_op jit(solution)/shard_map/ppermute | solution.py:20
  243.6 25.9 %collective-permute-start.22 = (bf16[512,512]{1,0:T(8,128)(2,1)S(1)}, bf16[512,512]{1,0:T(8,128)(2,1)S(1)}, u32[]{:S(2)}, u32[]{:S(2)}) collective-permute-start(bf16[512,512]{1,0:T(8,128)(2,1)S(1)} %copy-done.87), channel_id=1, source_target_pairs={{0,16},{8,24},{16,0},{24,8},{1,17},{9,25},{17,1},{25,9},{2,18},{10... | collective-permute-start | bytes 1572872 | tf_op jit(solution)/shard_map/ppermute | solution.py:20
  244.9 28.6 %collective-permute-start.29 = (bf16[512,2048]{1,0:T(8,128)(2,1)S(1)}, bf16[512,2048]{1,0:T(8,128)(2,1)S(1)}, u32[]{:S(2)}, u32[]{:S(2)}) collective-permute-start(bf16[512,2048]{1,0:T(8,128)(2,1)S(1)} %pad_maximum_fusion.6), channel_id=1, source_target_pairs={{0,2},{2,0},{4,6},{6,4},{1,3},{3,1},{5,7},{7,5},{8,10},{10,8},{12,... | collective-permute-start | bytes 6291464 | tf_op jit(solution)/shard_map/ppermute | solution.py:20
  251.0 18.5 %collective-permute-start.27 = (bf16[2,128,1024]{2,1,0:T(8,128)(2,1)S(1)}, bf16[2,128,1024]{2,1,0:T(8,128)(2,1)S(1)}, u32[]{:S(2)}, u32[]{:S(2)}) collective-permute-start(bf16[2,128,1024]{2,1,0:T(8,128)(2,1)S(1)} %bitcast.150), channel_id=1, source_target_pairs={{0,1},{1,0},{2,3},{3,2},{4,5},{5,4},{6,7},{7,6},{8,9},{9,8},{10,11... | collective-permute-start | bytes 1572872 | tf_op jit(solution)/shard_map/ppermute | solution.py:20
  252.6 16.9 %collective-permute-start.26 = (bf16[256,1024]{1,0:T(8,128)(2,1)S(1)}, bf16[256,1024]{1,0:T(8,128)(2,1)S(1)}, u32[]{:S(2)}, u32[]{:S(2)}) collective-permute-start(bf16[256,1024]{1,0:T(8,128)(2,1)S(1)} %constant_dynamic-update-slice_fusion.7), channel_id=1, source_target_pairs={{0,4},{2,6},{4,0},{6,2},{1,5},{3,7},{5,1},{7,3},{8,12},{10,14},{12... | collective-permute-start | bytes 1572872 | tf_op jit(solution)/shard_map/ppermute | solution.py:20
  273.4 25.1 %collective-permute-start.31 = (bf16[512,1024]{1,0:T(8,128)(2,1)S(1)}, bf16[512,1024]{1,0:T(8,128)(2,1)S(1)}, u32[]{:S(2)}, u32[]{:S(2)}) collective-permute-start(bf16[512,1024]{1,0:T(8,128)(2,1)S(1)} %maximum_select_fusion.2), channel_id=1, source_target_pairs={{0,8},{8,0},{16,24},{24,16},{1,9},{9,1},{17,25},{25,17},{2,10},{10... | collective-permute-start | bytes 3145736 | tf_op jit(solution)/shard_map/ppermute | solution.py:20
  316.0 14.3 %collective-permute-start.34 = (bf16[2,128,1024]{2,1,0:T(8,128)(2,1)S(1)}, bf16[2,128,1024]{2,1,0:T(8,128)(2,1)S(1)}, u32[]{:S(2)}, u32[]{:S(2)}) collective-permute-start(bf16[2,128,1024]{2,1,0:T(8,128)(2,1)S(1)} %get-tuple-element.649), channel_id=1, source_target_pairs={{0,1},{1,0},{2,3},{3,2},{4,5},{5,4},{6,7},{7,6},{8,9},{9,8},{10,11... | collective-permute-start | bytes 1572872 | tf_op jit(solution)/shard_map/ppermute | solution.py:20
  352.1 24.6 %collective-permute-start.42 = (bf16[512,1024]{1,0:T(8,128)(2,1)}, bf16[512,1024]{1,0:T(8,128)(2,1)}, u32[]{:S(2)}, u32[]{:S(2)}) collective-permute-start(bf16[512,1024]{1,0:T(8,128)(2,1)} %get-tuple-element.603), channel_id=1, source_target_pairs={{0,8},{8,0},{16,24},{24,16},{1,9},{9,1},{17,25},{25,17},{2,10},{10... | collective-permute-start | bytes 3145736 | tf_op jit(solution)/shard_map/ppermute | solution.py:20
  379.9 20.8 %collective-permute-start.44 = (bf16[512,512]{1,0:T(8,128)(2,1)S(1)}, bf16[512,512]{1,0:T(8,128)(2,1)S(1)}, u32[]{:S(2)}, u32[]{:S(2)}) collective-permute-start(bf16[512,512]{1,0:T(8,128)(2,1)S(1)} %get-tuple-element.500), channel_id=1, source_target_pairs={{0,4},{2,6},{4,0},{6,2},{1,5},{3,7},{5,1},{7,3},{8,12},{10,14},{12... | collective-permute-start | bytes 1572872 | tf_op jit(solution)/shard_map/ppermute | solution.py:20
  382.8 24.2 %collective-permute-start.43 = (bf16[128,2048]{1,0:T(8,128)(2,1)S(1)}, bf16[128,2048]{1,0:T(8,128)(2,1)S(1)}, u32[]{:S(2)}, u32[]{:S(2)}) collective-permute-start(bf16[128,2048]{1,0:T(8,128)(2,1)S(1)} %pad_maximum_fusion.28), channel_id=1, source_target_pairs={{0,16},{8,24},{16,0},{24,8},{1,17},{9,25},{17,1},{25,9},{2,18},{10... | collective-permute-start | bytes 1572872 | tf_op jit(solution)/shard_map/ppermute | solution.py:20
  407.8 18.6 %collective-permute-start.45 = (bf16[1024,2048]{1,0:T(8,128)(2,1)}, bf16[1024,2048]{1,0:T(8,128)(2,1)}, u32[]{:S(2)}, u32[]{:S(2)}) collective-permute-start(bf16[1024,2048]{1,0:T(8,128)(2,1)} %convolution_convert_fusion), channel_id=1, source_target_pairs={{0,2},{2,0},{4,6},{6,4},{1,3},{3,1},{5,7},{7,5},{8,10},{10,8},{12,... | collective-permute-start | bytes 12582920 | tf_op jit(solution)/shard_map/ppermute | solution.py:20
  415.6 36.2 %collective-permute-start.51 = (bf16[1024,512]{1,0:T(8,128)(2,1)S(1)}, bf16[1024,512]{1,0:T(8,128)(2,1)S(1)}, u32[]{:S(2)}, u32[]{:S(2)}) collective-permute-start(bf16[1024,512]{1,0:T(8,128)(2,1)S(1)} %get-tuple-element.601), channel_id=1, source_target_pairs={{0,8},{8,0},{16,24},{24,16},{1,9},{9,1},{17,25},{25,17},{2,10},{10... | collective-permute-start | bytes 3145736 | tf_op jit(solution)/shard_map/ppermute | solution.py:20
  415.6 34.0 %collective-permute-start.46 = (bf16[512,512]{1,0:T(8,128)(2,1)S(1)}, bf16[512,512]{1,0:T(8,128)(2,1)S(1)}, u32[]{:S(2)}, u32[]{:S(2)}) collective-permute-start(bf16[512,512]{1,0:T(8,128)(2,1)S(1)} %copy-done.100), channel_id=1, source_target_pairs={{0,16},{8,24},{16,0},{24,8},{1,17},{9,25},{17,1},{25,9},{2,18},{10... | collective-permute-start | bytes 1572872 | tf_op jit(solution)/shard_map/ppermute | solution.py:20
  425.0 24.7 %collective-permute-start.50 = (bf16[2,128,1024]{2,1,0:T(8,128)(2,1)S(1)}, bf16[2,128,1024]{2,1,0:T(8,128)(2,1)S(1)}, u32[]{:S(2)}, u32[]{:S(2)}) collective-permute-start(bf16[2,128,1024]{2,1,0:T(8,128)(2,1)S(1)} %bitcast.154), channel_id=1, source_target_pairs={{0,1},{1,0},{2,3},{3,2},{4,5},{5,4},{6,7},{7,6},{8,9},{9,8},{10,11... | collective-permute-start | bytes 1572872 | tf_op jit(solution)/shard_map/ppermute | solution.py:20
  425.9 23.7 %collective-permute-start.48 = (bf16[256,1024]{1,0:T(8,128)(2,1)S(1)}, bf16[256,1024]{1,0:T(8,128)(2,1)S(1)}, u32[]{:S(2)}, u32[]{:S(2)}) collective-permute-start(bf16[256,1024]{1,0:T(8,128)(2,1)S(1)} %pad_maximum_fusion.29), channel_id=1, source_target_pairs={{0,4},{2,6},{4,0},{6,2},{1,5},{3,7},{5,1},{7,3},{8,12},{10,14},{12... | collective-permute-start | bytes 1572872 | tf_op jit(solution)/shard_map/ppermute | solution.py:20
  458.9 52.0 %collective-permute-start.59 = (bf16[1024,512]{1,0:T(8,128)(2,1)}, bf16[1024,512]{1,0:T(8,128)(2,1)}, u32[]{:S(2)}, u32[]{:S(2)}) collective-permute-start(bf16[1024,512]{1,0:T(8,128)(2,1)} %get-tuple-element.597), channel_id=1, source_target_pairs={{0,8},{8,0},{16,24},{24,16},{1,9},{9,1},{17,25},{25,17},{2,10},{10... | collective-permute-start | bytes 3145736 | tf_op jit(solution)/shard_map/ppermute | solution.py:20
  472.5 42.6 %collective-permute-start.55 = (bf16[512,512]{1,0:T(8,128)(2,1)S(1)}, bf16[512,512]{1,0:T(8,128)(2,1)S(1)}, u32[]{:S(2)}, u32[]{:S(2)}) collective-permute-start(bf16[512,512]{1,0:T(8,128)(2,1)S(1)} %get-tuple-element.636), channel_id=1, source_target_pairs={{0,16},{8,24},{16,0},{24,8},{1,17},{9,25},{17,1},{25,9},{2,18},{10... | collective-permute-start | bytes 1572872 | tf_op jit(solution)/shard_map/ppermute | solution.py:20
  474.0 41.1 %collective-permute-start.58 = (bf16[512,512]{1,0:T(8,128)(2,1)S(1)}, bf16[512,512]{1,0:T(8,128)(2,1)S(1)}, u32[]{:S(2)}, u32[]{:S(2)}) collective-permute-start(bf16[512,512]{1,0:T(8,128)(2,1)S(1)} %get-tuple-element.486), channel_id=1, source_target_pairs={{0,4},{2,6},{4,0},{6,2},{1,5},{3,7},{5,1},{7,3},{8,12},{10,14},{12... | collective-permute-start | bytes 1572872 | tf_op jit(solution)/shard_map/ppermute | solution.py:20
  474.8 41.1 %collective-permute-start.57 = (bf16[2,128,2048]{2,1,0:T(8,128)(2,1)S(1)}, bf16[2,128,2048]{2,1,0:T(8,128)(2,1)S(1)}, u32[]{:S(2)}, u32[]{:S(2)}) collective-permute-start(bf16[2,128,2048]{2,1,0:T(8,128)(2,1)S(1)} %get-tuple-element.599), channel_id=1, source_target_pairs={{0,1},{1,0},{2,3},{3,2},{4,5},{5,4},{6,7},{7,6},{8,9},{9,8},{10,11... | collective-permute-start | bytes 3145736 | tf_op jit(solution)/shard_map/ppermute | solution.py:20
  475.9 40.1 %collective-permute-start.56 = (bf16[256,2048]{1,0:T(8,128)(2,1)S(1)}, bf16[256,2048]{1,0:T(8,128)(2,1)S(1)}, u32[]{:S(2)}, u32[]{:S(2)}) collective-permute-start(bf16[256,2048]{1,0:T(8,128)(2,1)S(1)} %copy-done.86), channel_id=1, source_target_pairs={{0,4},{2,6},{4,0},{6,2},{1,5},{3,7},{5,1},{7,3},{8,12},{10,14},{12... | collective-permute-start | bytes 3145736 | tf_op jit(solution)/shard_map/ppermute | solution.py:20
  528.3 15.8 %collective-permute-start.61 = (bf16[512,2048]{1,0:T(8,128)(2,1)S(1)}, bf16[512,2048]{1,0:T(8,128)(2,1)S(1)}, u32[]{:S(2)}, u32[]{:S(2)}) collective-permute-start(bf16[512,2048]{1,0:T(8,128)(2,1)S(1)} %get-tuple-element.567), channel_id=1, source_target_pairs={{0,2},{2,0},{4,6},{6,4},{1,3},{3,1},{5,7},{7,5},{8,10},{10,8},{12,... | collective-permute-start | bytes 6291464 | tf_op jit(solution)/shard_map/ppermute | solution.py:20
  531.7 58.6 %collective-permute-start.65 = (bf16[1024,768]{1,0:T(8,128)(2,1)S(1)}, bf16[1024,768]{1,0:T(8,128)(2,1)S(1)}, u32[]{:S(2)}, u32[]{:S(2)}) collective-permute-start(bf16[1024,768]{1,0:T(8,128)(2,1)S(1)} %get-tuple-element.591), channel_id=1, source_target_pairs={{0,8},{8,0},{16,24},{24,16},{1,9},{9,1},{17,25},{25,17},{2,10},{10... | collective-permute-start | bytes 4718600 | tf_op jit(solution)/shard_map/ppermute | solution.py:20
  533.7 44.1 %collective-permute-start.60 = (bf16[512,512]{1,0:T(8,128)(2,1)S(1)}, bf16[512,512]{1,0:T(8,128)(2,1)S(1)}, u32[]{:S(2)}, u32[]{:S(2)}) collective-permute-start(bf16[512,512]{1,0:T(8,128)(2,1)S(1)} %get-tuple-element.634), channel_id=1, source_target_pairs={{0,16},{8,24},{16,0},{24,8},{1,17},{9,25},{17,1},{25,9},{2,18},{10... | collective-permute-start | bytes 1572872 | tf_op jit(solution)/shard_map/ppermute | solution.py:20
  544.1 46.2 %collective-permute-start.66 = (bf16[3,512,512]{2,1,0:T(8,128)(2,1)S(1)}, bf16[3,512,512]{2,1,0:T(8,128)(2,1)S(1)}, u32[]{:S(2)}, u32[]{:S(2)}) collective-permute-start(bf16[3,512,512]{2,1,0:T(8,128)(2,1)S(1)} %pad_maximum_fusion.12.refs_4_.refs_0_), channel_id=1, source_target_pairs={{0,4},{2,6},{4,0},{6,2},{1,5},{3,7},{5,1},{7,3},{8,12},{10,14},{12... | collective-permute-start | bytes 4718600 | tf_op jit(solution)/shard_map/ppermute | solution.py:20
  545.7 44.6 %collective-permute-start.64 = (bf16[128,2048]{1,0:T(8,128)(2,1)S(1)}, bf16[128,2048]{1,0:T(8,128)(2,1)S(1)}, u32[]{:S(2)}, u32[]{:S(2)}) collective-permute-start(bf16[128,2048]{1,0:T(8,128)(2,1)S(1)} %add_convert_fusion.15), channel_id=1, source_target_pairs={{0,16},{8,24},{16,0},{24,8},{1,17},{9,25},{17,1},{25,9},{2,18},{10... | collective-permute-start | bytes 1572872 | tf_op jit(solution)/shard_map/ppermute | solution.py:20
  552.6 37.7 %collective-permute-start.67 = (bf16[512,512]{1,0:T(8,128)(2,1)S(1)}, bf16[512,512]{1,0:T(8,128)(2,1)S(1)}, u32[]{:S(2)}, u32[]{:S(2)}) collective-permute-start(bf16[512,512]{1,0:T(8,128)(2,1)S(1)} %copy-done.10), channel_id=1, source_target_pairs={{0,2},{2,0},{4,6},{6,4},{1,3},{3,1},{5,7},{7,5},{8,10},{10,8},{12,... | collective-permute-start | bytes 1572872 | tf_op jit(solution)/shard_map/ppermute | solution.py:20
  594.3 37.0 %collective-permute-start.70 = (bf16[512,768]{1,0:T(8,128)(2,1)S(1)}, bf16[512,768]{1,0:T(8,128)(2,1)S(1)}, u32[]{:S(2)}, u32[]{:S(2)}) collective-permute-start(bf16[512,768]{1,0:T(8,128)(2,1)S(1)} %get-tuple-element.616), channel_id=1, source_target_pairs={{0,16},{8,24},{16,0},{24,8},{1,17},{9,25},{17,1},{25,9},{2,18},{10... | collective-permute-start | bytes 2359304 | tf_op jit(solution)/shard_map/ppermute | solution.py:20
  603.7 27.5 %collective-permute-start.76 = (bf16[128,1024]{1,0:T(8,128)(2,1)S(1)}, bf16[128,1024]{1,0:T(8,128)(2,1)S(1)}, u32[]{:S(2)}, u32[]{:S(2)}) collective-permute-start(bf16[128,1024]{1,0:T(8,128)(2,1)S(1)} %get-tuple-element.661), channel_id=1, source_target_pairs={{0,4},{2,6},{4,0},{6,2},{1,5},{3,7},{5,1},{7,3},{8,12},{10,14},{12... | collective-permute-start | bytes 786440 | tf_op jit(solution)/shard_map/ppermute | solution.py:20
  605.2 26.0 %collective-permute-start.77 = (bf16[512,512]{1,0:T(8,128)(2,1)S(1)}, bf16[512,512]{1,0:T(8,128)(2,1)S(1)}, u32[]{:S(2)}, u32[]{:S(2)}) collective-permute-start(bf16[512,512]{1,0:T(8,128)(2,1)S(1)} %collective-permute-done.60), channel_id=1, source_target_pairs={{0,4},{2,6},{4,0},{6,2},{1,5},{3,7},{5,1},{7,3},{8,12},{10,14},{12... | collective-permute-start | bytes 1572872 | tf_op jit(solution)/shard_map/ppermute | solution.py:20
  605.8 26.2 %collective-permute-start.78 = (bf16[128,2048]{1,0:T(8,128)(2,1)S(1)}, bf16[128,2048]{1,0:T(8,128)(2,1)S(1)}, u32[]{:S(2)}, u32[]{:S(2)}) collective-permute-start(bf16[128,2048]{1,0:T(8,128)(2,1)S(1)} %fusion.40), channel_id=1, source_target_pairs={{0,1},{1,0},{2,3},{3,2},{4,5},{5,4},{6,7},{7,6},{8,9},{9,8},{10,11... | collective-permute-start | bytes 1572872 | tf_op jit(solution)/shard_map/ppermute | solution.py:20
  607.8 23.5 %collective-permute-start.75 = (bf16[128,1024]{1,0:T(8,128)(2,1)S(1)}, bf16[128,1024]{1,0:T(8,128)(2,1)S(1)}, u32[]{:S(2)}, u32[]{:S(2)}) collective-permute-start(bf16[128,1024]{1,0:T(8,128)(2,1)S(1)} %get-tuple-element.663), channel_id=1, source_target_pairs={{0,1},{1,0},{2,3},{3,2},{4,5},{5,4},{6,7},{7,6},{8,9},{9,8},{10,11... | collective-permute-start | bytes 786440 | tf_op jit(solution)/shard_map/ppermute | solution.py:20
  633.6 14.4 %collective-permute-start.81 = (bf16[128,2048]{1,0:T(8,128)(2,1)}, bf16[128,2048]{1,0:T(8,128)(2,1)}, u32[]{:S(2)}, u32[]{:S(2)}) collective-permute-start(bf16[128,2048]{1,0:T(8,128)(2,1)} %fusion.32), channel_id=1, source_target_pairs={{0,1},{1,0},{2,3},{3,2},{4,5},{5,4},{6,7},{7,6},{8,9},{9,8},{10,11... | collective-permute-start | bytes 1572872 | tf_op jit(solution)/shard_map/ppermute | solution.py:20
  635.5 19.5 %collective-permute-start.80 = (bf16[512,768]{1,0:T(8,128)(2,1)}, bf16[512,768]{1,0:T(8,128)(2,1)}, u32[]{:S(2)}, u32[]{:S(2)}) collective-permute-start(bf16[512,768]{1,0:T(8,128)(2,1)} %add_convert_fusion.12), channel_id=1, source_target_pairs={{0,4},{2,6},{4,0},{6,2},{1,5},{3,7},{5,1},{7,3},{8,12},{10,14},{12... | collective-permute-start | bytes 2359304 | tf_op jit(solution)/shard_map/ppermute | solution.py:20
  (167 other events, 1648.8 us)
Sparse Core Ops, SparseCore 0:
  11.2 105.4 all-gather.1
  470.9 40.6 reduce-scatter.1

commit v4 on v3

--- a/solution.py
+++ b/solution.py
@@ -83,10 +83,8 @@
     return (places[None, :] <= places[:, None]) | shared
 
 
-def attention_probs(query, key, bias):
-    scores = mm_nt(query, key) * (1.0 / math.sqrt(HD)) + bias
-    powers = jnp.exp(scores - jnp.max(scores, axis=-1, keepdims=True))
-    return powers * (1.0 / jnp.sum(powers, axis=-1, keepdims=True))
+def attention_scores(query, key, bias):
+    return mm_nt(query * jnp.asarray(1.0 / math.sqrt(HD), BF), key) + bias
 
 
 def pair_specs(rows, count):
@@ -97,21 +95,25 @@
     rows, columns = query.shape
     block = min(256, rows)
 
-    def kernel(query_ref, key_ref, value_ref, bias_ref, out_ref):
+    def kernel(query_ref, key_ref, value_ref, bias_ref, out_ref, totals_ref):
         for head in range(2):
             lanes = slice(head * HD, (head + 1) * HD)
             k, v = key_ref[:, lanes], value_ref[:, lanes]
             for start in range(0, rows, block):
                 now = slice(start, start + block)
-                probs = attention_probs(query_ref[now, lanes], k, bias_ref[now, :])
-                out_ref[now, lanes] = mm(probs.astype(BF), v).astype(BF)
+                scores = attention_scores(query_ref[now, lanes], k, bias_ref[now, :])
+                top = jnp.max(scores, axis=-1, keepdims=True)
+                powers = jnp.exp(scores - top)
+                total = jnp.sum(powers, axis=-1, keepdims=True)
+                out_ref[now, lanes] = (mm(powers.astype(BF), v) * (1.0 / total)).astype(BF)
+                totals_ref[now, lanes] = jnp.broadcast_to(top + jnp.log(total), (block, HD))
 
     return pl.pallas_call(
         kernel,
         grid=(columns // (2 * HD),),
         in_specs=pair_specs(rows, 3) + [pl.BlockSpec((rows, rows), lambda i: (0, 0))],
-        out_specs=pair_specs(rows, 1)[0],
-        out_shape=jax.ShapeDtypeStruct((rows, columns), BF),
+        out_specs=pair_specs(rows, 2),
+        out_shape=[jax.ShapeDtypeStruct((rows, columns), BF), jax.ShapeDtypeStruct((rows, columns), F32)],
         compiler_params=pltpu.CompilerParams(vmem_limit_bytes=40 * 1024 * 1024),
         cost_estimate=pl.CostEstimate(
             flops=16 * rows * rows * columns,
@@ -121,12 +123,12 @@
     )(query, key, value, bias)
 
 
-def attend_backward(query, key, value, grad, bias, cosine, sine):
+def attend_backward(query, key, value, totals, grad, bias, cosine, sine):
     rows, columns = query.shape
     block = min(256, rows)
     scale = 1.0 / math.sqrt(HD)
 
-    def kernel(query_ref, key_ref, value_ref, grad_ref, bias_ref, cos_ref, sin_ref, dq_ref, dk_ref, dv_ref, q_acc, k_acc):
+    def kernel(query_ref, key_ref, value_ref, totals_ref, grad_ref, bias_ref, cos_ref, sin_ref, dq_ref, dk_ref, dv_ref, q_acc, k_acc):
         lane = lax.broadcasted_iota(jnp.int32, (rows, 2 * HD), 1)
         front = lane % HD < HD // 2
 
@@ -142,7 +144,8 @@
             for start in range(0, rows, block):
                 now = slice(start, start + block)
                 q, g = query_ref[now, lanes], grad_ref[now, lanes]
-                probs = attention_probs(q, k, bias_ref[now, :])
+                total = totals_ref[now, head * HD : head * HD + 1]
+                probs = jnp.exp(attention_scores(q, k, bias_ref[now, :]) - total)
                 v_sum += mm_t(g, probs.astype(BF))
                 grad_probs = mm_nt(g, v)
                 centre = jnp.sum(probs * grad_probs, axis=-1, keepdims=True)
@@ -157,7 +160,7 @@
     return pl.pallas_call(
         kernel,
         grid=(columns // (2 * HD),),
-        in_specs=pair_specs(rows, 4)
+        in_specs=pair_specs(rows, 5)
         + [pl.BlockSpec((rows, rows), lambda i: (0, 0))]
         + [pl.BlockSpec((rows, 2 * HD), lambda i: (0, 0))] * 2,
         out_specs=pair_specs(rows, 3),
@@ -169,7 +172,7 @@
             transcendentals=rows * rows * columns // HD,
             bytes_accessed=14 * rows * columns + 4 * rows * rows,
         ),
-    )(query, key, value, grad, bias, cosine, sine)
+    )(query, key, value, totals, grad, bias, cosine, sine)
 
 
 def norm_forward(values):
@@ -322,6 +325,15 @@
     block = width // n_shard
     low_order = order_of(top)
     low_bits = bits_of(top)
+    planes = [[side * top + o for o in range(top)] for side in range(2)]
+
+    def low_sum(values, dim):
+        where = jnp.asarray([low_order.index(o) for o in range(top)], jnp.int32)
+        size = values.shape[dim] // top
+        parts = [lax.dynamic_slice_in_dim(values, where[low ^ o] * size, size, axis=dim) for o in range(top)]
+        return lax.psum_scatter(
+            jnp.concatenate(parts, axis=dim), "shard", scatter_dimension=dim, tiled=True, axis_index_groups=planes
+        )
 
     def folded(values):
         starts = [(side * top + (low ^ o)) * block for o in low_order for side in range(2)]
@@ -410,7 +422,7 @@
     query = rotate(qkv[:, :heads], cosine, sine).astype(BF)
     key = rotate(qkv[:, heads : 2 * heads], cosine, sine).astype(BF)
     value = qkv[:, 2 * heads :].astype(BF)
-    mixed = attend_forward(query, key, value, bias)
+    mixed, totals = attend_forward(query, key, value, bias)
     mixed, come_gate, give_up, give_down, *rest = tie(mixed, come_gate, give_up, give_down, *dy_far, *dy_near)
     dy_far, dy_near = rest[:4], rest[4:]
     come_up = pair(give_up)
@@ -471,35 +483,38 @@
     dy_far = [one, two]
     n2_far = stacked(*far)
     forward_far = wide_forward(n2_far)
-    n2_far, dy_near, *rest = tie(n2_far, dy_near, *forward_far, *dy_far, *down_blocks)
+    down_part = mm_t(forward_near[0], dy_near)
+    n2_far, dy_near, down_part, *rest = tie(n2_far, dy_near, down_part, *forward_far, *dy_far, *down_blocks)
     forward_far, dy_far, down_full = rest[:3], rest[3:5], jnp.concatenate(rest[5:], axis=1)
     gate_near, up_near = wide_backward(dy_near, *forward_near[1:])
     near = wide_input(gate_near, up_near)
-    near, gate_near, dy_near, n2_near, *dy_far = tie(near, gate_near, dy_near, n2_near, *dy_far)
+    near, gate_near, n2_near, *dy_far = tie(near, gate_near, n2_near, *dy_far)
     near = core_give(near)
     dy_far = stacked(*dy_far)
     gate_far, up_far = wide_backward(dy_far, *forward_far[1:])
-    gate_far, up_far, dy_far, dy_near, n2_near, *near = tie(gate_far, up_far, dy_far, dy_near, n2_near, *near)
+    gate_far, up_far, dy_far, n2_near, *near = tie(gate_far, up_far, dy_far, n2_near, *near)
     near = first_give(added(*near))
+    hidden_near, hidden_far = forward_near[0], forward_far[0]
+    grad_down = (down_part + mm_t(hidden_far, dy_far)).astype(BF)
+    down_low = low_sum(grad_down, 1)
     far = wide_input(gate_far, up_far)
-    far, dy_far, dy_near, n2_far, n2_near, *near = tie(far, dy_far, dy_near, n2_far, n2_near, *near)
+    far, grad_down, n2_far, n2_near, *near = tie(far, grad_down, n2_far, n2_near, *near)
     far = core_give(far)
     near = last_give(*near)
-    hidden_near, hidden_far = forward_near[0], forward_far[0]
-    grad_down = mm_t(stacked(hidden_near, hidden_far), stacked(dy_near, dy_far)).astype(BF)
-    grad_down, gate_near, hidden_near, n2_near, *rest = tie(grad_down, gate_near, hidden_near, n2_near, *far, *near)
+    gate_near, hidden_near, n2_near, down_low, *rest = tie(gate_near, hidden_near, n2_near, down_low, *far, *near)
     far, near = packed(rest, 2, 4)
     near = reduced(*near)
     far = first_give(added(*far))
-    down_low = low_give(grad_down, 1)
+    down_keep, down_give = swap(down_low, 1)
+    down_come = pair(down_give)
     near, gate_near, hidden_near, n2_far, n2_near, *far = tie(near, gate_near, hidden_near, n2_far, n2_near, *far)
     far = last_give(*far)
     n2_both = stacked(n2_near, n2_far)
-    n2_both, up_near, gate_near, hidden_near, *rest = tie(n2_both, up_near, gate_near, hidden_near, *far, *down_low)
-    far, down_low = packed(rest, 4, 2)
+    n2_both, up_near, gate_near, hidden_near, down_keep, down_come, *far = tie(
+        n2_both, up_near, gate_near, hidden_near, down_keep, down_come, *far
+    )
 
     far = pair(reduced(*far))
-    down_keep, down_give = swap(added(*down_low), 1)
     down_keep = ctx_two(down_keep)
     grad_gate_w = mm_t(n2_both, stacked(gate_near, gate_far)).astype(BF)
     middle = n1.shape[0] // 2
@@ -507,18 +522,17 @@
         mm(stacked(hidden_near[part], hidden_far[part]), down_full).astype(BF)
         for part in (slice(None, middle), slice(middle, None))
     ]
-    far, grad_gate_w, up_near, n2_both, down_give, result_keep, result_give, *down_keep = tie(
-        far, grad_gate_w, up_near, n2_both, down_give, result_keep, result_give, *down_keep
+    far, grad_gate_w, up_near, n2_both, result_keep, result_give, *down_keep = tie(
+        far, grad_gate_w, up_near, n2_both, result_keep, result_give, *down_keep
     )
     gate_low = low_give(grad_gate_w, 0)
-    down_come = pair(down_give)
     grad_n2 = unfolded(near.astype(F32) + far.astype(F32))
     back2, grad_norm2 = norm_backward(unit2, factor2, gain2_full, grad_n2)
     grad_h1 = seed.astype(F32) + back2
     dh1 = last_ask(*first_ask(grad_h1.astype(BF)))
     grad_up_w = mm_t(n2_both, stacked(up_near, up_far)).astype(BF)
     result = added(result_keep, flip(result_give, "ctx", 1, n_ctx))
-    grad_up_w, result, down_come, *rest = tie(grad_up_w, result, down_come, *dh1, *gate_low)
+    grad_up_w, result, *rest = tie(grad_up_w, result, *dh1, *gate_low)
     dh1, gate_low = packed(rest, 4, 2)
 
     dh1_own = joined(*dh1)
@@ -536,7 +550,7 @@
     grad_mixed = stacked(mixed_own, mm(dh1_come, out_full).astype(BF))
     gate_come = pair(gate_give)
     gate_keep = ctx_two(gate_keep)
-    dq, dk, dv = attend_backward(query, key, value, grad_mixed, bias, back_cosine, back_sine)
+    dq, dk, dv = attend_backward(query, key, value, totals, grad_mixed, bias, back_cosine, back_sine)
     dq, dk, dv, gate_come, down_come, *rest = tie(dq, dk, dv, gate_come, down_come, *result, *gate_keep, *up_low)
     result, gate_keep, up_low = packed(rest, 4, chips, 2)
     dqkv = jnp.concatenate([dq, dk, dv], axis=1)
@@ -594,17 +608,17 @@
     norms, output, *rest = tie(norms, output, *share_qkv, *input_grad, *up_come)
     share_qkv, input_grad, up_come = packed(rest, chips, 2, 2 * chips)
     norms, share_qkv, share_out = met(norms, "ctx", [1], n_ctx), core_two(share_qkv), core_two(share_out)
-    input_grad = as_placed(stacked(*input_grad))
-    (grad_u,) = place([(v, 2) for v in three] + [(v[None], 0) for v in up_come], both_halves, 2 * n_ctx, 1, 1)
-    grad_u, norms, *rest = tie(grad_u, norms, *share_qkv, *share_out)
+    norms, *rest = tie(norms, *share_qkv, *share_out)
     share_qkv, share_out = packed(rest, 2 * chips, 2 * chips)
     norms = met(norms, "ctx", far_bits, n_ctx)
-    (grad_o,) = place([(v[None], 0) for v in share_out], owners, n_ctx, 1, 0)
-    grad_o, norms, *share_qkv = tie(grad_o, norms, *share_qkv)
-    norms = met(norms, "shard", low_bits, n_shard)
+    input_grad = as_placed(stacked(*input_grad))
     grad_q, grad_k, grad_v = place([(v[None], 0) for v in share_qkv], owners, n_ctx, 3, 1)
     grad_q, grad_k, grad_v, norms = tie(grad_q, grad_k, grad_v, norms)
+    norms = met(norms, "shard", low_bits, n_shard)
+    (grad_u,) = place([(v, 2) for v in three] + [(v[None], 0) for v in up_come], both_halves, 2 * n_ctx, 1, 1)
+    grad_u, norms = tie(grad_u, norms)
     norms = met(norms, "shard", [top], n_shard)
+    (grad_o,) = place([(v[None], 0) for v in share_out], owners, n_ctx, 1, 0)
     norms = lax.dynamic_slice_in_dim(norms.reshape(2, width), z * block, block, axis=1)
     return (output, input_grad, norms[0], grad_q, grad_k, grad_v, grad_o, norms[1], grad_g, grad_u, grad_d)
 

time: 696 us -> 692 us (level)
  waiting for transfers between devices: 297 us -> 290 us
    ppermute x92 -> x91, waiting for transfers between devices: 270 us -> 263 us  [flip(): return lax.ppermute(values, axis, [(i, i ^ bit) for i in range(size)])]
    unnamed x251 -> x272, local copies, waits for them, and re-layouts: 27.9 us -> 31.5 us
    ppermute x92 -> x91, starting transfers between devices: 73.3 us -> 70 us  [flip(): return lax.ppermute(values, axis, [(i, i ^ bit) for i in range(size)])]
    convert_element_type x30 -> x29, other arithmetic: 24.6 us -> 27.7 us  [added(): return (keep.astype(F32) + come.astype(F32)).astype(BF)]
    dot_general x6 -> x7, matrix products: 28.9 us -> 31.3 us  [mm_t(): lax.dot_general(left, right, (((0,), (0,)), ((), ())), preferred_element_...]
    split x28 -> x27, local copies, waits for them, and re-layouts: 16.3 us -> 17.5 us  [halves(): keep, give = jnp.split(values, 2, axis=dim)]
  transfers between devices with their start and end apart: 94 -> 94, of which waited for: 41 -> 43; matrix products, arithmetic and copies ran while one was open for 24% -> 25% of each run, Pallas kernels for 8% -> 8%
where the time goes in v4:
time: 692 us; the launch traced here: 687 us
  waiting for transfers between devices  290 us (42%)
  other arithmetic  87.6 us (13%)
  matrix products  83.8 us (12%)
  local copies, waits for them, and re-layouts  72.9 us (11%)
  starting transfers between devices  70.1 us (10%)
  Pallas kernels  52.6 us (8%)
  between operations  16.5 us (2%)
  blocking collectives  13.5 us (2%)
    ppermute x91, waiting for transfers between devices, flip(): return lax.ppermute(values, axis, [(i, i ^ bit) for i in range(size)])  263 us
    ppermute x91, starting transfers between devices, flip(): return lax.ppermute(values, axis, [(i, i ^ bit) for i in range(size)])  70 us
    unnamed x272, local copies, waits for them, and re-layouts  31.5 us
    dot_general x7, matrix products, mm_t(): lax.dot_general(left, right, (((0,), (0,)), ((), ())), preferred_element_...  31.3 us
    dot_general x7, matrix products, mm(): return jnp.dot(left, right, preferred_element_type=F32)  28.4 us
    convert_element_type x29, other arithmetic, added(): return (keep.astype(F32) + come.astype(F32)).astype(BF)  27.7 us
    all_gather x1, waiting for transfers between devices, body(): lax.all_gather(jnp.concatenate(attn_pack, axis=1), 'shard', axis=0, tiled...  26.9 us
    dot_general x6, matrix products, mm_nt(): lax.dot_general(left, right, (((1,), (1,)), ((), ())), preferred_element_...  24.1 us
  transfers between devices with their start and end apart: 94, of which 43 were waited for; matrix products, arithmetic and copies ran while one was open for 25% of the time, Pallas kernels for 8%

profile of v4, /device:TPU:0, one launch (start us, length us, event | category | flops | bytes accessed | tf_op | source)
XLA Modules:
  0.0 687.4 jit_solution(14424081417593676563)
XLA Ops:
  11.2 13.5 %all_gather.7 = bf16[2,2048]{1,0:T(2,128)(2,1)S(1)} all-gather(bf16[2,512]{1,0:T(2,128)(2,1)S(1)} %pad_maximum_fusion.37), channel_id=1, replica_groups=mesh['shard'=4,'ctx'=4,'tp'=2] {'shard'}, dimensions={1}, use_global_device_ids=true | all-gather | bytes 10240 | tf_op jit(solution)/shard_map/all_gather | solution.py:392
  34.4 20.0 %collective-permute-done = bf16[256,2048]{1,0:T(8,128)(2,1)} collective-permute-done((bf16[256,2048]{1,0:T(8,128)(2,1)S(1)}, bf16[256,2048]{1,0:T(8,128)(2,1)}, u32[]{:S(2)}, u32[]{:S(2)}) %collective-permute-start) | collective-permute-done | bytes 1048608 | tf_op jit(solution)/shard_map/ppermute | solution.py:20
  61.0 4.1 or_select_fusion.bias_ref
  73.7 16.1 %collective-permute-done.2 = bf16[128,2048]{1,0:T(8,128)(2,1)} collective-permute-done((bf16[128,2048]{1,0:T(8,128)(2,1)}, bf16[128,2048]{1,0:T(8,128)(2,1)}, u32[]{:S(2)}, u32[]{:S(2)}) %collective-permute-start.2) | collective-permute-done | bytes 524320 | tf_op jit(solution)/shard_map/ppermute | solution.py:20
  89.8 26.9 %all-gather.2.cloned.1.call-done = bf16[2048,1024]{0,1:T(8,128)(2,1)} async-done(((bf16[512,1024]{0,1:T(8,128)(2,1)}), bf16[2048,1024]{0,1:T(8,128)(2,1)}) %all-gather.2.cloned.1.call-update) | async-done | bytes 4194320 | tf_op jit(solution)/shard_map/all_gather | solution.py:391
  120.8 6.2 fusion.1
  139.2 9.2 %shard_map.230 = (bf16[1024,256]{1,0:T(8,128)(2,1)S(1)}, f32[1024,256]{1,0:T(8,128)S(1)}) custom-call(bf16[1024,256]{1,0:T(8,128)(2,1)S(1)} %copy.56.query_ref, bf16[1024,256]{1,0:T(8,128)(2,1)S(1)} %copy.57.key_ref, bf16[1024,256]{1,0:T(8,128)(2,1)S(1)} %copy.64.value_ref, f32[1024,1024]{1,0:T(8,128)S(1)} %copy-done.6), custom_call_target="tpu_custom_call" | custom-call | flops 4294967296 | bytes 6291456 | tf_op jit(solution)/shard_map/pallas_call | solution.py:111
  148.5 5.0 collective-permute-done.4
  156.2 4.1 collective-permute-done.10
  169.3 8.2 %collective-permute-done.12 = bf16[2,128,1024]{2,1,0:T(8,128)(2,1)} collective-permute-done((bf16[2,128,1024]{2,1,0:T(8,128)(2,1)}, bf16[2,128,1024]{2,1,0:T(8,128)(2,1)}, u32[]{:S(2)}, u32[]{:S(2)}) %collective-permute-start.12) | collective-permute-done | bytes 524320 | tf_op jit(solution)/shard_map/ppermute | solution.py:20
  184.2 16.0 %collective-permute-done.9 = bf16[512,512]{1,0:T(8,128)(2,1)S(1)} collective-permute-done((bf16[512,512]{1,0:T(8,128)(2,1)S(1)}, bf16[512,512]{1,0:T(8,128)(2,1)S(1)}, u32[]{:S(2)}, u32[]{:S(2)}) %collective-permute-start.9) | collective-permute-done | bytes 524320 | tf_op jit(solution)/shard_map/ppermute | solution.py:20
  216.5 13.6 %collective-permute-done.16 = bf16[128,2048]{1,0:T(8,128)(2,1)S(1)} collective-permute-done((bf16[128,2048]{1,0:T(8,128)(2,1)S(1)}, bf16[128,2048]{1,0:T(8,128)(2,1)S(1)}, u32[]{:S(2)}, u32[]{:S(2)}) %collective-permute-start.16) | collective-permute-done | bytes 524320 | tf_op jit(solution)/shard_map/ppermute | solution.py:20
  230.2 11.1 %collective-permute-done.21 = bf16[1024,512]{1,0:T(8,128)(2,1)S(1)} collective-permute-done((bf16[1024,512]{1,0:T(8,128)(2,1)S(1)}, bf16[1024,512]{1,0:T(8,128)(2,1)S(1)}, u32[]{:S(2)}, u32[]{:S(2)}) %collective-permute-start.21) | collective-permute-done | bytes 1048608 | tf_op jit(solution)/shard_map/ppermute | solution.py:20
  245.7 4.8 collective-permute-done.24
  255.3 4.5 fusion.79
  260.9 8.3 %collective-permute-done.22 = bf16[512,512]{1,0:T(8,128)(2,1)S(1)} collective-permute-done((bf16[512,512]{1,0:T(8,128)(2,1)S(1)}, bf16[512,512]{1,0:T(8,128)(2,1)S(1)}, u32[]{:S(2)}, u32[]{:S(2)}) %collective-permute-start.22) | collective-permute-done | bytes 524320 | tf_op jit(solution)/shard_map/ppermute | solution.py:20
  281.5 4.5 fusion.81
  289.6 4.6 fusion.80
  294.2 5.0 collective-permute-done.31
  301.9 4.8 convolution_convert_fusion.5
  329.2 5.0 convolution_convert_fusion.4
  334.2 6.8 collective-permute-done.34
  349.1 5.4 collective-permute-done.37
  365.1 7.4 %collective-permute-done.39 = bf16[2,128,1024]{2,1,0:T(8,128)(2,1)S(1)} collective-permute-done((bf16[2,128,1024]{2,1,0:T(8,128)(2,1)S(1)}, bf16[2,128,1024]{2,1,0:T(8,128)(2,1)S(1)}, u32[]{:S(2)}, u32[]{:S(2)}) %collective-permute-start.39) | collective-permute-done | bytes 524320 | tf_op jit(solution)/shard_map/ppermute | solution.py:20
  376.9 8.5 %pad_maximum_fusion = bf16[2048,2048]{1,0:T(8,128)(2,1)} fusion(bf16[1024,2048]{1,0:T(8,128)(2,1)} %copy-done.54, bf16[1024,2048]{1,0:T(8,128)(2,1)} %copy-done.53), kind=kLoop, calls=%fused_computation | loop fusion | flops 16777216 | bytes 16777216 | tf_op jit(solution)/shard_map/concatenate | solution.py:320
  392.6 9.8 %convolution_convert_fusion.8 = bf16[2048,512]{1,0:T(8,128)(2,1)} fusion(bf16[2048,2048]{1,0:T(8,128)(2,1)} %pad_maximum_fusion, bf16[1024,512]{1,0:T(8,128)(2,1)S(1)} %copy-done.126, bf16[1024,512]{1,0:T(8,128)(2,1)S(1)} %copy-done.124), kind=kOutput, calls=%fused_computation.20 | convolution fusion | flops 4300210176 | bytes 12582912 | tf_op jit(solution)/shard_map/dot_general | solution.py:59
  402.4 4.4 convolution_convert_fusion
  406.8 4.3 convolution_convert_fusion.1
  411.0 5.4 collective-permute-done.43
  425.7 6.5 convolution_convert_fusion.7
  433.3 6.1 add_convert_fusion
  439.4 6.5 collective-permute-done.49
  477.9 20.2 %shard_map.231 = (bf16[1024,256]{1,0:T(8,128)(2,1)S(1)}, bf16[1024,256]{1,0:T(8,128)(2,1)S(1)}, bf16[1024,256]{1,0:T(8,128)(2,1)S(1)}) custom-call(bf16[1024,256]{1,0:T(8,128)(2,1)S(1)} %copy-done.36, bf16[1024,256]{1,0:T(8,128)(2,1)S(1)} %copy-done.34, bf16[1024,256]{1,0:T(8,128)(2,1)S(1)} %copy.64.value_ref, f32[1024,256]{1,0:T(8,128)S(1)} %copy-done.46, ...), custom_call_target="tpu_custom_call" | custom-call | flops 8053063680 | bytes 7864320 | tf_op jit(solution)/shard_map/pallas_call | solution.py:160
  498.2 11.2 %collective-permute-done.58 = bf16[1024,512]{1,0:T(8,128)(2,1)} collective-permute-done((bf16[1024,512]{1,0:T(8,128)(2,1)}, bf16[1024,512]{1,0:T(8,128)(2,1)}, u32[]{:S(2)}, u32[]{:S(2)}) %collective-permute-start.58) | collective-permute-done | bytes 1048608 | tf_op jit(solution)/shard_map/ppermute | solution.py:20
  514.5 4.9 convolution_convert_fusion.6
  519.4 5.8 convolution_convert_fusion.3
  534.4 6.2 collective-permute-done.62
  543.2 6.7 collective-permute-done.68
  549.9 25.3 %collective-permute-done.59 = bf16[512,512]{1,0:T(8,128)(2,1)S(1)} collective-permute-done((bf16[512,512]{1,0:T(8,128)(2,1)S(1)}, bf16[512,512]{1,0:T(8,128)(2,1)S(1)}, u32[]{:S(2)}, u32[]{:S(2)}) %collective-permute-start.59) | collective-permute-done | bytes 524320 | tf_op jit(solution)/shard_map/ppermute | solution.py:20
  576.1 11.6 %collective-permute-done.64 = bf16[1024,768]{1,0:T(8,128)(2,1)S(1)} collective-permute-done((bf16[1024,768]{1,0:T(8,128)(2,1)S(1)}, bf16[1024,768]{1,0:T(8,128)(2,1)S(1)}, u32[]{:S(2)}, u32[]{:S(2)}) %collective-permute-start.64) | collective-permute-done | bytes 1572896 | tf_op jit(solution)/shard_map/ppermute | solution.py:20
  593.0 7.7 %collective-permute-done.71 = bf16[2,128,1024]{2,1,0:T(8,128)(2,1)S(1)} collective-permute-done((bf16[2,128,1024]{2,1,0:T(8,128)(2,1)S(1)}, bf16[2,128,1024]{2,1,0:T(8,128)(2,1)S(1)}, u32[]{:S(2)}, u32[]{:S(2)}) %collective-permute-start.71) | collective-permute-done | bytes 524320 | tf_op jit(solution)/shard_map/ppermute | solution.py:20
  605.6 5.1 shard_map.233
  610.8 5.1 shard_map.232
  615.9 12.7 %collective-permute-done.69 = bf16[512,768]{1,0:T(8,128)(2,1)S(1)} collective-permute-done((bf16[512,768]{1,0:T(8,128)(2,1)S(1)}, bf16[512,768]{1,0:T(8,128)(2,1)S(1)}, u32[]{:S(2)}, u32[]{:S(2)}) %collective-permute-start.69) | collective-permute-done | bytes 786464 | tf_op jit(solution)/shard_map/ppermute | solution.py:20
  636.5 9.0 %collective-permute-done.78 = f32[32,128]{1,0:T(8,128)S(1)} collective-permute-done((f32[32,128]{1,0:T(8,128)S(1)}, f32[32,128]{1,0:T(8,128)S(1)}, u32[]{:S(2)}, u32[]{:S(2)}) %collective-permute-start.78) | collective-permute-done | bytes 16416 | tf_op jit(solution)/shard_map/ppermute | solution.py:20
  647.2 4.8 collective-permute-done.79
  662.8 5.3 shard_map.235
  669.4 5.1 shard_map.234
  (643 shorter events, 257.6 us)
Async XLA Ops:
  7.2 109.5 %all-gather.2.cloned.1.call-start = ((), (), s32[]{:S(2)}) async-start(), calls=%async_computation.2 | async-start | bytes 5242880 | tf_op jit(solution)/shard_map/all_gather | solution.py:391
  11.1 344.9 %reduce-scatter.3.cloned.1.call-start = ((), (), s32[]{:S(2)}) async-start(), calls=%async_computation.3 | async-start | bytes 3145728 | tf_op jit(solution)/shard_map/reduce_scatter | solution.py:334
  28.1 26.2 %collective-permute-start = (bf16[256,2048]{1,0:T(8,128)(2,1)S(1)}, bf16[256,2048]{1,0:T(8,128)(2,1)}, u32[]{:S(2)}, u32[]{:S(2)}) collective-permute-start(bf16[256,2048]{1,0:T(8,128)(2,1)S(1)} %get-tuple-element.606), channel_id=1, source_target_pairs={{0,4},{2,6},{4,0},{6,2},{1,5},{3,7},{5,1},{7,3},{8,12},{10,14},{12... | collective-permute-start | bytes 3145736 | tf_op jit(solution)/shard_map/ppermute | solution.py:20
  30.8 59.0 %collective-permute-start.3 = (bf16[256,2048]{1,0:T(8,128)(2,1)}, bf16[256,2048]{1,0:T(8,128)(2,1)}, u32[]{:S(2)}, u32[]{:S(2)}) collective-permute-start(bf16[256,2048]{1,0:T(8,128)(2,1)} %pad_maximum_fusion.14), channel_id=1, source_target_pairs={{0,4},{2,6},{4,0},{6,2},{1,5},{3,7},{5,1},{7,3},{8,12},{10,14},{12... | collective-permute-start | bytes 3145736 | tf_op jit(solution)/shard_map/ppermute | solution.py:20
  33.3 56.5 %collective-permute-start.2 = (bf16[128,2048]{1,0:T(8,128)(2,1)}, bf16[128,2048]{1,0:T(8,128)(2,1)}, u32[]{:S(2)}, u32[]{:S(2)}) collective-permute-start(bf16[128,2048]{1,0:T(8,128)(2,1)} %slice.184), channel_id=1, source_target_pairs={{0,16},{8,24},{16,0},{24,8},{1,17},{9,25},{17,1},{25,9},{2,18},{10... | collective-permute-start | bytes 1572872 | tf_op jit(solution)/shard_map/ppermute | solution.py:20
  129.4 24.1 %collective-permute-start.4 = (bf16[512,512]{1,0:T(8,128)(2,1)}, bf16[512,512]{1,0:T(8,128)(2,1)}, u32[]{:S(2)}, u32[]{:S(2)}) collective-permute-start(bf16[512,512]{1,0:T(8,128)(2,1)} %get-tuple-element.280), channel_id=1, source_target_pairs={{0,16},{8,24},{16,0},{24,8},{1,17},{9,25},{17,1},{25,9},{2,18},{10... | collective-permute-start | bytes 1572872 | tf_op jit(solution)/shard_map/ppermute | solution.py:20
  131.4 22.1 %collective-permute-start.8 = (bf16[2,128,1024]{2,1,0:T(8,128)(2,1)}, bf16[2,128,1024]{2,1,0:T(8,128)(2,1)}, u32[]{:S(2)}, u32[]{:S(2)}) collective-permute-start(bf16[2,128,1024]{2,1,0:T(8,128)(2,1)} %bitcast.11), channel_id=1, source_target_pairs={{0,1},{1,0},{2,3},{3,2},{4,5},{5,4},{6,7},{7,6},{8,9},{9,8},{10,11... | collective-permute-start | bytes 1572872 | tf_op jit(solution)/shard_map/ppermute | solution.py:20
  133.7 19.8 %collective-permute-start.6 = (bf16[256,1024]{1,0:T(8,128)(2,1)}, bf16[256,1024]{1,0:T(8,128)(2,1)}, u32[]{:S(2)}, u32[]{:S(2)}) collective-permute-start(bf16[256,1024]{1,0:T(8,128)(2,1)} %pad_maximum_fusion.22), channel_id=1, source_target_pairs={{0,4},{2,6},{4,0},{6,2},{1,5},{3,7},{5,1},{7,3},{8,12},{10,14},{12... | collective-permute-start | bytes 1572872 | tf_op jit(solution)/shard_map/ppermute | solution.py:20
  163.2 14.3 %collective-permute-start.12 = (bf16[2,128,1024]{2,1,0:T(8,128)(2,1)}, bf16[2,128,1024]{2,1,0:T(8,128)(2,1)}, u32[]{:S(2)}, u32[]{:S(2)}) collective-permute-start(bf16[2,128,1024]{2,1,0:T(8,128)(2,1)} %get-tuple-element.635), channel_id=1, source_target_pairs={{0,1},{1,0},{2,3},{3,2},{4,5},{5,4},{6,7},{7,6},{8,9},{9,8},{10,11... | collective-permute-start | bytes 1572872 | tf_op jit(solution)/shard_map/ppermute | solution.py:20
  166.0 36.3 %collective-permute-start.15 = (bf16[1024,512]{1,0:T(8,128)(2,1)S(1)}, bf16[1024,512]{1,0:T(8,128)(2,1)S(1)}, u32[]{:S(2)}, u32[]{:S(2)}) collective-permute-start(bf16[1024,512]{1,0:T(8,128)(2,1)S(1)} %maximum_select_fusion), channel_id=1, source_target_pairs={{0,8},{8,0},{16,24},{24,16},{1,9},{9,1},{17,25},{25,17},{2,10},{10... | collective-permute-start | bytes 3145736 | tf_op jit(solution)/shard_map/ppermute | solution.py:20
  166.1 34.0 %collective-permute-start.9 = (bf16[512,512]{1,0:T(8,128)(2,1)S(1)}, bf16[512,512]{1,0:T(8,128)(2,1)S(1)}, u32[]{:S(2)}, u32[]{:S(2)}) collective-permute-start(bf16[512,512]{1,0:T(8,128)(2,1)S(1)} %copy-done.97), channel_id=1, source_target_pairs={{0,16},{8,24},{16,0},{24,8},{1,17},{9,25},{17,1},{25,9},{2,18},{10... | collective-permute-start | bytes 1572872 | tf_op jit(solution)/shard_map/ppermute | solution.py:20
  179.0 23.3 %collective-permute-start.14 = (bf16[128,1024]{1,0:T(8,128)(2,1)S(1)}, bf16[128,1024]{1,0:T(8,128)(2,1)S(1)}, u32[]{:S(2)}, u32[]{:S(2)}) collective-permute-start(bf16[128,1024]{1,0:T(8,128)(2,1)S(1)} %get-tuple-element.665), channel_id=1, source_target_pairs={{0,4},{2,6},{4,0},{6,2},{1,5},{3,7},{5,1},{7,3},{8,12},{10,14},{12... | collective-permute-start | bytes 786440 | tf_op jit(solution)/shard_map/ppermute | solution.py:20
  180.7 21.6 %collective-permute-start.13 = (bf16[128,1024]{1,0:T(8,128)(2,1)S(1)}, bf16[128,1024]{1,0:T(8,128)(2,1)S(1)}, u32[]{:S(2)}, u32[]{:S(2)}) collective-permute-start(bf16[128,1024]{1,0:T(8,128)(2,1)S(1)} %get-tuple-element.667), channel_id=1, source_target_pairs={{0,1},{1,0},{2,3},{3,2},{4,5},{5,4},{6,7},{7,6},{8,9},{9,8},{10,11... | collective-permute-start | bytes 786440 | tf_op jit(solution)/shard_map/ppermute | solution.py:20
  205.9 24.3 %collective-permute-start.16 = (bf16[128,2048]{1,0:T(8,128)(2,1)S(1)}, bf16[128,2048]{1,0:T(8,128)(2,1)S(1)}, u32[]{:S(2)}, u32[]{:S(2)}) collective-permute-start(bf16[128,2048]{1,0:T(8,128)(2,1)S(1)} %pad_maximum_fusion.24), channel_id=1, source_target_pairs={{0,16},{8,24},{16,0},{24,8},{1,17},{9,25},{17,1},{25,9},{2,18},{10... | collective-permute-start | bytes 1572872 | tf_op jit(solution)/shard_map/ppermute | solution.py:20
  207.6 33.8 %collective-permute-start.21 = (bf16[1024,512]{1,0:T(8,128)(2,1)S(1)}, bf16[1024,512]{1,0:T(8,128)(2,1)S(1)}, u32[]{:S(2)}, u32[]{:S(2)}) collective-permute-start(bf16[1024,512]{1,0:T(8,128)(2,1)S(1)} %maximum_select_fusion.1), channel_id=1, source_target_pairs={{0,8},{8,0},{16,24},{24,16},{1,9},{9,1},{17,25},{25,17},{2,10},{10... | collective-permute-start | bytes 3145736 | tf_op jit(solution)/shard_map/ppermute | solution.py:20
  211.2 19.0 %collective-permute-start.20 = (bf16[2,128,1024]{2,1,0:T(8,128)(2,1)S(1)}, bf16[2,128,1024]{2,1,0:T(8,128)(2,1)S(1)}, u32[]{:S(2)}, u32[]{:S(2)}) collective-permute-start(bf16[2,128,1024]{2,1,0:T(8,128)(2,1)S(1)} %bitcast.157), channel_id=1, source_target_pairs={{0,1},{1,0},{2,3},{3,2},{4,5},{5,4},{6,7},{7,6},{8,9},{9,8},{10,11... | collective-permute-start | bytes 1572872 | tf_op jit(solution)/shard_map/ppermute | solution.py:20
  212.8 17.4 %collective-permute-start.19 = (bf16[256,1024]{1,0:T(8,128)(2,1)S(1)}, bf16[256,1024]{1,0:T(8,128)(2,1)S(1)}, u32[]{:S(2)}, u32[]{:S(2)}) collective-permute-start(bf16[256,1024]{1,0:T(8,128)(2,1)S(1)} %constant_dynamic-update-slice_fusion.1), channel_id=1, source_target_pairs={{0,4},{2,6},{4,0},{6,2},{1,5},{3,7},{5,1},{7,3},{8,12},{10,14},{12... | collective-permute-start | bytes 1572872 | tf_op jit(solution)/shard_map/ppermute | solution.py:20
  243.4 25.9 %collective-permute-start.22 = (bf16[512,512]{1,0:T(8,128)(2,1)S(1)}, bf16[512,512]{1,0:T(8,128)(2,1)S(1)}, u32[]{:S(2)}, u32[]{:S(2)}) collective-permute-start(bf16[512,512]{1,0:T(8,128)(2,1)S(1)} %copy-done.96), channel_id=1, source_target_pairs={{0,16},{8,24},{16,0},{24,8},{1,17},{9,25},{17,1},{25,9},{2,18},{10... | collective-permute-start | bytes 1572872 | tf_op jit(solution)/shard_map/ppermute | solution.py:20
  245.2 28.5 %collective-permute-start.29 = (bf16[512,2048]{1,0:T(8,128)(2,1)S(1)}, bf16[512,2048]{1,0:T(8,128)(2,1)S(1)}, u32[]{:S(2)}, u32[]{:S(2)}) collective-permute-start(bf16[512,2048]{1,0:T(8,128)(2,1)S(1)} %pad_maximum_fusion.5), channel_id=1, source_target_pairs={{0,2},{2,0},{4,6},{6,4},{1,3},{3,1},{5,7},{7,5},{8,10},{10,8},{12,... | collective-permute-start | bytes 6291464 | tf_op jit(solution)/shard_map/ppermute | solution.py:20
  250.8 18.5 %collective-permute-start.27 = (bf16[2,128,1024]{2,1,0:T(8,128)(2,1)S(1)}, bf16[2,128,1024]{2,1,0:T(8,128)(2,1)S(1)}, u32[]{:S(2)}, u32[]{:S(2)}) collective-permute-start(bf16[2,128,1024]{2,1,0:T(8,128)(2,1)S(1)} %bitcast.155), channel_id=1, source_target_pairs={{0,1},{1,0},{2,3},{3,2},{4,5},{5,4},{6,7},{7,6},{8,9},{9,8},{10,11... | collective-permute-start | bytes 1572872 | tf_op jit(solution)/shard_map/ppermute | solution.py:20
  252.3 16.9 %collective-permute-start.26 = (bf16[256,1024]{1,0:T(8,128)(2,1)S(1)}, bf16[256,1024]{1,0:T(8,128)(2,1)S(1)}, u32[]{:S(2)}, u32[]{:S(2)}) collective-permute-start(bf16[256,1024]{1,0:T(8,128)(2,1)S(1)} %constant_dynamic-update-slice_fusion.7), channel_id=1, source_target_pairs={{0,4},{2,6},{4,0},{6,2},{1,5},{3,7},{5,1},{7,3},{8,12},{10,14},{12... | collective-permute-start | bytes 1572872 | tf_op jit(solution)/shard_map/ppermute | solution.py:20
  273.6 25.6 %collective-permute-start.31 = (bf16[512,1024]{1,0:T(8,128)(2,1)S(1)}, bf16[512,1024]{1,0:T(8,128)(2,1)S(1)}, u32[]{:S(2)}, u32[]{:S(2)}) collective-permute-start(bf16[512,1024]{1,0:T(8,128)(2,1)S(1)} %maximum_select_fusion.2), channel_id=1, source_target_pairs={{0,8},{8,0},{16,24},{24,16},{1,9},{9,1},{17,25},{25,17},{2,10},{10... | collective-permute-start | bytes 3145736 | tf_op jit(solution)/shard_map/ppermute | solution.py:20
  322.5 196.9 %reduce-scatter.5.cloned.1.call-start = ((), (), s32[]{:S(2)}) async-start(), calls=%async_computation.4 | async-start | bytes 1310720 | tf_op jit(solution)/shard_map/reduce_scatter | solution.py:547
  326.6 14.3 %collective-permute-start.34 = (bf16[2,128,1024]{2,1,0:T(8,128)(2,1)S(1)}, bf16[2,128,1024]{2,1,0:T(8,128)(2,1)S(1)}, u32[]{:S(2)}, u32[]{:S(2)}) collective-permute-start(bf16[2,128,1024]{2,1,0:T(8,128)(2,1)S(1)} %get-tuple-element.633), channel_id=1, source_target_pairs={{0,1},{1,0},{2,3},{3,2},{4,5},{5,4},{6,7},{7,6},{8,9},{9,8},{10,11... | collective-permute-start | bytes 1572872 | tf_op jit(solution)/shard_map/ppermute | solution.py:20
  327.7 14.1 %collective-permute-start.33 = (bf16[256,1024]{1,0:T(8,128)(2,1)S(1)}, bf16[256,1024]{1,0:T(8,128)(2,1)S(1)}, u32[]{:S(2)}, u32[]{:S(2)}) collective-permute-start(bf16[256,1024]{1,0:T(8,128)(2,1)S(1)} %get-tuple-element.591), channel_id=1, source_target_pairs={{0,4},{2,6},{4,0},{6,2},{1,5},{3,7},{5,1},{7,3},{8,12},{10,14},{12... | collective-permute-start | bytes 1572872 | tf_op jit(solution)/shard_map/ppermute | solution.py:20
  361.8 25.3 %collective-permute-start.40 = (bf16[512,512]{1,0:T(8,128)(2,1)}, bf16[512,512]{1,0:T(8,128)(2,1)}, u32[]{:S(2)}, u32[]{:S(2)}) collective-permute-start(bf16[512,512]{1,0:T(8,128)(2,1)} %get-tuple-element.629), channel_id=1, source_target_pairs={{0,16},{8,24},{16,0},{24,8},{1,17},{9,25},{17,1},{25,9},{2,18},{10... | collective-permute-start | bytes 1572872 | tf_op jit(solution)/shard_map/ppermute | solution.py:20
  391.4 25.1 %collective-permute-start.43 = (bf16[128,2048]{1,0:T(8,128)(2,1)S(1)}, bf16[128,2048]{1,0:T(8,128)(2,1)S(1)}, u32[]{:S(2)}, u32[]{:S(2)}) collective-permute-start(bf16[128,2048]{1,0:T(8,128)(2,1)S(1)} %pad_maximum_fusion.28), channel_id=1, source_target_pairs={{0,16},{8,24},{16,0},{24,8},{1,17},{9,25},{17,1},{25,9},{2,18},{10... | collective-permute-start | bytes 1572872 | tf_op jit(solution)/shard_map/ppermute | solution.py:20
  391.9 24.6 %collective-permute-start.44 = (bf16[512,512]{1,0:T(8,128)(2,1)S(1)}, bf16[512,512]{1,0:T(8,128)(2,1)S(1)}, u32[]{:S(2)}, u32[]{:S(2)}) collective-permute-start(bf16[512,512]{1,0:T(8,128)(2,1)S(1)} %get-tuple-element.489), channel_id=1, source_target_pairs={{0,4},{2,6},{4,0},{6,2},{1,5},{3,7},{5,1},{7,3},{8,12},{10,14},{12... | collective-permute-start | bytes 1572872 | tf_op jit(solution)/shard_map/ppermute | solution.py:20
  417.2 16.1 %collective-permute-start.45 = (bf16[1024,2048]{1,0:T(8,128)(2,1)}, bf16[1024,2048]{1,0:T(8,128)(2,1)}, u32[]{:S(2)}, u32[]{:S(2)}) collective-permute-start(bf16[1024,2048]{1,0:T(8,128)(2,1)} %convolution_convert_fusion), channel_id=1, source_target_pairs={{0,2},{2,0},{4,6},{6,4},{1,3},{3,1},{5,7},{7,5},{8,10},{10,8},{12,... | collective-permute-start | bytes 12582920 | tf_op jit(solution)/shard_map/ppermute | solution.py:20
  425.6 24.8 %collective-permute-start.50 = (bf16[1024,512]{1,0:T(8,128)(2,1)S(1)}, bf16[1024,512]{1,0:T(8,128)(2,1)S(1)}, u32[]{:S(2)}, u32[]{:S(2)}) collective-permute-start(bf16[1024,512]{1,0:T(8,128)(2,1)S(1)} %get-tuple-element.585), channel_id=1, source_target_pairs={{0,8},{8,0},{16,24},{24,16},{1,9},{9,1},{17,25},{25,17},{2,10},{10... | collective-permute-start | bytes 3145736 | tf_op jit(solution)/shard_map/ppermute | solution.py:20
  457.5 51.9 %collective-permute-start.58 = (bf16[1024,512]{1,0:T(8,128)(2,1)}, bf16[1024,512]{1,0:T(8,128)(2,1)}, u32[]{:S(2)}, u32[]{:S(2)}) collective-permute-start(bf16[1024,512]{1,0:T(8,128)(2,1)} %get-tuple-element.581), channel_id=1, source_target_pairs={{0,8},{8,0},{16,24},{24,16},{1,9},{9,1},{17,25},{25,17},{2,10},{10... | collective-permute-start | bytes 3145736 | tf_op jit(solution)/shard_map/ppermute | solution.py:20
  469.9 42.6 %collective-permute-start.54 = (bf16[512,512]{1,0:T(8,128)(2,1)S(1)}, bf16[512,512]{1,0:T(8,128)(2,1)S(1)}, u32[]{:S(2)}, u32[]{:S(2)}) collective-permute-start(bf16[512,512]{1,0:T(8,128)(2,1)S(1)} %get-tuple-element.620), channel_id=1, source_target_pairs={{0,16},{8,24},{16,0},{24,8},{1,17},{9,25},{17,1},{25,9},{2,18},{10... | collective-permute-start | bytes 1572872 | tf_op jit(solution)/shard_map/ppermute | solution.py:20
  471.4 41.0 %collective-permute-start.57 = (bf16[512,512]{1,0:T(8,128)(2,1)S(1)}, bf16[512,512]{1,0:T(8,128)(2,1)S(1)}, u32[]{:S(2)}, u32[]{:S(2)}) collective-permute-start(bf16[512,512]{1,0:T(8,128)(2,1)S(1)} %get-tuple-element.475), channel_id=1, source_target_pairs={{0,4},{2,6},{4,0},{6,2},{1,5},{3,7},{5,1},{7,3},{8,12},{10,14},{12... | collective-permute-start | bytes 1572872 | tf_op jit(solution)/shard_map/ppermute | solution.py:20
  473.2 40.0 %collective-permute-start.56 = (bf16[2,128,2048]{2,1,0:T(8,128)(2,1)}, bf16[2,128,2048]{2,1,0:T(8,128)(2,1)S(1)}, u32[]{:S(2)}, u32[]{:S(2)}) collective-permute-start(bf16[2,128,2048]{2,1,0:T(8,128)(2,1)} %get-tuple-element.583), channel_id=1, source_target_pairs={{0,1},{1,0},{2,3},{3,2},{4,5},{5,4},{6,7},{7,6},{8,9},{9,8},{10,11... | collective-permute-start | bytes 3145736 | tf_op jit(solution)/shard_map/ppermute | solution.py:20
  474.4 38.8 %collective-permute-start.55 = (bf16[256,2048]{1,0:T(8,128)(2,1)S(1)}, bf16[256,2048]{1,0:T(8,128)(2,1)S(1)}, u32[]{:S(2)}, u32[]{:S(2)}) collective-permute-start(bf16[256,2048]{1,0:T(8,128)(2,1)S(1)} %copy-done.95), channel_id=1, source_target_pairs={{0,4},{2,6},{4,0},{6,2},{1,5},{3,7},{5,1},{7,3},{8,12},{10,14},{12... | collective-permute-start | bytes 3145736 | tf_op jit(solution)/shard_map/ppermute | solution.py:20
  525.7 15.6 %collective-permute-start.60 = (bf16[512,2048]{1,0:T(8,128)(2,1)S(1)}, bf16[512,2048]{1,0:T(8,128)(2,1)S(1)}, u32[]{:S(2)}, u32[]{:S(2)}) collective-permute-start(bf16[512,2048]{1,0:T(8,128)(2,1)S(1)} %get-tuple-element.551), channel_id=1, source_target_pairs={{0,2},{2,0},{4,6},{6,4},{1,3},{3,1},{5,7},{7,5},{8,10},{10,8},{12,... | collective-permute-start | bytes 6291464 | tf_op jit(solution)/shard_map/ppermute | solution.py:20
  529.1 58.6 %collective-permute-start.64 = (bf16[1024,768]{1,0:T(8,128)(2,1)S(1)}, bf16[1024,768]{1,0:T(8,128)(2,1)S(1)}, u32[]{:S(2)}, u32[]{:S(2)}) collective-permute-start(bf16[1024,768]{1,0:T(8,128)(2,1)S(1)} %get-tuple-element.575), channel_id=1, source_target_pairs={{0,8},{8,0},{16,24},{24,16},{1,9},{9,1},{17,25},{25,17},{2,10},{10... | collective-permute-start | bytes 4718600 | tf_op jit(solution)/shard_map/ppermute | solution.py:20
  530.9 44.3 %collective-permute-start.59 = (bf16[512,512]{1,0:T(8,128)(2,1)S(1)}, bf16[512,512]{1,0:T(8,128)(2,1)S(1)}, u32[]{:S(2)}, u32[]{:S(2)}) collective-permute-start(bf16[512,512]{1,0:T(8,128)(2,1)S(1)} %get-tuple-element.618), channel_id=1, source_target_pairs={{0,16},{8,24},{16,0},{24,8},{1,17},{9,25},{17,1},{25,9},{2,18},{10... | collective-permute-start | bytes 1572872 | tf_op jit(solution)/shard_map/ppermute | solution.py:20
  541.3 46.4 %collective-permute-start.65 = (bf16[3,512,512]{2,1,0:T(8,128)(2,1)S(1)}, bf16[3,512,512]{2,1,0:T(8,128)(2,1)S(1)}, u32[]{:S(2)}, u32[]{:S(2)}) collective-permute-start(bf16[3,512,512]{2,1,0:T(8,128)(2,1)S(1)} %pad_maximum_fusion.12.refs_4_.refs_0_), channel_id=1, source_target_pairs={{0,4},{2,6},{4,0},{6,2},{1,5},{3,7},{5,1},{7,3},{8,12},{10,14},{12... | collective-permute-start | bytes 4718600 | tf_op jit(solution)/shard_map/ppermute | solution.py:20
  543.1 44.6 %collective-permute-start.63 = (bf16[128,2048]{1,0:T(8,128)(2,1)S(1)}, bf16[128,2048]{1,0:T(8,128)(2,1)S(1)}, u32[]{:S(2)}, u32[]{:S(2)}) collective-permute-start(bf16[128,2048]{1,0:T(8,128)(2,1)S(1)} %add_convert_fusion.15), channel_id=1, source_target_pairs={{0,16},{8,24},{16,0},{24,8},{1,17},{9,25},{17,1},{25,9},{2,18},{10... | collective-permute-start | bytes 1572872 | tf_op jit(solution)/shard_map/ppermute | solution.py:20
  549.9 37.8 %collective-permute-start.66 = (bf16[512,512]{1,0:T(8,128)(2,1)S(1)}, bf16[512,512]{1,0:T(8,128)(2,1)S(1)}, u32[]{:S(2)}, u32[]{:S(2)}) collective-permute-start(bf16[512,512]{1,0:T(8,128)(2,1)S(1)} %copy-done.10), channel_id=1, source_target_pairs={{0,2},{2,0},{4,6},{6,4},{1,3},{3,1},{5,7},{7,5},{8,10},{10,8},{12,... | collective-permute-start | bytes 1572872 | tf_op jit(solution)/shard_map/ppermute | solution.py:20
  591.6 37.0 %collective-permute-start.69 = (bf16[512,768]{1,0:T(8,128)(2,1)S(1)}, bf16[512,768]{1,0:T(8,128)(2,1)S(1)}, u32[]{:S(2)}, u32[]{:S(2)}) collective-permute-start(bf16[512,768]{1,0:T(8,128)(2,1)S(1)} %get-tuple-element.600), channel_id=1, source_target_pairs={{0,16},{8,24},{16,0},{24,8},{1,17},{9,25},{17,1},{25,9},{2,18},{10... | collective-permute-start | bytes 2359304 | tf_op jit(solution)/shard_map/ppermute | solution.py:20
  601.1 27.5 %collective-permute-start.75 = (bf16[128,1024]{1,0:T(8,128)(2,1)S(1)}, bf16[128,1024]{1,0:T(8,128)(2,1)S(1)}, u32[]{:S(2)}, u32[]{:S(2)}) collective-permute-start(bf16[128,1024]{1,0:T(8,128)(2,1)S(1)} %get-tuple-element.645), channel_id=1, source_target_pairs={{0,4},{2,6},{4,0},{6,2},{1,5},{3,7},{5,1},{7,3},{8,12},{10,14},{12... | collective-permute-start | bytes 786440 | tf_op jit(solution)/shard_map/ppermute | solution.py:20
  602.5 26.1 %collective-permute-start.76 = (bf16[512,512]{1,0:T(8,128)(2,1)S(1)}, bf16[512,512]{1,0:T(8,128)(2,1)S(1)}, u32[]{:S(2)}, u32[]{:S(2)}) collective-permute-start(bf16[512,512]{1,0:T(8,128)(2,1)S(1)} %collective-permute-done.59), channel_id=1, source_target_pairs={{0,4},{2,6},{4,0},{6,2},{1,5},{3,7},{5,1},{7,3},{8,12},{10,14},{12... | collective-permute-start | bytes 1572872 | tf_op jit(solution)/shard_map/ppermute | solution.py:20
  603.2 26.2 %collective-permute-start.77 = (bf16[128,2048]{1,0:T(8,128)(2,1)S(1)}, bf16[128,2048]{1,0:T(8,128)(2,1)S(1)}, u32[]{:S(2)}, u32[]{:S(2)}) collective-permute-start(bf16[128,2048]{1,0:T(8,128)(2,1)S(1)} %fusion.30), channel_id=1, source_target_pairs={{0,1},{1,0},{2,3},{3,2},{4,5},{5,4},{6,7},{7,6},{8,9},{9,8},{10,11... | collective-permute-start | bytes 1572872 | tf_op jit(solution)/shard_map/ppermute | solution.py:20
  605.1 23.5 %collective-permute-start.74 = (bf16[128,1024]{1,0:T(8,128)(2,1)S(1)}, bf16[128,1024]{1,0:T(8,128)(2,1)S(1)}, u32[]{:S(2)}, u32[]{:S(2)}) collective-permute-start(bf16[128,1024]{1,0:T(8,128)(2,1)S(1)} %get-tuple-element.647), channel_id=1, source_target_pairs={{0,1},{1,0},{2,3},{3,2},{4,5},{5,4},{6,7},{7,6},{8,9},{9,8},{10,11... | collective-permute-start | bytes 786440 | tf_op jit(solution)/shard_map/ppermute | solution.py:20
  631.1 14.4 %collective-permute-start.80 = (bf16[128,2048]{1,0:T(8,128)(2,1)}, bf16[128,2048]{1,0:T(8,128)(2,1)}, u32[]{:S(2)}, u32[]{:S(2)}) collective-permute-start(bf16[128,2048]{1,0:T(8,128)(2,1)} %fusion.22), channel_id=1, source_target_pairs={{0,1},{1,0},{2,3},{3,2},{4,5},{5,4},{6,7},{7,6},{8,9},{9,8},{10,11... | collective-permute-start | bytes 1572872 | tf_op jit(solution)/shard_map/ppermute | solution.py:20
  632.4 19.5 %collective-permute-start.79 = (bf16[512,768]{1,0:T(8,128)(2,1)}, bf16[512,768]{1,0:T(8,128)(2,1)}, u32[]{:S(2)}, u32[]{:S(2)}) collective-permute-start(bf16[512,768]{1,0:T(8,128)(2,1)} %add_convert_fusion.12), channel_id=1, source_target_pairs={{0,4},{2,6},{4,0},{6,2},{1,5},{3,7},{5,1},{7,3},{8,12},{10,14},{12... | collective-permute-start | bytes 2359304 | tf_op jit(solution)/shard_map/ppermute | solution.py:20
  (177 other events, 1725.2 us)
Sparse Core Ops, SparseCore 0:
  11.2 105.4 all-gather.1
  322.7 31.6 reduce-scatter.2
  468.2 41.1 reduce-scatter.4

commit v5 on v4

--- a/solution.py
+++ b/solution.py
@@ -509,28 +509,27 @@
     down_come = pair(down_give)
     near, gate_near, hidden_near, n2_far, n2_near, *far = tie(near, gate_near, hidden_near, n2_far, n2_near, *far)
     far = last_give(*far)
-    n2_both = stacked(n2_near, n2_far)
-    n2_both, up_near, gate_near, hidden_near, down_keep, down_come, *far = tie(
-        n2_both, up_near, gate_near, hidden_near, down_keep, down_come, *far
+    n2_near, n2_far, up_near, gate_near, hidden_near, down_keep, down_come, *far = tie(
+        n2_near, n2_far, up_near, gate_near, hidden_near, down_keep, down_come, *far
     )
 
     far = pair(reduced(*far))
     down_keep = ctx_two(down_keep)
-    grad_gate_w = mm_t(n2_both, stacked(gate_near, gate_far)).astype(BF)
+    grad_gate_w = (mm_t(n2_near, gate_near) + mm_t(n2_far, gate_far)).astype(BF)
     middle = n1.shape[0] // 2
     result_keep, result_give = [
         mm(stacked(hidden_near[part], hidden_far[part]), down_full).astype(BF)
         for part in (slice(None, middle), slice(middle, None))
     ]
-    far, grad_gate_w, up_near, n2_both, result_keep, result_give, *down_keep = tie(
-        far, grad_gate_w, up_near, n2_both, result_keep, result_give, *down_keep
+    far, grad_gate_w, up_near, n2_near, n2_far, result_keep, result_give, *down_keep = tie(
+        far, grad_gate_w, up_near, n2_near, n2_far, result_keep, result_give, *down_keep
     )
     gate_low = low_give(grad_gate_w, 0)
     grad_n2 = unfolded(near.astype(F32) + far.astype(F32))
     back2, grad_norm2 = norm_backward(unit2, factor2, gain2_full, grad_n2)
     grad_h1 = seed.astype(F32) + back2
     dh1 = last_ask(*first_ask(grad_h1.astype(BF)))
-    grad_up_w = mm_t(n2_both, stacked(up_near, up_far)).astype(BF)
+    grad_up_w = (mm_t(n2_near, up_near) + mm_t(n2_far, up_far)).astype(BF)
     result = added(result_keep, flip(result_give, "ctx", 1, n_ctx))
     grad_up_w, result, *rest = tie(grad_up_w, result, *dh1, *gate_low)
     dh1, gate_low = packed(rest, 4, 2)

time: 692 us -> 690 us (level)
  waiting for transfers between devices: 290 us -> 306 us
  other arithmetic: 87.6 us -> 74 us
  local copies, waits for them, and re-layouts: 72.9 us -> 65.4 us
    ppermute x91, waiting for transfers between devices: 263 us -> 279 us  [flip(): return lax.ppermute(values, axis, [(i, i ^ bit) for i in range(size)])]
    concatenate x5 -> x4, other arithmetic: 10.5 us -> 1.99 us  [stacked(): return jnp.concatenate(parts, axis=0)]
    dot_general x7 -> x9, matrix products: 31.3 us -> 27.5 us  [mm_t(): lax.dot_general(left, right, (((0,), (0,)), ((), ())), preferred_element_...]
  transfers between devices with their start and end apart: 94 -> 94, of which waited for: 43 -> 44; matrix products, arithmetic and copies ran while one was open for 25% -> 22% of each run, Pallas kernels for 8% -> 8%
where the time goes in v5:
time: 690 us; the launch traced here: 685 us
  waiting for transfers between devices  306 us (44%)
  matrix products  80.5 us (12%)
  starting transfers between devices  76.9 us (11%)
  other arithmetic  74 us (11%)
  local copies, waits for them, and re-layouts  65.4 us (9%)
  Pallas kernels  52.3 us (8%)
  between operations  16.7 us (2%)
  blocking collectives  13.5 us (2%)
    ppermute x91, waiting for transfers between devices, flip(): return lax.ppermute(values, axis, [(i, i ^ bit) for i in range(size)])  279 us
    ppermute x91, starting transfers between devices, flip(): return lax.ppermute(values, axis, [(i, i ^ bit) for i in range(size)])  76.8 us
    unnamed x272, local copies, waits for them, and re-layouts  28.9 us
    dot_general x7, matrix products, mm(): return jnp.dot(left, right, preferred_element_type=F32)  28.7 us
    dot_general x9, matrix products, mm_t(): lax.dot_general(left, right, (((0,), (0,)), ((), ())), preferred_element_...  27.5 us
    all_gather x1, waiting for transfers between devices, body(): lax.all_gather(jnp.concatenate(attn_pack, axis=1), 'shard', axis=0, tiled...  26.9 us
    dot_general x6, matrix products, mm_nt(): lax.dot_general(left, right, (((1,), (1,)), ((), ())), preferred_element_...  24.2 us
    convert_element_type x29, other arithmetic, added(): return (keep.astype(F32) + come.astype(F32)).astype(BF)  23.6 us
  transfers between devices with their start and end apart: 94, of which 44 were waited for; matrix products, arithmetic and copies ran while one was open for 22% of the time, Pallas kernels for 8%

profile of v5, /device:TPU:0, one launch (start us, length us, event | category | flops | bytes accessed | tf_op | source)
XLA Modules:
  0.0 685.5 jit_solution(5054089306641809209)
XLA Ops:
  11.2 13.5 %all_gather.7 = bf16[2,2048]{1,0:T(2,128)(2,1)S(1)} all-gather(bf16[2,512]{1,0:T(2,128)(2,1)S(1)} %pad_maximum_fusion.36), channel_id=1, replica_groups=mesh['shard'=4,'ctx'=4,'tp'=2] {'shard'}, dimensions={1}, use_global_device_ids=true | all-gather | bytes 10240 | tf_op jit(solution)/shard_map/all_gather | solution.py:392
  34.4 20.0 %collective-permute-done = bf16[256,2048]{1,0:T(8,128)(2,1)} collective-permute-done((bf16[256,2048]{1,0:T(8,128)(2,1)S(1)}, bf16[256,2048]{1,0:T(8,128)(2,1)}, u32[]{:S(2)}, u32[]{:S(2)}) %collective-permute-start) | collective-permute-done | bytes 1048608 | tf_op jit(solution)/shard_map/ppermute | solution.py:20
  61.1 4.1 or_select_fusion.bias_ref
  73.7 16.1 %collective-permute-done.2 = bf16[128,2048]{1,0:T(8,128)(2,1)} collective-permute-done((bf16[128,2048]{1,0:T(8,128)(2,1)}, bf16[128,2048]{1,0:T(8,128)(2,1)}, u32[]{:S(2)}, u32[]{:S(2)}) %collective-permute-start.2) | collective-permute-done | bytes 524320 | tf_op jit(solution)/shard_map/ppermute | solution.py:20
  89.8 26.9 %all-gather.2.cloned.1.call-done = bf16[2048,1024]{0,1:T(8,128)(2,1)} async-done(((bf16[512,1024]{0,1:T(8,128)(2,1)}), bf16[2048,1024]{0,1:T(8,128)(2,1)}) %all-gather.2.cloned.1.call-update) | async-done | bytes 4194320 | tf_op jit(solution)/shard_map/all_gather | solution.py:391
  120.8 6.2 fusion.1
  139.3 9.3 %shard_map.230 = (bf16[1024,256]{1,0:T(8,128)(2,1)S(1)}, f32[1024,256]{1,0:T(8,128)S(1)}) custom-call(bf16[1024,256]{1,0:T(8,128)(2,1)S(1)} %copy.56.query_ref, bf16[1024,256]{1,0:T(8,128)(2,1)S(1)} %copy.57.key_ref, bf16[1024,256]{1,0:T(8,128)(2,1)S(1)} %copy.64.value_ref, f32[1024,1024]{1,0:T(8,128)S(1)} %copy-done.6), custom_call_target="tpu_custom_call" | custom-call | flops 4294967296 | bytes 6291456 | tf_op jit(solution)/shard_map/pallas_call | solution.py:111
  148.6 4.9 collective-permute-done.4
  156.2 4.1 collective-permute-done.10
  169.3 8.2 %collective-permute-done.12 = bf16[2,128,1024]{2,1,0:T(8,128)(2,1)} collective-permute-done((bf16[2,128,1024]{2,1,0:T(8,128)(2,1)}, bf16[2,128,1024]{2,1,0:T(8,128)(2,1)}, u32[]{:S(2)}, u32[]{:S(2)}) %collective-permute-start.12) | collective-permute-done | bytes 524320 | tf_op jit(solution)/shard_map/ppermute | solution.py:20
  184.1 16.0 %collective-permute-done.9 = bf16[512,512]{1,0:T(8,128)(2,1)S(1)} collective-permute-done((bf16[512,512]{1,0:T(8,128)(2,1)S(1)}, bf16[512,512]{1,0:T(8,128)(2,1)S(1)}, u32[]{:S(2)}, u32[]{:S(2)}) %collective-permute-start.9) | collective-permute-done | bytes 524320 | tf_op jit(solution)/shard_map/ppermute | solution.py:20
  216.6 13.6 %collective-permute-done.16 = bf16[128,2048]{1,0:T(8,128)(2,1)S(1)} collective-permute-done((bf16[128,2048]{1,0:T(8,128)(2,1)S(1)}, bf16[128,2048]{1,0:T(8,128)(2,1)S(1)}, u32[]{:S(2)}, u32[]{:S(2)}) %collective-permute-start.16) | collective-permute-done | bytes 524320 | tf_op jit(solution)/shard_map/ppermute | solution.py:20
  230.2 11.1 %collective-permute-done.21 = bf16[1024,512]{1,0:T(8,128)(2,1)S(1)} collective-permute-done((bf16[1024,512]{1,0:T(8,128)(2,1)S(1)}, bf16[1024,512]{1,0:T(8,128)(2,1)S(1)}, u32[]{:S(2)}, u32[]{:S(2)}) %collective-permute-start.21) | collective-permute-done | bytes 1048608 | tf_op jit(solution)/shard_map/ppermute | solution.py:20
  245.7 4.8 collective-permute-done.24
  255.3 4.5 fusion.71
  260.9 8.3 %collective-permute-done.22 = bf16[512,512]{1,0:T(8,128)(2,1)S(1)} collective-permute-done((bf16[512,512]{1,0:T(8,128)(2,1)S(1)}, bf16[512,512]{1,0:T(8,128)(2,1)S(1)}, u32[]{:S(2)}, u32[]{:S(2)}) %collective-permute-start.22) | collective-permute-done | bytes 524320 | tf_op jit(solution)/shard_map/ppermute | solution.py:20
  279.6 4.5 fusion.73
  287.7 4.7 fusion.72
  292.4 6.8 collective-permute-done.31
  301.8 4.8 convolution_convert_fusion.5
  328.4 5.2 convolution_convert_fusion.4
  333.6 6.5 collective-permute-done.34
  345.9 6.4 collective-permute-done.37
  363.4 7.9 %collective-permute-done.39 = bf16[2,128,1024]{2,1,0:T(8,128)(2,1)S(1)} collective-permute-done((bf16[2,128,1024]{2,1,0:T(8,128)(2,1)S(1)}, bf16[2,128,1024]{2,1,0:T(8,128)(2,1)S(1)}, u32[]{:S(2)}, u32[]{:S(2)}) %collective-permute-start.39) | collective-permute-done | bytes 524320 | tf_op jit(solution)/shard_map/ppermute | solution.py:20
  375.3 10.7 %collective-permute-done.40 = bf16[512,512]{1,0:T(8,128)(2,1)S(1)} collective-permute-done((bf16[512,512]{1,0:T(8,128)(2,1)S(1)}, bf16[512,512]{1,0:T(8,128)(2,1)S(1)}, u32[]{:S(2)}, u32[]{:S(2)}) %collective-permute-start.40) | collective-permute-done | bytes 524320 | tf_op jit(solution)/shard_map/ppermute | solution.py:20
  390.6 3.7 add_convert_fusion.3
  394.3 4.4 convolution_convert_fusion
  398.6 4.4 convolution_convert_fusion.1
  403.0 11.4 %collective-permute-done.43 = bf16[128,2048]{1,0:T(8,128)(2,1)S(1)} collective-permute-done((bf16[128,2048]{1,0:T(8,128)(2,1)S(1)}, bf16[128,2048]{1,0:T(8,128)(2,1)S(1)}, u32[]{:S(2)}, u32[]{:S(2)}) %collective-permute-start.43) | collective-permute-done | bytes 524320 | tf_op jit(solution)/shard_map/ppermute | solution.py:20
  424.5 3.8 add_convert_fusion.2
  430.9 6.1 add_convert_fusion
  437.0 5.6 collective-permute-done.49
  476.1 19.9 %shard_map.231 = (bf16[1024,256]{1,0:T(8,128)(2,1)S(1)}, bf16[1024,256]{1,0:T(8,128)(2,1)S(1)}, bf16[1024,256]{1,0:T(8,128)(2,1)S(1)}) custom-call(bf16[1024,256]{1,0:T(8,128)(2,1)S(1)} %copy-done.36, bf16[1024,256]{1,0:T(8,128)(2,1)S(1)} %copy-done.34, bf16[1024,256]{1,0:T(8,128)(2,1)S(1)} %copy.64.value_ref, f32[1024,256]{1,0:T(8,128)S(1)} %copy-done.46, ...), custom_call_target="tpu_custom_call" | custom-call | flops 8053063680 | bytes 7864320 | tf_op jit(solution)/shard_map/pallas_call | solution.py:160
  496.0 10.4 %collective-permute-done.58 = bf16[1024,512]{1,0:T(8,128)(2,1)} collective-permute-done((bf16[1024,512]{1,0:T(8,128)(2,1)}, bf16[1024,512]{1,0:T(8,128)(2,1)}, u32[]{:S(2)}, u32[]{:S(2)}) %collective-permute-start.58) | collective-permute-done | bytes 1048608 | tf_op jit(solution)/shard_map/ppermute | solution.py:20
  510.8 4.9 convolution_convert_fusion.6
  515.7 5.8 convolution_convert_fusion.3
  531.4 5.5 collective-permute-done.62
  539.4 6.7 collective-permute-done.68
  546.2 26.2 %collective-permute-done.59 = bf16[512,512]{1,0:T(8,128)(2,1)S(1)} collective-permute-done((bf16[512,512]{1,0:T(8,128)(2,1)S(1)}, bf16[512,512]{1,0:T(8,128)(2,1)S(1)}, u32[]{:S(2)}, u32[]{:S(2)}) %collective-permute-start.59) | collective-permute-done | bytes 524320 | tf_op jit(solution)/shard_map/ppermute | solution.py:20
  573.3 11.0 %collective-permute-done.64 = bf16[1024,768]{1,0:T(8,128)(2,1)S(1)} collective-permute-done((bf16[1024,768]{1,0:T(8,128)(2,1)S(1)}, bf16[1024,768]{1,0:T(8,128)(2,1)S(1)}, u32[]{:S(2)}, u32[]{:S(2)}) %collective-permute-start.64) | collective-permute-done | bytes 1572896 | tf_op jit(solution)/shard_map/ppermute | solution.py:20
  589.3 7.6 %collective-permute-done.71 = bf16[2,128,1024]{2,1,0:T(8,128)(2,1)S(1)} collective-permute-done((bf16[2,128,1024]{2,1,0:T(8,128)(2,1)S(1)}, bf16[2,128,1024]{2,1,0:T(8,128)(2,1)S(1)}, u32[]{:S(2)}, u32[]{:S(2)}) %collective-permute-start.71) | collective-permute-done | bytes 524320 | tf_op jit(solution)/shard_map/ppermute | solution.py:20
  602.0 5.1 shard_map.233
  607.1 5.1 shard_map.232
  612.3 12.9 %collective-permute-done.69 = bf16[512,768]{1,0:T(8,128)(2,1)S(1)} collective-permute-done((bf16[512,768]{1,0:T(8,128)(2,1)S(1)}, bf16[512,768]{1,0:T(8,128)(2,1)S(1)}, u32[]{:S(2)}, u32[]{:S(2)}) %collective-permute-start.69) | collective-permute-done | bytes 786464 | tf_op jit(solution)/shard_map/ppermute | solution.py:20
  633.4 7.8 %collective-permute-done.78 = f32[32,128]{1,0:T(8,128)S(1)} collective-permute-done((f32[32,128]{1,0:T(8,128)S(1)}, f32[32,128]{1,0:T(8,128)S(1)}, u32[]{:S(2)}, u32[]{:S(2)}) %collective-permute-start.78) | collective-permute-done | bytes 16416 | tf_op jit(solution)/shard_map/ppermute | solution.py:20
  642.9 5.2 collective-permute-done.79
  658.9 5.3 shard_map.235
  665.7 5.1 shard_map.234
  (643 shorter events, 255.7 us)
Async XLA Ops:
  7.2 109.5 %all-gather.2.cloned.1.call-start = ((), (), s32[]{:S(2)}) async-start(), calls=%async_computation.2 | async-start | bytes 5242880 | tf_op jit(solution)/shard_map/all_gather | solution.py:391
  11.1 343.2 %reduce-scatter.3.cloned.1.call-start = ((), (), s32[]{:S(2)}) async-start(), calls=%async_computation.3 | async-start | bytes 3145728 | tf_op jit(solution)/shard_map/reduce_scatter | solution.py:334
  28.1 26.2 %collective-permute-start = (bf16[256,2048]{1,0:T(8,128)(2,1)S(1)}, bf16[256,2048]{1,0:T(8,128)(2,1)}, u32[]{:S(2)}, u32[]{:S(2)}) collective-permute-start(bf16[256,2048]{1,0:T(8,128)(2,1)S(1)} %get-tuple-element.610), channel_id=1, source_target_pairs={{0,4},{2,6},{4,0},{6,2},{1,5},{3,7},{5,1},{7,3},{8,12},{10,14},{12... | collective-permute-start | bytes 3145736 | tf_op jit(solution)/shard_map/ppermute | solution.py:20
  30.8 59.0 %collective-permute-start.3 = (bf16[256,2048]{1,0:T(8,128)(2,1)}, bf16[256,2048]{1,0:T(8,128)(2,1)}, u32[]{:S(2)}, u32[]{:S(2)}) collective-permute-start(bf16[256,2048]{1,0:T(8,128)(2,1)} %pad_maximum_fusion.13), channel_id=1, source_target_pairs={{0,4},{2,6},{4,0},{6,2},{1,5},{3,7},{5,1},{7,3},{8,12},{10,14},{12... | collective-permute-start | bytes 3145736 | tf_op jit(solution)/shard_map/ppermute | solution.py:20
  33.3 56.5 %collective-permute-start.2 = (bf16[128,2048]{1,0:T(8,128)(2,1)}, bf16[128,2048]{1,0:T(8,128)(2,1)}, u32[]{:S(2)}, u32[]{:S(2)}) collective-permute-start(bf16[128,2048]{1,0:T(8,128)(2,1)} %slice.184), channel_id=1, source_target_pairs={{0,16},{8,24},{16,0},{24,8},{1,17},{9,25},{17,1},{25,9},{2,18},{10... | collective-permute-start | bytes 1572872 | tf_op jit(solution)/shard_map/ppermute | solution.py:20
  129.4 24.1 %collective-permute-start.4 = (bf16[512,512]{1,0:T(8,128)(2,1)}, bf16[512,512]{1,0:T(8,128)(2,1)}, u32[]{:S(2)}, u32[]{:S(2)}) collective-permute-start(bf16[512,512]{1,0:T(8,128)(2,1)} %get-tuple-element.282), channel_id=1, source_target_pairs={{0,16},{8,24},{16,0},{24,8},{1,17},{9,25},{17,1},{25,9},{2,18},{10... | collective-permute-start | bytes 1572872 | tf_op jit(solution)/shard_map/ppermute | solution.py:20
  131.4 22.1 %collective-permute-start.8 = (bf16[2,128,1024]{2,1,0:T(8,128)(2,1)}, bf16[2,128,1024]{2,1,0:T(8,128)(2,1)}, u32[]{:S(2)}, u32[]{:S(2)}) collective-permute-start(bf16[2,128,1024]{2,1,0:T(8,128)(2,1)} %bitcast.11), channel_id=1, source_target_pairs={{0,1},{1,0},{2,3},{3,2},{4,5},{5,4},{6,7},{7,6},{8,9},{9,8},{10,11... | collective-permute-start | bytes 1572872 | tf_op jit(solution)/shard_map/ppermute | solution.py:20
  133.8 19.7 %collective-permute-start.6 = (bf16[256,1024]{1,0:T(8,128)(2,1)}, bf16[256,1024]{1,0:T(8,128)(2,1)}, u32[]{:S(2)}, u32[]{:S(2)}) collective-permute-start(bf16[256,1024]{1,0:T(8,128)(2,1)} %pad_maximum_fusion.21), channel_id=1, source_target_pairs={{0,4},{2,6},{4,0},{6,2},{1,5},{3,7},{5,1},{7,3},{8,12},{10,14},{12... | collective-permute-start | bytes 1572872 | tf_op jit(solution)/shard_map/ppermute | solution.py:20
  163.2 14.3 %collective-permute-start.12 = (bf16[2,128,1024]{2,1,0:T(8,128)(2,1)}, bf16[2,128,1024]{2,1,0:T(8,128)(2,1)}, u32[]{:S(2)}, u32[]{:S(2)}) collective-permute-start(bf16[2,128,1024]{2,1,0:T(8,128)(2,1)} %get-tuple-element.639), channel_id=1, source_target_pairs={{0,1},{1,0},{2,3},{3,2},{4,5},{5,4},{6,7},{7,6},{8,9},{9,8},{10,11... | collective-permute-start | bytes 1572872 | tf_op jit(solution)/shard_map/ppermute | solution.py:20
  166.0 36.3 %collective-permute-start.15 = (bf16[1024,512]{1,0:T(8,128)(2,1)S(1)}, bf16[1024,512]{1,0:T(8,128)(2,1)S(1)}, u32[]{:S(2)}, u32[]{:S(2)}) collective-permute-start(bf16[1024,512]{1,0:T(8,128)(2,1)S(1)} %maximum_select_fusion), channel_id=1, source_target_pairs={{0,8},{8,0},{16,24},{24,16},{1,9},{9,1},{17,25},{25,17},{2,10},{10... | collective-permute-start | bytes 3145736 | tf_op jit(solution)/shard_map/ppermute | solution.py:20
  166.1 34.0 %collective-permute-start.9 = (bf16[512,512]{1,0:T(8,128)(2,1)S(1)}, bf16[512,512]{1,0:T(8,128)(2,1)S(1)}, u32[]{:S(2)}, u32[]{:S(2)}) collective-permute-start(bf16[512,512]{1,0:T(8,128)(2,1)S(1)} %copy-done.103), channel_id=1, source_target_pairs={{0,16},{8,24},{16,0},{24,8},{1,17},{9,25},{17,1},{25,9},{2,18},{10... | collective-permute-start | bytes 1572872 | tf_op jit(solution)/shard_map/ppermute | solution.py:20
  179.0 23.3 %collective-permute-start.14 = (bf16[128,1024]{1,0:T(8,128)(2,1)S(1)}, bf16[128,1024]{1,0:T(8,128)(2,1)S(1)}, u32[]{:S(2)}, u32[]{:S(2)}) collective-permute-start(bf16[128,1024]{1,0:T(8,128)(2,1)S(1)} %get-tuple-element.669), channel_id=1, source_target_pairs={{0,4},{2,6},{4,0},{6,2},{1,5},{3,7},{5,1},{7,3},{8,12},{10,14},{12... | collective-permute-start | bytes 786440 | tf_op jit(solution)/shard_map/ppermute | solution.py:20
  180.7 21.6 %collective-permute-start.13 = (bf16[128,1024]{1,0:T(8,128)(2,1)S(1)}, bf16[128,1024]{1,0:T(8,128)(2,1)S(1)}, u32[]{:S(2)}, u32[]{:S(2)}) collective-permute-start(bf16[128,1024]{1,0:T(8,128)(2,1)S(1)} %get-tuple-element.671), channel_id=1, source_target_pairs={{0,1},{1,0},{2,3},{3,2},{4,5},{5,4},{6,7},{7,6},{8,9},{9,8},{10,11... | collective-permute-start | bytes 786440 | tf_op jit(solution)/shard_map/ppermute | solution.py:20
  205.9 24.3 %collective-permute-start.16 = (bf16[128,2048]{1,0:T(8,128)(2,1)S(1)}, bf16[128,2048]{1,0:T(8,128)(2,1)S(1)}, u32[]{:S(2)}, u32[]{:S(2)}) collective-permute-start(bf16[128,2048]{1,0:T(8,128)(2,1)S(1)} %pad_maximum_fusion.23), channel_id=1, source_target_pairs={{0,16},{8,24},{16,0},{24,8},{1,17},{9,25},{17,1},{25,9},{2,18},{10... | collective-permute-start | bytes 1572872 | tf_op jit(solution)/shard_map/ppermute | solution.py:20
  207.6 33.8 %collective-permute-start.21 = (bf16[1024,512]{1,0:T(8,128)(2,1)S(1)}, bf16[1024,512]{1,0:T(8,128)(2,1)S(1)}, u32[]{:S(2)}, u32[]{:S(2)}) collective-permute-start(bf16[1024,512]{1,0:T(8,128)(2,1)S(1)} %maximum_select_fusion.1), channel_id=1, source_target_pairs={{0,8},{8,0},{16,24},{24,16},{1,9},{9,1},{17,25},{25,17},{2,10},{10... | collective-permute-start | bytes 3145736 | tf_op jit(solution)/shard_map/ppermute | solution.py:20
  211.2 19.0 %collective-permute-start.20 = (bf16[2,128,1024]{2,1,0:T(8,128)(2,1)S(1)}, bf16[2,128,1024]{2,1,0:T(8,128)(2,1)S(1)}, u32[]{:S(2)}, u32[]{:S(2)}) collective-permute-start(bf16[2,128,1024]{2,1,0:T(8,128)(2,1)S(1)} %bitcast.161), channel_id=1, source_target_pairs={{0,1},{1,0},{2,3},{3,2},{4,5},{5,4},{6,7},{7,6},{8,9},{9,8},{10,11... | collective-permute-start | bytes 1572872 | tf_op jit(solution)/shard_map/ppermute | solution.py:20
  212.8 17.4 %collective-permute-start.19 = (bf16[256,1024]{1,0:T(8,128)(2,1)S(1)}, bf16[256,1024]{1,0:T(8,128)(2,1)S(1)}, u32[]{:S(2)}, u32[]{:S(2)}) collective-permute-start(bf16[256,1024]{1,0:T(8,128)(2,1)S(1)} %constant_dynamic-update-slice_fusion.1), channel_id=1, source_target_pairs={{0,4},{2,6},{4,0},{6,2},{1,5},{3,7},{5,1},{7,3},{8,12},{10,14},{12... | collective-permute-start | bytes 1572872 | tf_op jit(solution)/shard_map/ppermute | solution.py:20
  243.4 25.9 %collective-permute-start.22 = (bf16[512,512]{1,0:T(8,128)(2,1)S(1)}, bf16[512,512]{1,0:T(8,128)(2,1)S(1)}, u32[]{:S(2)}, u32[]{:S(2)}) collective-permute-start(bf16[512,512]{1,0:T(8,128)(2,1)S(1)} %copy-done.102), channel_id=1, source_target_pairs={{0,16},{8,24},{16,0},{24,8},{1,17},{9,25},{17,1},{25,9},{2,18},{10... | collective-permute-start | bytes 1572872 | tf_op jit(solution)/shard_map/ppermute | solution.py:20
  245.2 28.4 %collective-permute-start.29 = (bf16[512,2048]{1,0:T(8,128)(2,1)S(1)}, bf16[512,2048]{1,0:T(8,128)(2,1)S(1)}, u32[]{:S(2)}, u32[]{:S(2)}) collective-permute-start(bf16[512,2048]{1,0:T(8,128)(2,1)S(1)} %pad_maximum_fusion.4), channel_id=1, source_target_pairs={{0,2},{2,0},{4,6},{6,4},{1,3},{3,1},{5,7},{7,5},{8,10},{10,8},{12,... | collective-permute-start | bytes 6291464 | tf_op jit(solution)/shard_map/ppermute | solution.py:20
  250.7 18.5 %collective-permute-start.27 = (bf16[2,128,1024]{2,1,0:T(8,128)(2,1)S(1)}, bf16[2,128,1024]{2,1,0:T(8,128)(2,1)S(1)}, u32[]{:S(2)}, u32[]{:S(2)}) collective-permute-start(bf16[2,128,1024]{2,1,0:T(8,128)(2,1)S(1)} %bitcast.159), channel_id=1, source_target_pairs={{0,1},{1,0},{2,3},{3,2},{4,5},{5,4},{6,7},{7,6},{8,9},{9,8},{10,11... | collective-permute-start | bytes 1572872 | tf_op jit(solution)/shard_map/ppermute | solution.py:20
  252.3 16.9 %collective-permute-start.26 = (bf16[256,1024]{1,0:T(8,128)(2,1)S(1)}, bf16[256,1024]{1,0:T(8,128)(2,1)S(1)}, u32[]{:S(2)}, u32[]{:S(2)}) collective-permute-start(bf16[256,1024]{1,0:T(8,128)(2,1)S(1)} %constant_dynamic-update-slice_fusion.7), channel_id=1, source_target_pairs={{0,4},{2,6},{4,0},{6,2},{1,5},{3,7},{5,1},{7,3},{8,12},{10,14},{12... | collective-permute-start | bytes 1572872 | tf_op jit(solution)/shard_map/ppermute | solution.py:20
  273.6 25.6 %collective-permute-start.31 = (bf16[512,1024]{1,0:T(8,128)(2,1)S(1)}, bf16[512,1024]{1,0:T(8,128)(2,1)S(1)}, u32[]{:S(2)}, u32[]{:S(2)}) collective-permute-start(bf16[512,1024]{1,0:T(8,128)(2,1)S(1)} %maximum_select_fusion.2), channel_id=1, source_target_pairs={{0,8},{8,0},{16,24},{24,16},{1,9},{9,1},{17,25},{25,17},{2,10},{10... | collective-permute-start | bytes 3145736 | tf_op jit(solution)/shard_map/ppermute | solution.py:20
  322.5 193.2 %reduce-scatter.5.cloned.1.call-start = ((), (), s32[]{:S(2)}) async-start(), calls=%async_computation.4 | async-start | bytes 1310720 | tf_op jit(solution)/shard_map/reduce_scatter | solution.py:546
  325.7 14.4 %collective-permute-start.34 = (bf16[2,128,1024]{2,1,0:T(8,128)(2,1)S(1)}, bf16[2,128,1024]{2,1,0:T(8,128)(2,1)S(1)}, u32[]{:S(2)}, u32[]{:S(2)}) collective-permute-start(bf16[2,128,1024]{2,1,0:T(8,128)(2,1)S(1)} %get-tuple-element.637), channel_id=1, source_target_pairs={{0,1},{1,0},{2,3},{3,2},{4,5},{5,4},{6,7},{7,6},{8,9},{9,8},{10,11... | collective-permute-start | bytes 1572872 | tf_op jit(solution)/shard_map/ppermute | solution.py:20
  326.9 14.1 %collective-permute-start.33 = (bf16[256,1024]{1,0:T(8,128)(2,1)S(1)}, bf16[256,1024]{1,0:T(8,128)(2,1)S(1)}, u32[]{:S(2)}, u32[]{:S(2)}) collective-permute-start(bf16[256,1024]{1,0:T(8,128)(2,1)S(1)} %get-tuple-element.595), channel_id=1, source_target_pairs={{0,4},{2,6},{4,0},{6,2},{1,5},{3,7},{5,1},{7,3},{8,12},{10,14},{12... | collective-permute-start | bytes 1572872 | tf_op jit(solution)/shard_map/ppermute | solution.py:20
  360.7 25.3 %collective-permute-start.40 = (bf16[512,512]{1,0:T(8,128)(2,1)S(1)}, bf16[512,512]{1,0:T(8,128)(2,1)S(1)}, u32[]{:S(2)}, u32[]{:S(2)}) collective-permute-start(bf16[512,512]{1,0:T(8,128)(2,1)S(1)} %get-tuple-element.633), channel_id=1, source_target_pairs={{0,16},{8,24},{16,0},{24,8},{1,17},{9,25},{17,1},{25,9},{2,18},{10... | collective-permute-start | bytes 1572872 | tf_op jit(solution)/shard_map/ppermute | solution.py:20
  389.6 24.8 %collective-permute-start.43 = (bf16[128,2048]{1,0:T(8,128)(2,1)S(1)}, bf16[128,2048]{1,0:T(8,128)(2,1)S(1)}, u32[]{:S(2)}, u32[]{:S(2)}) collective-permute-start(bf16[128,2048]{1,0:T(8,128)(2,1)S(1)} %pad_maximum_fusion.27), channel_id=1, source_target_pairs={{0,16},{8,24},{16,0},{24,8},{1,17},{9,25},{17,1},{25,9},{2,18},{10... | collective-permute-start | bytes 1572872 | tf_op jit(solution)/shard_map/ppermute | solution.py:20
  389.6 24.7 %collective-permute-start.44 = (bf16[512,512]{1,0:T(8,128)(2,1)S(1)}, bf16[512,512]{1,0:T(8,128)(2,1)S(1)}, u32[]{:S(2)}, u32[]{:S(2)}) collective-permute-start(bf16[512,512]{1,0:T(8,128)(2,1)S(1)} %get-tuple-element.493), channel_id=1, source_target_pairs={{0,4},{2,6},{4,0},{6,2},{1,5},{3,7},{5,1},{7,3},{8,12},{10,14},{12... | collective-permute-start | bytes 1572872 | tf_op jit(solution)/shard_map/ppermute | solution.py:20
  415.2 15.7 %collective-permute-start.45 = (bf16[1024,2048]{1,0:T(8,128)(2,1)}, bf16[1024,2048]{1,0:T(8,128)(2,1)}, u32[]{:S(2)}, u32[]{:S(2)}) collective-permute-start(bf16[1024,2048]{1,0:T(8,128)(2,1)} %convolution_convert_fusion), channel_id=1, source_target_pairs={{0,2},{2,0},{4,6},{6,4},{1,3},{3,1},{5,7},{7,5},{8,10},{10,8},{12,... | collective-permute-start | bytes 12582920 | tf_op jit(solution)/shard_map/ppermute | solution.py:20
  421.8 24.8 %collective-permute-start.50 = (bf16[1024,512]{1,0:T(8,128)(2,1)S(1)}, bf16[1024,512]{1,0:T(8,128)(2,1)S(1)}, u32[]{:S(2)}, u32[]{:S(2)}) collective-permute-start(bf16[1024,512]{1,0:T(8,128)(2,1)S(1)} %get-tuple-element.589), channel_id=1, source_target_pairs={{0,8},{8,0},{16,24},{24,16},{1,9},{9,1},{17,25},{25,17},{2,10},{10... | collective-permute-start | bytes 3145736 | tf_op jit(solution)/shard_map/ppermute | solution.py:20
  428.3 14.2 %collective-permute-start.49 = (bf16[2,128,1024]{2,1,0:T(8,128)(2,1)S(1)}, bf16[2,128,1024]{2,1,0:T(8,128)(2,1)S(1)}, u32[]{:S(2)}, u32[]{:S(2)}) collective-permute-start(bf16[2,128,1024]{2,1,0:T(8,128)(2,1)S(1)} %bitcast.163), channel_id=1, source_target_pairs={{0,1},{1,0},{2,3},{3,2},{4,5},{5,4},{6,7},{7,6},{8,9},{9,8},{10,11... | collective-permute-start | bytes 1572872 | tf_op jit(solution)/shard_map/ppermute | solution.py:20
  453.7 52.8 %collective-permute-start.58 = (bf16[1024,512]{1,0:T(8,128)(2,1)}, bf16[1024,512]{1,0:T(8,128)(2,1)}, u32[]{:S(2)}, u32[]{:S(2)}) collective-permute-start(bf16[1024,512]{1,0:T(8,128)(2,1)} %get-tuple-element.585), channel_id=1, source_target_pairs={{0,8},{8,0},{16,24},{24,16},{1,9},{9,1},{17,25},{25,17},{2,10},{10... | collective-permute-start | bytes 3145736 | tf_op jit(solution)/shard_map/ppermute | solution.py:20
  466.1 42.6 %collective-permute-start.54 = (bf16[512,512]{1,0:T(8,128)(2,1)S(1)}, bf16[512,512]{1,0:T(8,128)(2,1)S(1)}, u32[]{:S(2)}, u32[]{:S(2)}) collective-permute-start(bf16[512,512]{1,0:T(8,128)(2,1)S(1)} %get-tuple-element.624), channel_id=1, source_target_pairs={{0,16},{8,24},{16,0},{24,8},{1,17},{9,25},{17,1},{25,9},{2,18},{10... | collective-permute-start | bytes 1572872 | tf_op jit(solution)/shard_map/ppermute | solution.py:20
  468.8 39.9 %collective-permute-start.57 = (bf16[512,512]{1,0:T(8,128)(2,1)S(1)}, bf16[512,512]{1,0:T(8,128)(2,1)S(1)}, u32[]{:S(2)}, u32[]{:S(2)}) collective-permute-start(bf16[512,512]{1,0:T(8,128)(2,1)S(1)} %get-tuple-element.479), channel_id=1, source_target_pairs={{0,4},{2,6},{4,0},{6,2},{1,5},{3,7},{5,1},{7,3},{8,12},{10,14},{12... | collective-permute-start | bytes 1572872 | tf_op jit(solution)/shard_map/ppermute | solution.py:20
  471.0 38.5 %collective-permute-start.56 = (bf16[2,128,2048]{2,1,0:T(8,128)(2,1)}, bf16[2,128,2048]{2,1,0:T(8,128)(2,1)S(1)}, u32[]{:S(2)}, u32[]{:S(2)}) collective-permute-start(bf16[2,128,2048]{2,1,0:T(8,128)(2,1)} %get-tuple-element.587), channel_id=1, source_target_pairs={{0,1},{1,0},{2,3},{3,2},{4,5},{5,4},{6,7},{7,6},{8,9},{9,8},{10,11... | collective-permute-start | bytes 3145736 | tf_op jit(solution)/shard_map/ppermute | solution.py:20
  472.5 37.0 %collective-permute-start.55 = (bf16[256,2048]{1,0:T(8,128)(2,1)S(1)}, bf16[256,2048]{1,0:T(8,128)(2,1)S(1)}, u32[]{:S(2)}, u32[]{:S(2)}) collective-permute-start(bf16[256,2048]{1,0:T(8,128)(2,1)S(1)} %copy-done.101), channel_id=1, source_target_pairs={{0,4},{2,6},{4,0},{6,2},{1,5},{3,7},{5,1},{7,3},{8,12},{10,14},{12... | collective-permute-start | bytes 3145736 | tf_op jit(solution)/shard_map/ppermute | solution.py:20
  521.9 15.9 %collective-permute-start.60 = (bf16[512,2048]{1,0:T(8,128)(2,1)S(1)}, bf16[512,2048]{1,0:T(8,128)(2,1)S(1)}, u32[]{:S(2)}, u32[]{:S(2)}) collective-permute-start(bf16[512,2048]{1,0:T(8,128)(2,1)S(1)} %get-tuple-element.555), channel_id=1, source_target_pairs={{0,2},{2,0},{4,6},{6,4},{1,3},{3,1},{5,7},{7,5},{8,10},{10,8},{12,... | collective-permute-start | bytes 6291464 | tf_op jit(solution)/shard_map/ppermute | solution.py:20
  526.2 58.1 %collective-permute-start.64 = (bf16[1024,768]{1,0:T(8,128)(2,1)S(1)}, bf16[1024,768]{1,0:T(8,128)(2,1)S(1)}, u32[]{:S(2)}, u32[]{:S(2)}) collective-permute-start(bf16[1024,768]{1,0:T(8,128)(2,1)S(1)} %get-tuple-element.579), channel_id=1, source_target_pairs={{0,8},{8,0},{16,24},{24,16},{1,9},{9,1},{17,25},{25,17},{2,10},{10... | collective-permute-start | bytes 4718600 | tf_op jit(solution)/shard_map/ppermute | solution.py:20
  528.0 44.4 %collective-permute-start.59 = (bf16[512,512]{1,0:T(8,128)(2,1)S(1)}, bf16[512,512]{1,0:T(8,128)(2,1)S(1)}, u32[]{:S(2)}, u32[]{:S(2)}) collective-permute-start(bf16[512,512]{1,0:T(8,128)(2,1)S(1)} %get-tuple-element.622), channel_id=1, source_target_pairs={{0,16},{8,24},{16,0},{24,8},{1,17},{9,25},{17,1},{25,9},{2,18},{10... | collective-permute-start | bytes 1572872 | tf_op jit(solution)/shard_map/ppermute | solution.py:20
  537.9 46.5 %collective-permute-start.65 = (bf16[3,512,512]{2,1,0:T(8,128)(2,1)S(1)}, bf16[3,512,512]{2,1,0:T(8,128)(2,1)S(1)}, u32[]{:S(2)}, u32[]{:S(2)}) collective-permute-start(bf16[3,512,512]{2,1,0:T(8,128)(2,1)S(1)} %pad_maximum_fusion.11.refs_4_.refs_0_), channel_id=1, source_target_pairs={{0,4},{2,6},{4,0},{6,2},{1,5},{3,7},{5,1},{7,3},{8,12},{10,14},{12... | collective-permute-start | bytes 4718600 | tf_op jit(solution)/shard_map/ppermute | solution.py:20
  539.4 45.0 %collective-permute-start.63 = (bf16[128,2048]{1,0:T(8,128)(2,1)S(1)}, bf16[128,2048]{1,0:T(8,128)(2,1)S(1)}, u32[]{:S(2)}, u32[]{:S(2)}) collective-permute-start(bf16[128,2048]{1,0:T(8,128)(2,1)S(1)} %add_convert_fusion.17), channel_id=1, source_target_pairs={{0,16},{8,24},{16,0},{24,8},{1,17},{9,25},{17,1},{25,9},{2,18},{10... | collective-permute-start | bytes 1572872 | tf_op jit(solution)/shard_map/ppermute | solution.py:20
  546.2 38.2 %collective-permute-start.66 = (bf16[512,512]{1,0:T(8,128)(2,1)S(1)}, bf16[512,512]{1,0:T(8,128)(2,1)S(1)}, u32[]{:S(2)}, u32[]{:S(2)}) collective-permute-start(bf16[512,512]{1,0:T(8,128)(2,1)S(1)} %copy-done.10), channel_id=1, source_target_pairs={{0,2},{2,0},{4,6},{6,4},{1,3},{3,1},{5,7},{7,5},{8,10},{10,8},{12,... | collective-permute-start | bytes 1572872 | tf_op jit(solution)/shard_map/ppermute | solution.py:20
  587.9 37.3 %collective-permute-start.69 = (bf16[512,768]{1,0:T(8,128)(2,1)S(1)}, bf16[512,768]{1,0:T(8,128)(2,1)S(1)}, u32[]{:S(2)}, u32[]{:S(2)}) collective-permute-start(bf16[512,768]{1,0:T(8,128)(2,1)S(1)} %get-tuple-element.604), channel_id=1, source_target_pairs={{0,16},{8,24},{16,0},{24,8},{1,17},{9,25},{17,1},{25,9},{2,18},{10... | collective-permute-start | bytes 2359304 | tf_op jit(solution)/shard_map/ppermute | solution.py:20
  597.4 27.7 %collective-permute-start.75 = (bf16[128,1024]{1,0:T(8,128)(2,1)S(1)}, bf16[128,1024]{1,0:T(8,128)(2,1)S(1)}, u32[]{:S(2)}, u32[]{:S(2)}) collective-permute-start(bf16[128,1024]{1,0:T(8,128)(2,1)S(1)} %get-tuple-element.649), channel_id=1, source_target_pairs={{0,4},{2,6},{4,0},{6,2},{1,5},{3,7},{5,1},{7,3},{8,12},{10,14},{12... | collective-permute-start | bytes 786440 | tf_op jit(solution)/shard_map/ppermute | solution.py:20
  598.8 26.4 %collective-permute-start.76 = (bf16[512,512]{1,0:T(8,128)(2,1)S(1)}, bf16[512,512]{1,0:T(8,128)(2,1)S(1)}, u32[]{:S(2)}, u32[]{:S(2)}) collective-permute-start(bf16[512,512]{1,0:T(8,128)(2,1)S(1)} %collective-permute-done.59), channel_id=1, source_target_pairs={{0,4},{2,6},{4,0},{6,2},{1,5},{3,7},{5,1},{7,3},{8,12},{10,14},{12... | collective-permute-start | bytes 1572872 | tf_op jit(solution)/shard_map/ppermute | solution.py:20
  599.5 26.5 %collective-permute-start.77 = (bf16[128,2048]{1,0:T(8,128)(2,1)S(1)}, bf16[128,2048]{1,0:T(8,128)(2,1)S(1)}, u32[]{:S(2)}, u32[]{:S(2)}) collective-permute-start(bf16[128,2048]{1,0:T(8,128)(2,1)S(1)} %fusion.24), channel_id=1, source_target_pairs={{0,1},{1,0},{2,3},{3,2},{4,5},{5,4},{6,7},{7,6},{8,9},{9,8},{10,11... | collective-permute-start | bytes 1572872 | tf_op jit(solution)/shard_map/ppermute | solution.py:20
  601.3 23.9 %collective-permute-start.74 = (bf16[128,1024]{1,0:T(8,128)(2,1)S(1)}, bf16[128,1024]{1,0:T(8,128)(2,1)S(1)}, u32[]{:S(2)}, u32[]{:S(2)}) collective-permute-start(bf16[128,1024]{1,0:T(8,128)(2,1)S(1)} %get-tuple-element.651), channel_id=1, source_target_pairs={{0,1},{1,0},{2,3},{3,2},{4,5},{5,4},{6,7},{7,6},{8,9},{9,8},{10,11... | collective-permute-start | bytes 786440 | tf_op jit(solution)/shard_map/ppermute | solution.py:20
  629.4 18.6 %collective-permute-start.79 = (bf16[512,768]{1,0:T(8,128)(2,1)}, bf16[512,768]{1,0:T(8,128)(2,1)}, u32[]{:S(2)}, u32[]{:S(2)}) collective-permute-start(bf16[512,768]{1,0:T(8,128)(2,1)} %add_convert_fusion.14), channel_id=1, source_target_pairs={{0,4},{2,6},{4,0},{6,2},{1,5},{3,7},{5,1},{7,3},{8,12},{10,14},{12... | collective-permute-start | bytes 2359304 | tf_op jit(solution)/shard_map/ppermute | solution.py:20
  (177 other events, 1742.6 us)
Sparse Core Ops, SparseCore 0:
  11.2 105.4 all-gather.1
  322.6 31.6 reduce-scatter.2
  464.4 42.6 reduce-scatter.4

commit v6 on v5

--- a/solution.py
+++ b/solution.py
@@ -93,7 +93,7 @@
 
 def attend_forward(query, key, value, bias):
     rows, columns = query.shape
-    block = min(256, rows)
+    block = min(512, rows)
 
     def kernel(query_ref, key_ref, value_ref, bias_ref, out_ref, totals_ref):
         for head in range(2):
@@ -125,7 +125,7 @@
 
 def attend_backward(query, key, value, totals, grad, bias, cosine, sine):
     rows, columns = query.shape
-    block = min(256, rows)
+    block = min(512, rows)
     scale = 1.0 / math.sqrt(HD)
 
     def kernel(query_ref, key_ref, value_ref, totals_ref, grad_ref, bias_ref, cos_ref, sin_ref, dq_ref, dk_ref, dv_ref, q_acc, k_acc):

time: 690 us -> 690 us (level)
  transfers between devices with their start and end apart: 94 -> 94, of which waited for: 44 -> 44; matrix products, arithmetic and copies ran while one was open for 22% -> 22% of each run, Pallas kernels for 8% -> 7%
where the time goes in v6:
time: 690 us; the launch traced here: 685 us
  waiting for transfers between devices  310 us (45%)
  matrix products  80.5 us (12%)
  starting transfers between devices  76.9 us (11%)
  other arithmetic  74 us (11%)
  local copies, waits for them, and re-layouts  65.4 us (9%)
  Pallas kernels  48.5 us (7%)
  between operations  16.7 us (2%)
  blocking collectives  13.5 us (2%)
    ppermute x91, waiting for transfers between devices, flip(): return lax.ppermute(values, axis, [(i, i ^ bit) for i in range(size)])  283 us
    ppermute x91, starting transfers between devices, flip(): return lax.ppermute(values, axis, [(i, i ^ bit) for i in range(size)])  76.8 us
    unnamed x272, local copies, waits for them, and re-layouts  28.9 us
    dot_general x7, matrix products, mm(): return jnp.dot(left, right, preferred_element_type=F32)  28.7 us
    dot_general x9, matrix products, mm_t(): lax.dot_general(left, right, (((0,), (0,)), ((), ())), preferred_element_...  27.5 us
    all_gather x1, waiting for transfers between devices, body(): lax.all_gather(jnp.concatenate(attn_pack, axis=1), 'shard', axis=0, tiled...  26.9 us
    dot_general x6, matrix products, mm_nt(): lax.dot_general(left, right, (((1,), (1,)), ((), ())), preferred_element_...  24.2 us
    convert_element_type x29, other arithmetic, added(): return (keep.astype(F32) + come.astype(F32)).astype(BF)  23.6 us
  transfers between devices with their start and end apart: 94, of which 44 were waited for; matrix products, arithmetic and copies ran while one was open for 22% of the time, Pallas kernels for 7%

profile of v6, /device:TPU:0, one launch (start us, length us, event | category | flops | bytes accessed | tf_op | source)
XLA Modules:
  0.0 685.5 jit_solution(5088164428241798654)
XLA Ops:
  11.2 13.5 %all_gather.7 = bf16[2,2048]{1,0:T(2,128)(2,1)S(1)} all-gather(bf16[2,512]{1,0:T(2,128)(2,1)S(1)} %pad_maximum_fusion.36), channel_id=1, replica_groups=mesh['shard'=4,'ctx'=4,'tp'=2] {'shard'}, dimensions={1}, use_global_device_ids=true | all-gather | bytes 10240 | tf_op jit(solution)/shard_map/all_gather | solution.py:392
  34.4 20.0 %collective-permute-done = bf16[256,2048]{1,0:T(8,128)(2,1)} collective-permute-done((bf16[256,2048]{1,0:T(8,128)(2,1)S(1)}, bf16[256,2048]{1,0:T(8,128)(2,1)}, u32[]{:S(2)}, u32[]{:S(2)}) %collective-permute-start) | collective-permute-done | bytes 1048608 | tf_op jit(solution)/shard_map/ppermute | solution.py:20
  61.1 4.1 or_select_fusion.bias_ref
  73.7 16.1 %collective-permute-done.2 = bf16[128,2048]{1,0:T(8,128)(2,1)} collective-permute-done((bf16[128,2048]{1,0:T(8,128)(2,1)}, bf16[128,2048]{1,0:T(8,128)(2,1)}, u32[]{:S(2)}, u32[]{:S(2)}) %collective-permute-start.2) | collective-permute-done | bytes 524320 | tf_op jit(solution)/shard_map/ppermute | solution.py:20
  89.8 26.9 %all-gather.2.cloned.1.call-done = bf16[2048,1024]{0,1:T(8,128)(2,1)} async-done(((bf16[512,1024]{0,1:T(8,128)(2,1)}), bf16[2048,1024]{0,1:T(8,128)(2,1)}) %all-gather.2.cloned.1.call-update) | async-done | bytes 4194320 | tf_op jit(solution)/shard_map/all_gather | solution.py:391
  120.8 6.2 fusion.1
  139.3 8.6 %shard_map.230 = (bf16[1024,256]{1,0:T(8,128)(2,1)S(1)}, f32[1024,256]{1,0:T(8,128)S(1)}) custom-call(bf16[1024,256]{1,0:T(8,128)(2,1)S(1)} %copy.56.query_ref, bf16[1024,256]{1,0:T(8,128)(2,1)S(1)} %copy.57.key_ref, bf16[1024,256]{1,0:T(8,128)(2,1)S(1)} %copy.64.value_ref, f32[1024,1024]{1,0:T(8,128)S(1)} %copy-done.6), custom_call_target="tpu_custom_call" | custom-call | flops 4294967296 | bytes 6291456 | tf_op jit(solution)/shard_map/pallas_call | solution.py:111
  147.9 5.6 collective-permute-done.4
  156.2 4.1 collective-permute-done.10
  169.3 8.2 %collective-permute-done.12 = bf16[2,128,1024]{2,1,0:T(8,128)(2,1)} collective-permute-done((bf16[2,128,1024]{2,1,0:T(8,128)(2,1)}, bf16[2,128,1024]{2,1,0:T(8,128)(2,1)}, u32[]{:S(2)}, u32[]{:S(2)}) %collective-permute-start.12) | collective-permute-done | bytes 524320 | tf_op jit(solution)/shard_map/ppermute | solution.py:20
  184.1 16.0 %collective-permute-done.9 = bf16[512,512]{1,0:T(8,128)(2,1)S(1)} collective-permute-done((bf16[512,512]{1,0:T(8,128)(2,1)S(1)}, bf16[512,512]{1,0:T(8,128)(2,1)S(1)}, u32[]{:S(2)}, u32[]{:S(2)}) %collective-permute-start.9) | collective-permute-done | bytes 524320 | tf_op jit(solution)/shard_map/ppermute | solution.py:20
  216.6 13.6 %collective-permute-done.16 = bf16[128,2048]{1,0:T(8,128)(2,1)S(1)} collective-permute-done((bf16[128,2048]{1,0:T(8,128)(2,1)S(1)}, bf16[128,2048]{1,0:T(8,128)(2,1)S(1)}, u32[]{:S(2)}, u32[]{:S(2)}) %collective-permute-start.16) | collective-permute-done | bytes 524320 | tf_op jit(solution)/shard_map/ppermute | solution.py:20
  230.2 11.1 %collective-permute-done.21 = bf16[1024,512]{1,0:T(8,128)(2,1)S(1)} collective-permute-done((bf16[1024,512]{1,0:T(8,128)(2,1)S(1)}, bf16[1024,512]{1,0:T(8,128)(2,1)S(1)}, u32[]{:S(2)}, u32[]{:S(2)}) %collective-permute-start.21) | collective-permute-done | bytes 1048608 | tf_op jit(solution)/shard_map/ppermute | solution.py:20
  245.7 4.8 collective-permute-done.24
  255.3 4.5 fusion.71
  260.9 8.3 %collective-permute-done.22 = bf16[512,512]{1,0:T(8,128)(2,1)S(1)} collective-permute-done((bf16[512,512]{1,0:T(8,128)(2,1)S(1)}, bf16[512,512]{1,0:T(8,128)(2,1)S(1)}, u32[]{:S(2)}, u32[]{:S(2)}) %collective-permute-start.22) | collective-permute-done | bytes 524320 | tf_op jit(solution)/shard_map/ppermute | solution.py:20
  279.6 4.5 fusion.73
  287.7 4.7 fusion.72
  292.4 6.8 collective-permute-done.31
  301.8 4.8 convolution_convert_fusion.5
  328.4 5.2 convolution_convert_fusion.4
  333.6 6.5 collective-permute-done.34
  345.9 6.4 collective-permute-done.37
  363.4 7.9 %collective-permute-done.39 = bf16[2,128,1024]{2,1,0:T(8,128)(2,1)S(1)} collective-permute-done((bf16[2,128,1024]{2,1,0:T(8,128)(2,1)S(1)}, bf16[2,128,1024]{2,1,0:T(8,128)(2,1)S(1)}, u32[]{:S(2)}, u32[]{:S(2)}) %collective-permute-start.39) | collective-permute-done | bytes 524320 | tf_op jit(solution)/shard_map/ppermute | solution.py:20
  375.3 10.7 %collective-permute-done.40 = bf16[512,512]{1,0:T(8,128)(2,1)S(1)} collective-permute-done((bf16[512,512]{1,0:T(8,128)(2,1)S(1)}, bf16[512,512]{1,0:T(8,128)(2,1)S(1)}, u32[]{:S(2)}, u32[]{:S(2)}) %collective-permute-start.40) | collective-permute-done | bytes 524320 | tf_op jit(solution)/shard_map/ppermute | solution.py:20
  390.6 3.7 add_convert_fusion.3
  394.3 4.4 convolution_convert_fusion
  398.6 4.4 convolution_convert_fusion.1
  403.0 11.4 %collective-permute-done.43 = bf16[128,2048]{1,0:T(8,128)(2,1)S(1)} collective-permute-done((bf16[128,2048]{1,0:T(8,128)(2,1)S(1)}, bf16[128,2048]{1,0:T(8,128)(2,1)S(1)}, u32[]{:S(2)}, u32[]{:S(2)}) %collective-permute-start.43) | collective-permute-done | bytes 524320 | tf_op jit(solution)/shard_map/ppermute | solution.py:20
  424.5 3.8 add_convert_fusion.2
  430.9 6.1 add_convert_fusion
  437.0 5.6 collective-permute-done.49
  476.1 16.8 %shard_map.231 = (bf16[1024,256]{1,0:T(8,128)(2,1)S(1)}, bf16[1024,256]{1,0:T(8,128)(2,1)S(1)}, bf16[1024,256]{1,0:T(8,128)(2,1)S(1)}) custom-call(bf16[1024,256]{1,0:T(8,128)(2,1)S(1)} %copy-done.36, bf16[1024,256]{1,0:T(8,128)(2,1)S(1)} %copy-done.34, bf16[1024,256]{1,0:T(8,128)(2,1)S(1)} %copy.64.value_ref, f32[1024,256]{1,0:T(8,128)S(1)} %copy-done.46, ...), custom_call_target="tpu_custom_call" | custom-call | flops 8053063680 | bytes 7864320 | tf_op jit(solution)/shard_map/pallas_call | solution.py:160
  492.9 13.6 %collective-permute-done.58 = bf16[1024,512]{1,0:T(8,128)(2,1)} collective-permute-done((bf16[1024,512]{1,0:T(8,128)(2,1)}, bf16[1024,512]{1,0:T(8,128)(2,1)}, u32[]{:S(2)}, u32[]{:S(2)}) %collective-permute-start.58) | collective-permute-done | bytes 1048608 | tf_op jit(solution)/shard_map/ppermute | solution.py:20
  510.8 4.9 convolution_convert_fusion.6
  515.7 5.8 convolution_convert_fusion.3
  531.4 5.5 collective-permute-done.62
  539.4 6.7 collective-permute-done.68
  546.2 26.2 %collective-permute-done.59 = bf16[512,512]{1,0:T(8,128)(2,1)S(1)} collective-permute-done((bf16[512,512]{1,0:T(8,128)(2,1)S(1)}, bf16[512,512]{1,0:T(8,128)(2,1)S(1)}, u32[]{:S(2)}, u32[]{:S(2)}) %collective-permute-start.59) | collective-permute-done | bytes 524320 | tf_op jit(solution)/shard_map/ppermute | solution.py:20
  573.3 11.0 %collective-permute-done.64 = bf16[1024,768]{1,0:T(8,128)(2,1)S(1)} collective-permute-done((bf16[1024,768]{1,0:T(8,128)(2,1)S(1)}, bf16[1024,768]{1,0:T(8,128)(2,1)S(1)}, u32[]{:S(2)}, u32[]{:S(2)}) %collective-permute-start.64) | collective-permute-done | bytes 1572896 | tf_op jit(solution)/shard_map/ppermute | solution.py:20
  589.3 7.6 %collective-permute-done.71 = bf16[2,128,1024]{2,1,0:T(8,128)(2,1)S(1)} collective-permute-done((bf16[2,128,1024]{2,1,0:T(8,128)(2,1)S(1)}, bf16[2,128,1024]{2,1,0:T(8,128)(2,1)S(1)}, u32[]{:S(2)}, u32[]{:S(2)}) %collective-permute-start.71) | collective-permute-done | bytes 524320 | tf_op jit(solution)/shard_map/ppermute | solution.py:20
  602.0 5.1 shard_map.233
  607.1 5.1 shard_map.232
  612.3 12.9 %collective-permute-done.69 = bf16[512,768]{1,0:T(8,128)(2,1)S(1)} collective-permute-done((bf16[512,768]{1,0:T(8,128)(2,1)S(1)}, bf16[512,768]{1,0:T(8,128)(2,1)S(1)}, u32[]{:S(2)}, u32[]{:S(2)}) %collective-permute-start.69) | collective-permute-done | bytes 786464 | tf_op jit(solution)/shard_map/ppermute | solution.py:20
  633.4 7.8 %collective-permute-done.78 = f32[32,128]{1,0:T(8,128)S(1)} collective-permute-done((f32[32,128]{1,0:T(8,128)S(1)}, f32[32,128]{1,0:T(8,128)S(1)}, u32[]{:S(2)}, u32[]{:S(2)}) %collective-permute-start.78) | collective-permute-done | bytes 16416 | tf_op jit(solution)/shard_map/ppermute | solution.py:20
  642.9 5.2 collective-permute-done.79
  658.9 5.3 shard_map.235
  665.7 5.1 shard_map.234
  (643 shorter events, 255.7 us)
Async XLA Ops:
  7.2 109.5 %all-gather.2.cloned.1.call-start = ((), (), s32[]{:S(2)}) async-start(), calls=%async_computation.2 | async-start | bytes 5242880 | tf_op jit(solution)/shard_map/all_gather | solution.py:391
  11.1 343.2 %reduce-scatter.3.cloned.1.call-start = ((), (), s32[]{:S(2)}) async-start(), calls=%async_computation.3 | async-start | bytes 3145728 | tf_op jit(solution)/shard_map/reduce_scatter | solution.py:334
  28.1 26.2 %collective-permute-start = (bf16[256,2048]{1,0:T(8,128)(2,1)S(1)}, bf16[256,2048]{1,0:T(8,128)(2,1)}, u32[]{:S(2)}, u32[]{:S(2)}) collective-permute-start(bf16[256,2048]{1,0:T(8,128)(2,1)S(1)} %get-tuple-element.610), channel_id=1, source_target_pairs={{0,4},{2,6},{4,0},{6,2},{1,5},{3,7},{5,1},{7,3},{8,12},{10,14},{12... | collective-permute-start | bytes 3145736 | tf_op jit(solution)/shard_map/ppermute | solution.py:20
  30.8 59.0 %collective-permute-start.3 = (bf16[256,2048]{1,0:T(8,128)(2,1)}, bf16[256,2048]{1,0:T(8,128)(2,1)}, u32[]{:S(2)}, u32[]{:S(2)}) collective-permute-start(bf16[256,2048]{1,0:T(8,128)(2,1)} %pad_maximum_fusion.13), channel_id=1, source_target_pairs={{0,4},{2,6},{4,0},{6,2},{1,5},{3,7},{5,1},{7,3},{8,12},{10,14},{12... | collective-permute-start | bytes 3145736 | tf_op jit(solution)/shard_map/ppermute | solution.py:20
  33.3 56.5 %collective-permute-start.2 = (bf16[128,2048]{1,0:T(8,128)(2,1)}, bf16[128,2048]{1,0:T(8,128)(2,1)}, u32[]{:S(2)}, u32[]{:S(2)}) collective-permute-start(bf16[128,2048]{1,0:T(8,128)(2,1)} %slice.184), channel_id=1, source_target_pairs={{0,16},{8,24},{16,0},{24,8},{1,17},{9,25},{17,1},{25,9},{2,18},{10... | collective-permute-start | bytes 1572872 | tf_op jit(solution)/shard_map/ppermute | solution.py:20
  129.4 24.1 %collective-permute-start.4 = (bf16[512,512]{1,0:T(8,128)(2,1)}, bf16[512,512]{1,0:T(8,128)(2,1)}, u32[]{:S(2)}, u32[]{:S(2)}) collective-permute-start(bf16[512,512]{1,0:T(8,128)(2,1)} %get-tuple-element.282), channel_id=1, source_target_pairs={{0,16},{8,24},{16,0},{24,8},{1,17},{9,25},{17,1},{25,9},{2,18},{10... | collective-permute-start | bytes 1572872 | tf_op jit(solution)/shard_map/ppermute | solution.py:20
  131.4 22.1 %collective-permute-start.8 = (bf16[2,128,1024]{2,1,0:T(8,128)(2,1)}, bf16[2,128,1024]{2,1,0:T(8,128)(2,1)}, u32[]{:S(2)}, u32[]{:S(2)}) collective-permute-start(bf16[2,128,1024]{2,1,0:T(8,128)(2,1)} %bitcast.11), channel_id=1, source_target_pairs={{0,1},{1,0},{2,3},{3,2},{4,5},{5,4},{6,7},{7,6},{8,9},{9,8},{10,11... | collective-permute-start | bytes 1572872 | tf_op jit(solution)/shard_map/ppermute | solution.py:20
  133.8 19.7 %collective-permute-start.6 = (bf16[256,1024]{1,0:T(8,128)(2,1)}, bf16[256,1024]{1,0:T(8,128)(2,1)}, u32[]{:S(2)}, u32[]{:S(2)}) collective-permute-start(bf16[256,1024]{1,0:T(8,128)(2,1)} %pad_maximum_fusion.21), channel_id=1, source_target_pairs={{0,4},{2,6},{4,0},{6,2},{1,5},{3,7},{5,1},{7,3},{8,12},{10,14},{12... | collective-permute-start | bytes 1572872 | tf_op jit(solution)/shard_map/ppermute | solution.py:20
  163.2 14.3 %collective-permute-start.12 = (bf16[2,128,1024]{2,1,0:T(8,128)(2,1)}, bf16[2,128,1024]{2,1,0:T(8,128)(2,1)}, u32[]{:S(2)}, u32[]{:S(2)}) collective-permute-start(bf16[2,128,1024]{2,1,0:T(8,128)(2,1)} %get-tuple-element.639), channel_id=1, source_target_pairs={{0,1},{1,0},{2,3},{3,2},{4,5},{5,4},{6,7},{7,6},{8,9},{9,8},{10,11... | collective-permute-start | bytes 1572872 | tf_op jit(solution)/shard_map/ppermute | solution.py:20
  166.0 36.3 %collective-permute-start.15 = (bf16[1024,512]{1,0:T(8,128)(2,1)S(1)}, bf16[1024,512]{1,0:T(8,128)(2,1)S(1)}, u32[]{:S(2)}, u32[]{:S(2)}) collective-permute-start(bf16[1024,512]{1,0:T(8,128)(2,1)S(1)} %maximum_select_fusion), channel_id=1, source_target_pairs={{0,8},{8,0},{16,24},{24,16},{1,9},{9,1},{17,25},{25,17},{2,10},{10... | collective-permute-start | bytes 3145736 | tf_op jit(solution)/shard_map/ppermute | solution.py:20
  166.1 34.0 %collective-permute-start.9 = (bf16[512,512]{1,0:T(8,128)(2,1)S(1)}, bf16[512,512]{1,0:T(8,128)(2,1)S(1)}, u32[]{:S(2)}, u32[]{:S(2)}) collective-permute-start(bf16[512,512]{1,0:T(8,128)(2,1)S(1)} %copy-done.103), channel_id=1, source_target_pairs={{0,16},{8,24},{16,0},{24,8},{1,17},{9,25},{17,1},{25,9},{2,18},{10... | collective-permute-start | bytes 1572872 | tf_op jit(solution)/shard_map/ppermute | solution.py:20
  179.0 23.3 %collective-permute-start.14 = (bf16[128,1024]{1,0:T(8,128)(2,1)S(1)}, bf16[128,1024]{1,0:T(8,128)(2,1)S(1)}, u32[]{:S(2)}, u32[]{:S(2)}) collective-permute-start(bf16[128,1024]{1,0:T(8,128)(2,1)S(1)} %get-tuple-element.669), channel_id=1, source_target_pairs={{0,4},{2,6},{4,0},{6,2},{1,5},{3,7},{5,1},{7,3},{8,12},{10,14},{12... | collective-permute-start | bytes 786440 | tf_op jit(solution)/shard_map/ppermute | solution.py:20
  180.7 21.6 %collective-permute-start.13 = (bf16[128,1024]{1,0:T(8,128)(2,1)S(1)}, bf16[128,1024]{1,0:T(8,128)(2,1)S(1)}, u32[]{:S(2)}, u32[]{:S(2)}) collective-permute-start(bf16[128,1024]{1,0:T(8,128)(2,1)S(1)} %get-tuple-element.671), channel_id=1, source_target_pairs={{0,1},{1,0},{2,3},{3,2},{4,5},{5,4},{6,7},{7,6},{8,9},{9,8},{10,11... | collective-permute-start | bytes 786440 | tf_op jit(solution)/shard_map/ppermute | solution.py:20
  205.9 24.3 %collective-permute-start.16 = (bf16[128,2048]{1,0:T(8,128)(2,1)S(1)}, bf16[128,2048]{1,0:T(8,128)(2,1)S(1)}, u32[]{:S(2)}, u32[]{:S(2)}) collective-permute-start(bf16[128,2048]{1,0:T(8,128)(2,1)S(1)} %pad_maximum_fusion.23), channel_id=1, source_target_pairs={{0,16},{8,24},{16,0},{24,8},{1,17},{9,25},{17,1},{25,9},{2,18},{10... | collective-permute-start | bytes 1572872 | tf_op jit(solution)/shard_map/ppermute | solution.py:20
  207.6 33.8 %collective-permute-start.21 = (bf16[1024,512]{1,0:T(8,128)(2,1)S(1)}, bf16[1024,512]{1,0:T(8,128)(2,1)S(1)}, u32[]{:S(2)}, u32[]{:S(2)}) collective-permute-start(bf16[1024,512]{1,0:T(8,128)(2,1)S(1)} %maximum_select_fusion.1), channel_id=1, source_target_pairs={{0,8},{8,0},{16,24},{24,16},{1,9},{9,1},{17,25},{25,17},{2,10},{10... | collective-permute-start | bytes 3145736 | tf_op jit(solution)/shard_map/ppermute | solution.py:20
  211.2 19.0 %collective-permute-start.20 = (bf16[2,128,1024]{2,1,0:T(8,128)(2,1)S(1)}, bf16[2,128,1024]{2,1,0:T(8,128)(2,1)S(1)}, u32[]{:S(2)}, u32[]{:S(2)}) collective-permute-start(bf16[2,128,1024]{2,1,0:T(8,128)(2,1)S(1)} %bitcast.161), channel_id=1, source_target_pairs={{0,1},{1,0},{2,3},{3,2},{4,5},{5,4},{6,7},{7,6},{8,9},{9,8},{10,11... | collective-permute-start | bytes 1572872 | tf_op jit(solution)/shard_map/ppermute | solution.py:20
  212.8 17.4 %collective-permute-start.19 = (bf16[256,1024]{1,0:T(8,128)(2,1)S(1)}, bf16[256,1024]{1,0:T(8,128)(2,1)S(1)}, u32[]{:S(2)}, u32[]{:S(2)}) collective-permute-start(bf16[256,1024]{1,0:T(8,128)(2,1)S(1)} %constant_dynamic-update-slice_fusion.1), channel_id=1, source_target_pairs={{0,4},{2,6},{4,0},{6,2},{1,5},{3,7},{5,1},{7,3},{8,12},{10,14},{12... | collective-permute-start | bytes 1572872 | tf_op jit(solution)/shard_map/ppermute | solution.py:20
  243.4 25.9 %collective-permute-start.22 = (bf16[512,512]{1,0:T(8,128)(2,1)S(1)}, bf16[512,512]{1,0:T(8,128)(2,1)S(1)}, u32[]{:S(2)}, u32[]{:S(2)}) collective-permute-start(bf16[512,512]{1,0:T(8,128)(2,1)S(1)} %copy-done.102), channel_id=1, source_target_pairs={{0,16},{8,24},{16,0},{24,8},{1,17},{9,25},{17,1},{25,9},{2,18},{10... | collective-permute-start | bytes 1572872 | tf_op jit(solution)/shard_map/ppermute | solution.py:20
  245.2 28.4 %collective-permute-start.29 = (bf16[512,2048]{1,0:T(8,128)(2,1)S(1)}, bf16[512,2048]{1,0:T(8,128)(2,1)S(1)}, u32[]{:S(2)}, u32[]{:S(2)}) collective-permute-start(bf16[512,2048]{1,0:T(8,128)(2,1)S(1)} %pad_maximum_fusion.4), channel_id=1, source_target_pairs={{0,2},{2,0},{4,6},{6,4},{1,3},{3,1},{5,7},{7,5},{8,10},{10,8},{12,... | collective-permute-start | bytes 6291464 | tf_op jit(solution)/shard_map/ppermute | solution.py:20
  250.7 18.5 %collective-permute-start.27 = (bf16[2,128,1024]{2,1,0:T(8,128)(2,1)S(1)}, bf16[2,128,1024]{2,1,0:T(8,128)(2,1)S(1)}, u32[]{:S(2)}, u32[]{:S(2)}) collective-permute-start(bf16[2,128,1024]{2,1,0:T(8,128)(2,1)S(1)} %bitcast.159), channel_id=1, source_target_pairs={{0,1},{1,0},{2,3},{3,2},{4,5},{5,4},{6,7},{7,6},{8,9},{9,8},{10,11... | collective-permute-start | bytes 1572872 | tf_op jit(solution)/shard_map/ppermute | solution.py:20
  252.3 16.9 %collective-permute-start.26 = (bf16[256,1024]{1,0:T(8,128)(2,1)S(1)}, bf16[256,1024]{1,0:T(8,128)(2,1)S(1)}, u32[]{:S(2)}, u32[]{:S(2)}) collective-permute-start(bf16[256,1024]{1,0:T(8,128)(2,1)S(1)} %constant_dynamic-update-slice_fusion.7), channel_id=1, source_target_pairs={{0,4},{2,6},{4,0},{6,2},{1,5},{3,7},{5,1},{7,3},{8,12},{10,14},{12... | collective-permute-start | bytes 1572872 | tf_op jit(solution)/shard_map/ppermute | solution.py:20
  273.6 25.6 %collective-permute-start.31 = (bf16[512,1024]{1,0:T(8,128)(2,1)S(1)}, bf16[512,1024]{1,0:T(8,128)(2,1)S(1)}, u32[]{:S(2)}, u32[]{:S(2)}) collective-permute-start(bf16[512,1024]{1,0:T(8,128)(2,1)S(1)} %maximum_select_fusion.2), channel_id=1, source_target_pairs={{0,8},{8,0},{16,24},{24,16},{1,9},{9,1},{17,25},{25,17},{2,10},{10... | collective-permute-start | bytes 3145736 | tf_op jit(solution)/shard_map/ppermute | solution.py:20
  322.5 193.2 %reduce-scatter.5.cloned.1.call-start = ((), (), s32[]{:S(2)}) async-start(), calls=%async_computation.4 | async-start | bytes 1310720 | tf_op jit(solution)/shard_map/reduce_scatter | solution.py:546
  325.7 14.4 %collective-permute-start.34 = (bf16[2,128,1024]{2,1,0:T(8,128)(2,1)S(1)}, bf16[2,128,1024]{2,1,0:T(8,128)(2,1)S(1)}, u32[]{:S(2)}, u32[]{:S(2)}) collective-permute-start(bf16[2,128,1024]{2,1,0:T(8,128)(2,1)S(1)} %get-tuple-element.637), channel_id=1, source_target_pairs={{0,1},{1,0},{2,3},{3,2},{4,5},{5,4},{6,7},{7,6},{8,9},{9,8},{10,11... | collective-permute-start | bytes 1572872 | tf_op jit(solution)/shard_map/ppermute | solution.py:20
  326.9 14.1 %collective-permute-start.33 = (bf16[256,1024]{1,0:T(8,128)(2,1)S(1)}, bf16[256,1024]{1,0:T(8,128)(2,1)S(1)}, u32[]{:S(2)}, u32[]{:S(2)}) collective-permute-start(bf16[256,1024]{1,0:T(8,128)(2,1)S(1)} %get-tuple-element.595), channel_id=1, source_target_pairs={{0,4},{2,6},{4,0},{6,2},{1,5},{3,7},{5,1},{7,3},{8,12},{10,14},{12... | collective-permute-start | bytes 1572872 | tf_op jit(solution)/shard_map/ppermute | solution.py:20
  360.7 25.3 %collective-permute-start.40 = (bf16[512,512]{1,0:T(8,128)(2,1)S(1)}, bf16[512,512]{1,0:T(8,128)(2,1)S(1)}, u32[]{:S(2)}, u32[]{:S(2)}) collective-permute-start(bf16[512,512]{1,0:T(8,128)(2,1)S(1)} %get-tuple-element.633), channel_id=1, source_target_pairs={{0,16},{8,24},{16,0},{24,8},{1,17},{9,25},{17,1},{25,9},{2,18},{10... | collective-permute-start | bytes 1572872 | tf_op jit(solution)/shard_map/ppermute | solution.py:20
  389.6 24.8 %collective-permute-start.43 = (bf16[128,2048]{1,0:T(8,128)(2,1)S(1)}, bf16[128,2048]{1,0:T(8,128)(2,1)S(1)}, u32[]{:S(2)}, u32[]{:S(2)}) collective-permute-start(bf16[128,2048]{1,0:T(8,128)(2,1)S(1)} %pad_maximum_fusion.27), channel_id=1, source_target_pairs={{0,16},{8,24},{16,0},{24,8},{1,17},{9,25},{17,1},{25,9},{2,18},{10... | collective-permute-start | bytes 1572872 | tf_op jit(solution)/shard_map/ppermute | solution.py:20
  389.6 24.7 %collective-permute-start.44 = (bf16[512,512]{1,0:T(8,128)(2,1)S(1)}, bf16[512,512]{1,0:T(8,128)(2,1)S(1)}, u32[]{:S(2)}, u32[]{:S(2)}) collective-permute-start(bf16[512,512]{1,0:T(8,128)(2,1)S(1)} %get-tuple-element.493), channel_id=1, source_target_pairs={{0,4},{2,6},{4,0},{6,2},{1,5},{3,7},{5,1},{7,3},{8,12},{10,14},{12... | collective-permute-start | bytes 1572872 | tf_op jit(solution)/shard_map/ppermute | solution.py:20
  415.2 15.7 %collective-permute-start.45 = (bf16[1024,2048]{1,0:T(8,128)(2,1)}, bf16[1024,2048]{1,0:T(8,128)(2,1)}, u32[]{:S(2)}, u32[]{:S(2)}) collective-permute-start(bf16[1024,2048]{1,0:T(8,128)(2,1)} %convolution_convert_fusion), channel_id=1, source_target_pairs={{0,2},{2,0},{4,6},{6,4},{1,3},{3,1},{5,7},{7,5},{8,10},{10,8},{12,... | collective-permute-start | bytes 12582920 | tf_op jit(solution)/shard_map/ppermute | solution.py:20
  421.8 24.8 %collective-permute-start.50 = (bf16[1024,512]{1,0:T(8,128)(2,1)S(1)}, bf16[1024,512]{1,0:T(8,128)(2,1)S(1)}, u32[]{:S(2)}, u32[]{:S(2)}) collective-permute-start(bf16[1024,512]{1,0:T(8,128)(2,1)S(1)} %get-tuple-element.589), channel_id=1, source_target_pairs={{0,8},{8,0},{16,24},{24,16},{1,9},{9,1},{17,25},{25,17},{2,10},{10... | collective-permute-start | bytes 3145736 | tf_op jit(solution)/shard_map/ppermute | solution.py:20
  428.3 14.2 %collective-permute-start.49 = (bf16[2,128,1024]{2,1,0:T(8,128)(2,1)S(1)}, bf16[2,128,1024]{2,1,0:T(8,128)(2,1)S(1)}, u32[]{:S(2)}, u32[]{:S(2)}) collective-permute-start(bf16[2,128,1024]{2,1,0:T(8,128)(2,1)S(1)} %bitcast.163), channel_id=1, source_target_pairs={{0,1},{1,0},{2,3},{3,2},{4,5},{5,4},{6,7},{7,6},{8,9},{9,8},{10,11... | collective-permute-start | bytes 1572872 | tf_op jit(solution)/shard_map/ppermute | solution.py:20
  453.7 52.8 %collective-permute-start.58 = (bf16[1024,512]{1,0:T(8,128)(2,1)}, bf16[1024,512]{1,0:T(8,128)(2,1)}, u32[]{:S(2)}, u32[]{:S(2)}) collective-permute-start(bf16[1024,512]{1,0:T(8,128)(2,1)} %get-tuple-element.585), channel_id=1, source_target_pairs={{0,8},{8,0},{16,24},{24,16},{1,9},{9,1},{17,25},{25,17},{2,10},{10... | collective-permute-start | bytes 3145736 | tf_op jit(solution)/shard_map/ppermute | solution.py:20
  466.1 42.6 %collective-permute-start.54 = (bf16[512,512]{1,0:T(8,128)(2,1)S(1)}, bf16[512,512]{1,0:T(8,128)(2,1)S(1)}, u32[]{:S(2)}, u32[]{:S(2)}) collective-permute-start(bf16[512,512]{1,0:T(8,128)(2,1)S(1)} %get-tuple-element.624), channel_id=1, source_target_pairs={{0,16},{8,24},{16,0},{24,8},{1,17},{9,25},{17,1},{25,9},{2,18},{10... | collective-permute-start | bytes 1572872 | tf_op jit(solution)/shard_map/ppermute | solution.py:20
  468.8 39.9 %collective-permute-start.57 = (bf16[512,512]{1,0:T(8,128)(2,1)S(1)}, bf16[512,512]{1,0:T(8,128)(2,1)S(1)}, u32[]{:S(2)}, u32[]{:S(2)}) collective-permute-start(bf16[512,512]{1,0:T(8,128)(2,1)S(1)} %get-tuple-element.479), channel_id=1, source_target_pairs={{0,4},{2,6},{4,0},{6,2},{1,5},{3,7},{5,1},{7,3},{8,12},{10,14},{12... | collective-permute-start | bytes 1572872 | tf_op jit(solution)/shard_map/ppermute | solution.py:20
  471.0 38.5 %collective-permute-start.56 = (bf16[2,128,2048]{2,1,0:T(8,128)(2,1)}, bf16[2,128,2048]{2,1,0:T(8,128)(2,1)S(1)}, u32[]{:S(2)}, u32[]{:S(2)}) collective-permute-start(bf16[2,128,2048]{2,1,0:T(8,128)(2,1)} %get-tuple-element.587), channel_id=1, source_target_pairs={{0,1},{1,0},{2,3},{3,2},{4,5},{5,4},{6,7},{7,6},{8,9},{9,8},{10,11... | collective-permute-start | bytes 3145736 | tf_op jit(solution)/shard_map/ppermute | solution.py:20
  472.5 37.0 %collective-permute-start.55 = (bf16[256,2048]{1,0:T(8,128)(2,1)S(1)}, bf16[256,2048]{1,0:T(8,128)(2,1)S(1)}, u32[]{:S(2)}, u32[]{:S(2)}) collective-permute-start(bf16[256,2048]{1,0:T(8,128)(2,1)S(1)} %copy-done.101), channel_id=1, source_target_pairs={{0,4},{2,6},{4,0},{6,2},{1,5},{3,7},{5,1},{7,3},{8,12},{10,14},{12... | collective-permute-start | bytes 3145736 | tf_op jit(solution)/shard_map/ppermute | solution.py:20
  521.9 15.9 %collective-permute-start.60 = (bf16[512,2048]{1,0:T(8,128)(2,1)S(1)}, bf16[512,2048]{1,0:T(8,128)(2,1)S(1)}, u32[]{:S(2)}, u32[]{:S(2)}) collective-permute-start(bf16[512,2048]{1,0:T(8,128)(2,1)S(1)} %get-tuple-element.555), channel_id=1, source_target_pairs={{0,2},{2,0},{4,6},{6,4},{1,3},{3,1},{5,7},{7,5},{8,10},{10,8},{12,... | collective-permute-start | bytes 6291464 | tf_op jit(solution)/shard_map/ppermute | solution.py:20
  526.2 58.1 %collective-permute-start.64 = (bf16[1024,768]{1,0:T(8,128)(2,1)S(1)}, bf16[1024,768]{1,0:T(8,128)(2,1)S(1)}, u32[]{:S(2)}, u32[]{:S(2)}) collective-permute-start(bf16[1024,768]{1,0:T(8,128)(2,1)S(1)} %get-tuple-element.579), channel_id=1, source_target_pairs={{0,8},{8,0},{16,24},{24,16},{1,9},{9,1},{17,25},{25,17},{2,10},{10... | collective-permute-start | bytes 4718600 | tf_op jit(solution)/shard_map/ppermute | solution.py:20
  528.0 44.4 %collective-permute-start.59 = (bf16[512,512]{1,0:T(8,128)(2,1)S(1)}, bf16[512,512]{1,0:T(8,128)(2,1)S(1)}, u32[]{:S(2)}, u32[]{:S(2)}) collective-permute-start(bf16[512,512]{1,0:T(8,128)(2,1)S(1)} %get-tuple-element.622), channel_id=1, source_target_pairs={{0,16},{8,24},{16,0},{24,8},{1,17},{9,25},{17,1},{25,9},{2,18},{10... | collective-permute-start | bytes 1572872 | tf_op jit(solution)/shard_map/ppermute | solution.py:20
  537.9 46.5 %collective-permute-start.65 = (bf16[3,512,512]{2,1,0:T(8,128)(2,1)S(1)}, bf16[3,512,512]{2,1,0:T(8,128)(2,1)S(1)}, u32[]{:S(2)}, u32[]{:S(2)}) collective-permute-start(bf16[3,512,512]{2,1,0:T(8,128)(2,1)S(1)} %pad_maximum_fusion.11.refs_4_.refs_0_), channel_id=1, source_target_pairs={{0,4},{2,6},{4,0},{6,2},{1,5},{3,7},{5,1},{7,3},{8,12},{10,14},{12... | collective-permute-start | bytes 4718600 | tf_op jit(solution)/shard_map/ppermute | solution.py:20
  539.4 45.0 %collective-permute-start.63 = (bf16[128,2048]{1,0:T(8,128)(2,1)S(1)}, bf16[128,2048]{1,0:T(8,128)(2,1)S(1)}, u32[]{:S(2)}, u32[]{:S(2)}) collective-permute-start(bf16[128,2048]{1,0:T(8,128)(2,1)S(1)} %add_convert_fusion.17), channel_id=1, source_target_pairs={{0,16},{8,24},{16,0},{24,8},{1,17},{9,25},{17,1},{25,9},{2,18},{10... | collective-permute-start | bytes 1572872 | tf_op jit(solution)/shard_map/ppermute | solution.py:20
  546.2 38.2 %collective-permute-start.66 = (bf16[512,512]{1,0:T(8,128)(2,1)S(1)}, bf16[512,512]{1,0:T(8,128)(2,1)S(1)}, u32[]{:S(2)}, u32[]{:S(2)}) collective-permute-start(bf16[512,512]{1,0:T(8,128)(2,1)S(1)} %copy-done.10), channel_id=1, source_target_pairs={{0,2},{2,0},{4,6},{6,4},{1,3},{3,1},{5,7},{7,5},{8,10},{10,8},{12,... | collective-permute-start | bytes 1572872 | tf_op jit(solution)/shard_map/ppermute | solution.py:20
  587.9 37.3 %collective-permute-start.69 = (bf16[512,768]{1,0:T(8,128)(2,1)S(1)}, bf16[512,768]{1,0:T(8,128)(2,1)S(1)}, u32[]{:S(2)}, u32[]{:S(2)}) collective-permute-start(bf16[512,768]{1,0:T(8,128)(2,1)S(1)} %get-tuple-element.604), channel_id=1, source_target_pairs={{0,16},{8,24},{16,0},{24,8},{1,17},{9,25},{17,1},{25,9},{2,18},{10... | collective-permute-start | bytes 2359304 | tf_op jit(solution)/shard_map/ppermute | solution.py:20
  597.4 27.7 %collective-permute-start.75 = (bf16[128,1024]{1,0:T(8,128)(2,1)S(1)}, bf16[128,1024]{1,0:T(8,128)(2,1)S(1)}, u32[]{:S(2)}, u32[]{:S(2)}) collective-permute-start(bf16[128,1024]{1,0:T(8,128)(2,1)S(1)} %get-tuple-element.649), channel_id=1, source_target_pairs={{0,4},{2,6},{4,0},{6,2},{1,5},{3,7},{5,1},{7,3},{8,12},{10,14},{12... | collective-permute-start | bytes 786440 | tf_op jit(solution)/shard_map/ppermute | solution.py:20
  598.8 26.4 %collective-permute-start.76 = (bf16[512,512]{1,0:T(8,128)(2,1)S(1)}, bf16[512,512]{1,0:T(8,128)(2,1)S(1)}, u32[]{:S(2)}, u32[]{:S(2)}) collective-permute-start(bf16[512,512]{1,0:T(8,128)(2,1)S(1)} %collective-permute-done.59), channel_id=1, source_target_pairs={{0,4},{2,6},{4,0},{6,2},{1,5},{3,7},{5,1},{7,3},{8,12},{10,14},{12... | collective-permute-start | bytes 1572872 | tf_op jit(solution)/shard_map/ppermute | solution.py:20
  599.5 26.5 %collective-permute-start.77 = (bf16[128,2048]{1,0:T(8,128)(2,1)S(1)}, bf16[128,2048]{1,0:T(8,128)(2,1)S(1)}, u32[]{:S(2)}, u32[]{:S(2)}) collective-permute-start(bf16[128,2048]{1,0:T(8,128)(2,1)S(1)} %fusion.24), channel_id=1, source_target_pairs={{0,1},{1,0},{2,3},{3,2},{4,5},{5,4},{6,7},{7,6},{8,9},{9,8},{10,11... | collective-permute-start | bytes 1572872 | tf_op jit(solution)/shard_map/ppermute | solution.py:20
  601.3 23.9 %collective-permute-start.74 = (bf16[128,1024]{1,0:T(8,128)(2,1)S(1)}, bf16[128,1024]{1,0:T(8,128)(2,1)S(1)}, u32[]{:S(2)}, u32[]{:S(2)}) collective-permute-start(bf16[128,1024]{1,0:T(8,128)(2,1)S(1)} %get-tuple-element.651), channel_id=1, source_target_pairs={{0,1},{1,0},{2,3},{3,2},{4,5},{5,4},{6,7},{7,6},{8,9},{9,8},{10,11... | collective-permute-start | bytes 786440 | tf_op jit(solution)/shard_map/ppermute | solution.py:20
  629.4 18.6 %collective-permute-start.79 = (bf16[512,768]{1,0:T(8,128)(2,1)}, bf16[512,768]{1,0:T(8,128)(2,1)}, u32[]{:S(2)}, u32[]{:S(2)}) collective-permute-start(bf16[512,768]{1,0:T(8,128)(2,1)} %add_convert_fusion.14), channel_id=1, source_target_pairs={{0,4},{2,6},{4,0},{6,2},{1,5},{3,7},{5,1},{7,3},{8,12},{10,14},{12... | collective-permute-start | bytes 2359304 | tf_op jit(solution)/shard_map/ppermute | solution.py:20
  (177 other events, 1743.3 us)
Sparse Core Ops, SparseCore 0:
  11.2 105.4 all-gather.1
  322.6 31.6 reduce-scatter.2
  464.4 42.6 reduce-scatter.4
